TPU v7x, 128 devices: a whole 4x4x4 slice. The times are simulated.
128 devices in a mesh: gx: 16 (over y, x_hi, core), gy: 8 (over x_lo, z).
Axes of the slice: x: 4 (x_hi: 2, x_lo: 2; x = x_hi * 2 + x_lo), y: 4, z: 4, core: 2. Of those that a mesh axis runs over, the one named last changes fastest.
Arguments:
- atom_cells: int32 [3, 4, 64, 1024], P(None, None, 'gx', 'gy'), may hold values from 0 to 511, as said below
- atom_frac: float32 [3, 4, 64, 1024], P(None, None, 'gx', 'gy'), may hold values from 0 to 1
- species: int32 [4, 64, 1024], P(None, 'gx', 'gy'), may hold values from 0 to 1
- w_first: float32 [2, 32, 15], replicated, may hold values from -1 to 1
- b_first: float32 [2, 15], replicated, may hold values from -3 to 3
- w_second: float32 [2, 15, 15], replicated, may hold values from -1.5 to 1.5
- b_second: float32 [2, 15], replicated, may hold values from -3 to 3
- w_out: float32 [2, 15, 2], replicated, may hold values from -1.5 to 1.5
- b_out: float32 [2, 2], replicated, may hold values from -4 to 4
Outputs:
- atom_energy: float32 [4, 64, 1024], P(None, 'gx', 'gy')
- atom_force: float32 [3, 4, 64, 1024], P(None, None, 'gx', 'gy')
- atom_charge: float32 [4, 64, 1024], P(None, 'gx', 'gy')
Inputs may be any that keep to these rules, and one draw needn't show every extreme that they name: `atom_cells`: each atom lies in its block: along x cells 8 bx to 8 bx + 7, along y likewise with by, along z cells 8 (bz + 1) to 8 (bz + 2) - 1; every block holds exactly 16 atoms.
All inputs are finite; a program needn't handle non-finite values.
Results may differ from a plain program's by a relative error of at most 0.0003.
Values sent between devices are 32-bit elements; how exact they have to be, the bound alone decides.
No kernel may reach another device: no remote copies, remote signals or barrier semaphores. Data moves between devices by JAX's collectives and lax.ppermute only.
A program may use at most 192 MiB of HBM per device.

v0:
```python
import jax
import jax.numpy as jnp
from jax import lax
from jax.sharding import PartitionSpec as P

NX = 512
NY = 512
NZ = 256
BLOCK = 8
SLOTS = 16
ZBLOCKS = 4
RADIAL = 16
SPECIES = 2
ZROWS = 35


EWALD_BETA = 1.0
far_cell = -100000


def extended(x, sides, width):
    for axis, dim in sides:
        size, length = (lax.axis_size(axis), x.shape[dim])
        up = [(i, (i + 1) % size) for i in range(size)]
        down = [(j, i) for i, j in up]
        last = lax.slice_in_dim(x, length - width, length, axis=dim)
        leading = lax.slice_in_dim(x, 0, width, axis=dim)
        before = lax.ppermute(last, axis, up)
        after = lax.ppermute(leading, axis, down)
        x = jnp.concatenate([before, x, after], axis=dim)
    return x


def spline(fraction):
    remain = 1.0 - fraction
    square = fraction * fraction
    cube_term = square * fraction
    weights = jnp.stack(
        [
            remain * remain * remain / 6.0,
            (3.0 * cube_term - 6.0 * square + 4.0) / 6.0,
            (-3.0 * cube_term + 3.0 * square + 3.0 * fraction + 1.0) / 6.0,
            cube_term / 6.0,
        ]
    )
    slopes = jnp.stack(
        [
            -0.5 * remain * remain,
            0.5 * (3.0 * square - 4.0 * fraction),
            0.5 * (-3.0 * square + 2.0 * fraction + 1.0),
            0.5 * square,
        ]
    )
    return (weights, slopes)


def stencil(local_cell, values):
    length = BLOCK + 3
    places = jnp.arange(length, dtype=jnp.int32).reshape((length,) + (1,) * local_cell.ndim)
    summed = jnp.zeros((length,) + local_cell.shape, jnp.float32)
    for offset in range(4):
        summed = summed + jnp.where(
            places == local_cell[None] + offset, values[offset][None], jnp.float32(0.0)
        )
    return summed


def wrap_gap(spacing, period):
    spacing = jnp.where(spacing > period // 2, spacing - period, spacing)
    return jnp.where(spacing < -(period // 2), spacing + period, spacing)


def neighbours(tensor, width_x, width_y):
    layers = tensor.shape[-4] - 2
    pieces = []
    for shift_z in range(3):
        for shift_x in range(3):
            for shift_y in range(3):
                pieces.append(
                    tensor[
                        ...,
                        shift_z : shift_z + layers,
                        shift_x : shift_x + width_x,
                        shift_y : shift_y + width_y,
                        :,
                    ]
                )
    return jnp.concatenate(pieces, axis=-1)


def pair_terms(own_cells, own_frac, near_cells, near_frac, near_kinds):
    gap_list = []
    for component in range(3):
        cell_gap = near_cells[component][..., None, :] - own_cells[component][..., :, None]
        if component == 0:
            cell_gap = wrap_gap(cell_gap, NX)
        if component == 1:
            cell_gap = wrap_gap(cell_gap, NY)
        gap_list.append(
            cell_gap.astype(jnp.float32)
            + (near_frac[component][..., None, :] - own_frac[component][..., :, None])
        )
    ratio_sq = (
        gap_list[0] * gap_list[0] + gap_list[1] * gap_list[1] + gap_list[2] * gap_list[2]
    ) / float(BLOCK * BLOCK)
    row_index = jnp.arange(SLOTS, dtype=jnp.int32)[:, None]
    col_index = jnp.arange(27 * SLOTS, dtype=jnp.int32)[None, :]
    keep_mask = col_index != row_index + 13 * SLOTS
    remain = 1.0 - ratio_sq
    smooth = jnp.where(keep_mask & (ratio_sq < 1.0), remain * remain, jnp.float32(0.0))
    argument = jnp.minimum(2.0 * ratio_sq - 1.0, 1.0)
    masked = [
        jnp.where(near_kinds[..., None, :] == species_index, smooth, jnp.float32(0.0))
        for species_index in range(SPECIES)
    ]
    previous = jnp.ones_like(argument)
    current = argument
    features = [[] for species_index in range(SPECIES)]
    for degree in range(RADIAL):
        if degree == 0:
            chebyshev = previous
        elif degree == 1:
            chebyshev = current
        else:
            chebyshev = 2.0 * argument * current - previous
            previous = current
            current = chebyshev
        for species_index in range(SPECIES):
            features[species_index].append(
                jnp.sum(masked[species_index] * chebyshev, axis=-1) / SLOTS
            )
    return jnp.stack([item_value for group_list in features for item_value in group_list], axis=0)


def describe(ext_cells, ext_frac, ext_kinds, groups):
    layers = ext_cells.shape[1]
    width_x = ext_cells.shape[2] - 2
    width_y = ext_cells.shape[3] - 2
    padding = ((0, 0), (1, 1), (0, 0), (0, 0), (0, 0))
    near_cells = neighbours(jnp.pad(ext_cells, padding, constant_values=far_cell), width_x, width_y)
    near_frac = neighbours(jnp.pad(ext_frac, padding), width_x, width_y)
    near_kinds = neighbours(jnp.pad(ext_kinds, padding[1:]), width_x, width_y)
    own_cells = ext_cells[:, :, 1:-1, 1:-1, :]
    own_frac = ext_frac[:, :, 1:-1, 1:-1, :]
    per_group = layers * width_x * width_y // groups

    def grouped(tensor):
        return jnp.moveaxis(
            tensor.reshape(tensor.shape[:-4] + (groups, per_group, tensor.shape[-1])), -3, 0
        )

    def layer_terms(inputs):
        return pair_terms(inputs[0], inputs[1], inputs[2], inputs[3], inputs[4])

    result = lax.map(
        layer_terms,
        (
            grouped(own_cells),
            grouped(own_frac),
            grouped(near_cells),
            grouped(near_frac),
            grouped(near_kinds),
        ),
    )
    return jnp.moveaxis(result, 0, 1).reshape(SPECIES * RADIAL, layers * width_x * width_y * SLOTS)


def network(features, species_ids, w_first, b_first, w_second, b_second, w_out, b_out):
    highest = lax.Precision.HIGHEST
    result = jnp.zeros((2, features.shape[1]), jnp.float32)
    for species_index in range(SPECIES):
        first_layer = jnp.tanh(
            jnp.dot(
                w_first[species_index].T,
                features,
                precision=highest,
                preferred_element_type=jnp.float32,
            )
            + b_first[species_index][:, None]
        )
        second = jnp.tanh(
            jnp.dot(
                w_second[species_index].T,
                first_layer,
                precision=highest,
                preferred_element_type=jnp.float32,
            )
            + b_second[species_index][:, None]
        )
        output = (
            jnp.dot(
                w_out[species_index].T,
                second,
                precision=highest,
                preferred_element_type=jnp.float32,
            )
            + b_out[species_index][:, None]
        )
        result = result + jnp.where(species_ids[None, :] == species_index, output, jnp.float32(0.0))
    return result


def charge_regions(cell_ids, fraction, charge):
    local_cell = jnp.remainder(cell_ids, BLOCK)
    weights, slopes = spline(fraction)
    along_x = stencil(local_cell[0], weights[:, 0])
    along_y = stencil(local_cell[1], weights[:, 1])
    along_z = stencil(local_cell[2], weights[:, 2]) * charge[None]
    return jnp.einsum(
        "xbefa,ybefa,zbefa->befxyz", along_x, along_y, along_z, precision=lax.Precision.HIGHEST
    )


def fold_blocks(regions, block_axis, region_axis, keep_tail):
    shifted_axes = jnp.moveaxis(regions, (block_axis, region_axis), (-2, -1))
    core_part = shifted_axes[..., :BLOCK]
    tail_part = shifted_axes[..., BLOCK:]
    leading = [(0, 0)] * (tail_part.ndim - 2)
    tail_part = jnp.pad(tail_part, leading + [(0, 0), (0, BLOCK - 3)])
    if keep_tail:
        core_part = jnp.pad(core_part, leading + [(0, 1), (0, 0)])
        tail_part = jnp.pad(tail_part, leading + [(1, 0), (0, 0)])
    else:
        tail_part = jnp.pad(tail_part, leading + [(1, 0), (0, 0)])[..., :-1, :]
    combined = core_part + tail_part
    return combined.reshape(combined.shape[:-2] + (combined.shape[-2] * BLOCK,))


def spread_grid(regions, width_x, width_y):
    folded = fold_blocks(regions, 1, 3, False)
    folded = fold_blocks(folded, 1, 2, False)
    folded = fold_blocks(folded, 0, 1, True)
    return folded[BLOCK + 1 : BLOCK + 1 + width_x, BLOCK + 1 : BLOCK + 1 + width_y, :ZROWS]


def cut_regions(tensor, dim_index, block_count, first_index):
    shifted_axes = jnp.moveaxis(tensor, dim_index, -1)
    needed = first_index + BLOCK * (block_count + 1) - shifted_axes.shape[-1]
    shifted_axes = jnp.pad(shifted_axes, [(0, 0)] * (shifted_axes.ndim - 1) + [(0, needed)])
    core_part = shifted_axes[..., first_index : first_index + BLOCK * block_count].reshape(
        shifted_axes.shape[:-1] + (block_count, BLOCK)
    )
    tail_part = shifted_axes[
        ..., first_index + BLOCK : first_index + BLOCK * (block_count + 1)
    ].reshape(shifted_axes.shape[:-1] + (block_count, BLOCK))[..., :3]
    return jnp.concatenate([core_part, tail_part], axis=-1)


def potential_regions(padded, count_x, count_y):
    pieces = cut_regions(padded, 0, count_x, 1)
    pieces = cut_regions(pieces, 0, count_y, 1)
    pieces = cut_regions(pieces, 0, ZBLOCKS, 0)
    return jnp.transpose(pieces, (4, 0, 2, 1, 3, 5))


def interpolate(regions, cell_ids, fraction):
    highest = lax.Precision.HIGHEST
    local_cell = jnp.remainder(cell_ids, BLOCK)
    weights, slopes = spline(fraction)
    along_x = stencil(local_cell[0], weights[:, 0])
    along_y = stencil(local_cell[1], weights[:, 1])
    along_z = stencil(local_cell[2], weights[:, 2])
    slope_x = stencil(local_cell[0], slopes[:, 0])
    slope_y = stencil(local_cell[1], slopes[:, 1])
    slope_z = stencil(local_cell[2], slopes[:, 2])
    inner_sum = jnp.einsum("befxyz,zbefa->befxya", regions, along_z, precision=highest)
    inner_slope = jnp.einsum("befxyz,zbefa->befxya", regions, slope_z, precision=highest)
    potential = jnp.einsum(
        "befxya,xbefa,ybefa->befa", inner_sum, along_x, along_y, precision=highest
    )
    gradient = jnp.stack(
        [
            jnp.einsum("befxya,xbefa,ybefa->befa", inner_sum, slope_x, along_y, precision=highest),
            jnp.einsum("befxya,xbefa,ybefa->befa", inner_sum, along_x, slope_y, precision=highest),
            jnp.einsum(
                "befxya,xbefa,ybefa->befa", inner_slope, along_x, along_y, precision=highest
            ),
        ]
    )
    return (potential, gradient)


def influence(wave_z, wave_x, wave_y):

    def axis_terms(wave_index, length):
        signed = (
            jnp.where(wave_index > length // 2, wave_index - length, wave_index).astype(jnp.float32)
            / length
        )
        smooth = 2.0 / 3.0 + jnp.cos(2.0 * jnp.pi / length * wave_index.astype(jnp.float32)) / 3.0
        return (signed * signed, smooth * smooth)

    square_z, factor_z = axis_terms(wave_z, NZ)
    square_x, factor_x = axis_terms(wave_x, NX)
    square_y, factor_y = axis_terms(wave_y, NY)
    wave_sq = square_z[:, None, None] + square_x[None, :, None] + square_y[None, None, :]
    spread = factor_z[:, None, None] * factor_x[None, :, None] * factor_y[None, None, :]
    safe_sq = jnp.where(wave_sq > 0.0, wave_sq, 1.0)
    raw_value = jnp.exp(-((jnp.pi / EWALD_BETA) ** 2) * safe_sq) / (
        jnp.pi * float(NX * NY * NZ) * safe_sq * spread
    )
    return jnp.where(wave_sq > 0.0, raw_value, jnp.float32(0.0))


def twiddle(length):
    index_row = jnp.arange(length, dtype=jnp.int32)
    angles = (
        2.0
        * jnp.pi
        / length
        * (index_row[:, None] * index_row[None, :] % length).astype(jnp.float32)
    )
    return (jnp.cos(angles), jnp.sin(angles))


def rotate(real_part, imag_part, einsum_form, length, sign_value):
    highest = lax.Precision.HIGHEST
    cosine, sine_table = twiddle(length)
    new_real = jnp.einsum(
        einsum_form, real_part, cosine, precision=highest
    ) - sign_value * jnp.einsum(einsum_form, imag_part, sine_table, precision=highest)
    new_imag = jnp.einsum(
        einsum_form, imag_part, cosine, precision=highest
    ) + sign_value * jnp.einsum(einsum_form, real_part, sine_table, precision=highest)
    return (new_real, new_imag)


def transform(real_part, imag_part, sign_value):
    for einsum_form, length in (
        ("zxy,yk->zxk", real_part.shape[2]),
        ("zxy,xk->zky", real_part.shape[1]),
    ):
        real_part, imag_part = rotate(real_part, imag_part, einsum_form, length, sign_value)
    return (real_part, imag_part)


def shards(atom_cells, atom_frac, species, w_first, b_first, w_second, b_second, w_out, b_out):
    highest = lax.Precision.HIGHEST
    layers, width_x, lane_width = species.shape
    width_y = lane_width // SLOTS
    cell_ids = atom_cells.reshape(3, layers, width_x, width_y, SLOTS)
    fraction = atom_frac.reshape(3, layers, width_x, width_y, SLOTS)
    species_ids = species.reshape(layers, width_x, width_y, SLOTS)
    packed = jnp.concatenate(
        [cell_ids.astype(jnp.float32), fraction, species_ids[None].astype(jnp.float32)], axis=0
    )
    cycle_atoms = extended(packed, (("gx", 2), ("gy", 3)), 1)
    cycle_cells = cycle_atoms[0:3].astype(jnp.int32)
    cycle_frac = cycle_atoms[3:6]
    cycle_kinds = cycle_atoms[6].astype(jnp.int32)
    features = describe(cycle_cells, cycle_frac, cycle_kinds, layers)
    outputs = network(
        features, species_ids.reshape(-1), w_first, b_first, w_second, b_second, w_out, b_out
    )
    outputs = outputs.reshape(2, layers, width_x, width_y, SLOTS)
    short_energy = outputs[0]
    charge = outputs[1]
    cycle_charge = extended(charge, (("gx", 1), ("gy", 2)), 1)
    size_x = width_x * BLOCK
    size_y = width_y * BLOCK
    charge_grid = spread_grid(charge_regions(cycle_cells, cycle_frac, cycle_charge), size_x, size_y)
    row_cells = BLOCK - 1 + jnp.arange(ZROWS, dtype=jnp.int32)
    wave_index = jnp.arange(NZ, dtype=jnp.int32)
    angles = 2.0 * jnp.pi / NZ * (row_cells[:, None] * wave_index[None, :] % NZ).astype(jnp.float32)
    cosine = jnp.cos(angles)
    sine_table = jnp.sin(angles)
    spectrum = jnp.stack(
        [
            jnp.einsum("xyz,zk->xyk", charge_grid, cosine, precision=highest),
            -jnp.einsum("xyz,zk->xyk", charge_grid, sine_table, precision=highest),
        ]
    )
    count_x = lax.axis_size("gx")
    count_y = lax.axis_size("gy")
    planes = NZ // (count_x * count_y)
    outgoing = spectrum.reshape(2, size_x, size_y, count_x, count_y, planes).transpose(
        3, 4, 0, 1, 2, 5
    )
    incoming = lax.all_to_all(
        outgoing.reshape(count_x * count_y, 2, size_x, size_y, planes),
        ("gx", "gy"),
        split_axis=0,
        concat_axis=0,
        tiled=True,
    )
    incoming = incoming.reshape(count_x, count_y, 2, size_x, size_y, planes)
    slab_data = incoming.transpose(2, 5, 0, 3, 1, 4).reshape(
        2, planes, count_x * size_x, count_y * size_y
    )
    real_part, imag_part = transform(slab_data[0], slab_data[1], -1.0)
    first_plane = lax.axis_index(("gx", "gy")) * planes
    filter_values = influence(
        first_plane + jnp.arange(planes, dtype=jnp.int32),
        jnp.arange(NX, dtype=jnp.int32),
        jnp.arange(NY, dtype=jnp.int32),
    )
    real_part, imag_part = transform(filter_values * real_part, filter_values * imag_part, 1.0)
    filtered = (
        jnp.stack([real_part, imag_part])
        .reshape(2, planes, count_x, size_x, count_y, size_y)
        .transpose(2, 4, 0, 3, 5, 1)
    )
    returned = lax.all_to_all(
        filtered.reshape(count_x * count_y, 2, size_x, size_y, planes),
        ("gx", "gy"),
        split_axis=0,
        concat_axis=0,
        tiled=True,
    )
    returned = returned.reshape(count_x, count_y, 2, size_x, size_y, planes)
    columns = returned.transpose(2, 3, 4, 0, 1, 5).reshape(2, size_x, size_y, NZ)
    potential_grid = jnp.einsum("xyk,zk->xyz", columns[0], cosine, precision=highest) - jnp.einsum(
        "xyk,zk->xyz", columns[1], sine_table, precision=highest
    )
    padded = extended(potential_grid, (("gx", 0), ("gy", 1)), 2)
    regions = potential_regions(padded, width_x, width_y)
    potential, gradient = interpolate(regions, cell_ids, fraction)
    energy = short_energy + 0.5 * charge * potential
    atom_force = -charge[None] * gradient
    return (
        energy.reshape(layers, width_x, lane_width),
        atom_force.reshape(3, layers, width_x, lane_width),
        charge.reshape(layers, width_x, lane_width),
    )


def solution(mesh):
    return jax.shard_map(
        shards,
        mesh=mesh,
        in_specs=(
            P(None, None, "gx", "gy"),
            P(None, None, "gx", "gy"),
            P(None, "gx", "gy"),
            P(),
            P(),
            P(),
            P(),
            P(),
            P(),
        ),
        out_specs=(P(None, "gx", "gy"), P(None, None, "gx", "gy"), P(None, "gx", "gy")),
        check_vma=False,
    )
```

profile of v0, /device:TPU:1, one launch (start us, length us, event | category | flops | bytes accessed | tf_op | source)
XLA Modules:
  0.0 668.7 jit_solution(4409513775158754018)
XLA Ops:
  44.7 38.6 %while.13 = (s32[]{:T(128)}, f32[4,32,32,16]{3,2,1,0:T(8,128)}, s32[4,32,432]{2,1,0:T(8,128)}, s32[4,3,32,432]{3,2,1,0:T(8,128)S(1)}, s32[4,3,32,16]{3,2,0,1:T(8...) while((s32[]{:T(128)}, f32[4,32,32,16]{3,2,1,0:T(8,128)}, ...), condition=%wide.region_33.34_spmd, body=%wide.region_0.33_spmd.sunk | while | flops 29009684 | bytes 3203361 | solution.py:155
  45.8 7.3 %multiply_reduce_fusion.38 = (f32[32,16]{1,0:T(8,128)S(1)}, f32[32,16]{1,0:T(8,128)S(1)}, f32[32,16]{1,0:T(8,128)S(1)}, f32[32,16]{1,0:T(8,128)S(1)}, f32[32,16]...) fusion(f32[32,16]{1,0:T(8,128)S(1)} %get-tuple-element.542, ...), kind=kLoop, calls=%fused_computation.12.clone.1 | loop fusion | flops 28958720 | bytes 444160 | tf_op jit(solution)/shard_map/while/body/eval_jaxpr/reduce_sum | solution.py:130
  55.4 7.3 %multiply_reduce_fusion.38 = (f32[32,16]{1,0:T(8,128)S(1)}, f32[32,16]{1,0:T(8,128)S(1)}, f32[32,16]{1,0:T(8,128)S(1)}, f32[32,16]{1,0:T(8,128)S(1)}, f32[32,16]...) fusion(f32[32,16]{1,0:T(8,128)S(1)} %get-tuple-element.542, ...), kind=kLoop, calls=%fused_computation.12.clone.1 | loop fusion | flops 28958720 | bytes 444160 | tf_op jit(solution)/shard_map/while/body/eval_jaxpr/reduce_sum | solution.py:130
  65.1 7.3 %multiply_reduce_fusion.38 = (f32[32,16]{1,0:T(8,128)S(1)}, f32[32,16]{1,0:T(8,128)S(1)}, f32[32,16]{1,0:T(8,128)S(1)}, f32[32,16]{1,0:T(8,128)S(1)}, f32[32,16]...) fusion(f32[32,16]{1,0:T(8,128)S(1)} %get-tuple-element.542, ...), kind=kLoop, calls=%fused_computation.12.clone.1 | loop fusion | flops 28958720 | bytes 444160 | tf_op jit(solution)/shard_map/while/body/eval_jaxpr/reduce_sum | solution.py:130
  74.8 7.3 %multiply_reduce_fusion.38 = (f32[32,16]{1,0:T(8,128)S(1)}, f32[32,16]{1,0:T(8,128)S(1)}, f32[32,16]{1,0:T(8,128)S(1)}, f32[32,16]{1,0:T(8,128)S(1)}, f32[32,16]...) fusion(f32[32,16]{1,0:T(8,128)S(1)} %get-tuple-element.542, ...), kind=kLoop, calls=%fused_computation.12.clone.1 | loop fusion | flops 28958720 | bytes 444160 | tf_op jit(solution)/shard_map/while/body/eval_jaxpr/reduce_sum | solution.py:130
  90.5 5.0 collective-permute-start.4
  105.4 23.6 %fusion.19 = f32[4,10,11,11,6,11]{3,5,2,1,4,0:T(8,128)} fusion(f32[4,6,10,16,11]{3,4,2,1,0:T(8,128)S(1)} %add_bitcast_fusion.1, f32[4,6,10,16,11]{3,4,2,1,0:T(8,128)S(1)} %add_bitcast_fusion.2, f32[4,6,10,16]{3,2,1,0:T(8,128)S(1)} %pad_maximum_fusion.25, f32[4,6,10,16]{3,2,1,0:T(8,128)S(1)} %get-tuple-element.281, ...), kind=kOutput, calls=%fused_computation.131 | convolution fusion | flops 62304000 | bytes 1753920 | tf_op jit(solution)/shard_map/xbefa,ybefa,zbefa->befxyz/dot_general | solution.py:209
  133.7 5.4 copy_bitcast_fusion
  143.6 5.5 copy.155
  156.0 5.5 copy.157
  174.8 9.4 %reshape.1119 = f32[128,1,8192]{2,1,0:T(1,128)} reshape(f32[128,2,2,32,64]{4,3,2,1,0:T(8,128)} %bitcast.606) | data formatting | bytes 8388608
  184.2 12.4 %all-to-all-start = ((f32[128,1,8192]{2,1,0:T(1,128)}), f32[128,1,8192]{2,1,0:T(1,128)}, u32[]{:S(2)}, u32[]{:S(2)}) async-start(f32[128,1,8192]{2,1,0:T(1,128)} %reshape.1119), calls=%async_computation | async-start | bytes 8388608 | tf_op jit(solution)/shard_map/all_to_all | solution.py:379
  196.9 50.8 %all-to-all-done = f32[128,1,8192]{2,1,0:T(1,128)} async-done(((f32[128,1,8192]{2,1,0:T(1,128)}), f32[128,1,8192]{2,1,0:T(1,128)}, u32[]{:S(2)}, u32[]{:S(2)}) %all-to-all-start) | async-done | bytes 4194336 | tf_op jit(solution)/shard_map/all_to_all | solution.py:379
  248.3 13.8 %reduce.22 = f32[128,8192]{1,0:T(8,128)} reduce(f32[128,1,8192]{2,1,0:T(1,128)} %all-to-all-done, f32[]{:T(128)} %broadcast.2637), dimensions={1}, to_apply=%all_to_all.6.reduce_sub_computation | reduce | bytes 8388612 | tf_op jit(solution)/shard_map/all_to_all | solution.py:379
  262.1 7.9 %reshape.1120 = f32[128,2,2,32,64]{4,3,2,1,0:T(8,128)} reshape(f32[128,8192]{1,0:T(8,128)} %reduce.22) | data formatting | bytes 8388608
  269.9 6.9 %fusion.305 = (f32[1,2,16,32,8,64]{5,3,1,0,4,2:T(8,128)S(1)}, f32[1,2,16,32,8,64]{5,3,1,0,4,2:T(8,128)}) fusion(f32[2,2,16,32,8,64]{5,3,1,0,4,2:T(8,128)} %bitcast.602), kind=kLoop, calls=%fused_computation.659 | loop fusion | bytes 8388608 | tf_op jit(solution)/shard_map/slice | solution.py:390
  276.9 5.7 copy.160
  286.0 8.9 %fusion.73 = f32[2,512,512]{2,1,0:T(8,128)} fusion(f32[2,512,512]{2,1,0:T(8,128)S(1)} %squeeze.54), kind=kOutput, calls=%fused_computation.257 | convolution fusion | flops 3224895488 | bytes 4194304 | tf_op jit(solution)/shard_map/zxy,yk->zxk/dot_general | solution.py:319
  295.0 5.7 copy.162
  300.7 4.9 squeeze.55
  305.6 9.1 %fusion.71 = f32[2,512,512]{2,1,0:T(8,128)S(1)} fusion(f32[2,512,512]{2,1,0:T(8,128)} %squeeze.55), kind=kOutput, calls=%fused_computation.255 | convolution fusion | flops 3224895488 | bytes 4194304 | tf_op jit(solution)/shard_map/zxy,yk->zxk/dot_general | solution.py:322
  314.7 8.7 %multiply_subtract_fusion.13 = f32[2,512,512]{2,1,0:T(8,128)S(1)} fusion(f32[2,512,512]{2,1,0:T(8,128)S(1)} %copy-done.42, f32[2,512,512]{2,1,0:T(8,128)S(1)} %copy-done.11), kind=kOutput, calls=%fused_computation.202 | convolution fusion | flops 3225944064 | bytes 6291456 | tf_op jit(solution)/shard_map/zxy,yk->zxk/dot_general | solution.py:321
  323.5 7.3 %fusion.81 = f32[512,2,512]{2,0,1:T(8,128)S(1)} fusion(f32[2,512,512]{2,1,0:T(8,128)S(1)} %multiply_subtract_fusion.13), kind=kOutput, calls=%fused_computation.265 | convolution fusion | flops 3224895488 | bytes 4194304 | tf_op jit(solution)/shard_map/zxy,xk->zky/dot_general | solution.py:319
  330.8 8.9 %multiply_add_fusion.1 = f32[2,512,512]{2,1,0:T(8,128)S(1)} fusion(f32[2,512,512]{2,1,0:T(8,128)S(1)} %fusion.71, f32[2,512,512]{2,1,0:T(8,128)S(1)} %squeeze.54), kind=kOutput, calls=%fused_computation.201 | convolution fusion | flops 3225944064 | bytes 6291456 | tf_op jit(solution)/shard_map/zxy,yk->zxk/dot_general | solution.py:324
  339.7 7.3 %fusion.79 = f32[512,2,512]{2,0,1:T(8,128)S(1)} fusion(f32[2,512,512]{2,1,0:T(8,128)S(1)} %multiply_add_fusion.1), kind=kOutput, calls=%fused_computation.263 | convolution fusion | flops 3224895488 | bytes 4194304 | tf_op jit(solution)/shard_map/zxy,xk->zky/dot_general | solution.py:322
  347.1 8.4 %bitcast_multiply_fusion.1 = f32[2,512,512]{2,1,0:T(8,128)S(1)} fusion(f32[512,2,512]{2,0,1:T(8,128)S(1)} %fusion.81, f32[2,512,512]{2,1,0:T(8,128)S(1)} %multiply_add_fusion.1, f32[512]{0:T(512)S(1)} %get-tuple-element.452, f32[2,512]{1,0:T(2,128)S(1)} %broadcast_multiply_fusion, f32[512]{0:T(512)S(1)} %get-tuple-element.451, ...), kind=kOutput, calls=%fused_computation.198 | convolution fusion | flops 3231186944 | bytes 6303744 | tf_op jit(solution)/shard_map/zxy,xk->zky/dot_general | solution.py:321
  355.4 8.6 %fusion.69 = f32[2,512,512]{2,1,0:T(8,128)S(1)} fusion(f32[2,512,512]{2,1,0:T(8,128)S(1)} %bitcast_multiply_fusion.1), kind=kOutput, calls=%fused_computation.253 | convolution fusion | flops 3224895488 | bytes 4194304 | tf_op jit(solution)/shard_map/zxy,yk->zxk/dot_general | solution.py:319
  364.1 8.2 %bitcast_multiply_fusion = f32[2,512,512]{2,1,0:T(8,128)S(1)} fusion(f32[512,2,512]{2,0,1:T(8,128)S(1)} %fusion.79, f32[2,512,512]{2,1,0:T(8,128)S(1)} %multiply_subtract_fusion.13, f32[512]{0:T(512)S(1)} %get-tuple-element.452, f32[2,512]{1,0:T(2,128)S(1)} %broadcast_multiply_fusion, f32[512]{0:T(512)S(1)} %get-tuple-element.451, ...), kind=kOutput, calls=%fused_computation.197 | convolution fusion | flops 3231186944 | bytes 6303744 | tf_op jit(solution)/shard_map/zxy,xk->zky/dot_general | solution.py:324
  372.2 8.4 %fusion.67 = f32[2,512,512]{2,1,0:T(8,128)S(1)} fusion(f32[2,512,512]{2,1,0:T(8,128)S(1)} %bitcast_multiply_fusion), kind=kOutput, calls=%fused_computation.251 | convolution fusion | flops 3224895488 | bytes 4194304 | tf_op jit(solution)/shard_map/zxy,yk->zxk/dot_general | solution.py:322
  380.6 8.9 %convolution_subtract_fusion = f32[2,512,512]{2,1,0:T(8,128)S(1)} fusion(f32[2,512,512]{2,1,0:T(8,128)S(1)} %fusion.69, f32[2,512,512]{2,1,0:T(8,128)S(1)} %bitcast_multiply_fusion), kind=kOutput, calls=%fused_computation.230 | convolution fusion | flops 3225419776 | bytes 6291456 | tf_op jit(solution)/shard_map/zxy,yk->zxk/dot_general | solution.py:321
  389.5 7.3 %fusion.77 = f32[512,2,512]{2,0,1:T(8,128)S(1)} fusion(f32[2,512,512]{2,1,0:T(8,128)S(1)} %convolution_subtract_fusion), kind=kOutput, calls=%fused_computation.261 | convolution fusion | flops 3224895488 | bytes 4194304 | tf_op jit(solution)/shard_map/zxy,xk->zky/dot_general | solution.py:319
  396.9 8.7 %convolution_add_fusion.6 = f32[2,512,512]{2,1,0:T(8,128)S(1)} fusion(f32[2,512,512]{2,1,0:T(8,128)S(1)} %fusion.67, f32[2,512,512]{2,1,0:T(8,128)S(1)} %bitcast_multiply_fusion.1), kind=kOutput, calls=%fused_computation.229 | convolution fusion | flops 3225419776 | bytes 6291456 | tf_op jit(solution)/shard_map/zxy,yk->zxk/dot_general | solution.py:324
  405.5 9.1 %fusion.75 = f32[512,2,512]{2,0,1:T(8,128)} fusion(f32[2,512,512]{2,1,0:T(8,128)S(1)} %convolution_add_fusion.6), kind=kOutput, calls=%fused_computation.259 | convolution fusion | flops 3224895488 | bytes 4194304 | tf_op jit(solution)/shard_map/zxy,xk->zky/dot_general | solution.py:322
  414.7 9.1 %subtract_bitcast_fusion = f32[2,512,512]{2,1,0:T(8,128)} fusion(f32[512,2,512]{2,0,1:T(8,128)S(1)} %fusion.77, f32[2,512,512]{2,1,0:T(8,128)S(1)} %convolution_add_fusion.6), kind=kOutput, calls=%fused_computation.200 | convolution fusion | flops 3225419776 | bytes 6291456 | tf_op jit(solution)/shard_map/zxy,xk->zky/dot_general | solution.py:321
  428.6 5.0 copy.170
  433.6 9.0 %add_bitcast_fusion = f32[2,512,512]{2,1,0:T(8,128)} fusion(f32[512,2,512]{2,0,1:T(8,128)S(1)} %copy-done.10, f32[2,512,512]{2,1,0:T(8,128)S(1)} %convolution_subtract_fusion), kind=kOutput, calls=%fused_computation.199 | convolution fusion | flops 3225419776 | bytes 6291456 | tf_op jit(solution)/shard_map/zxy,xk->zky/dot_general | solution.py:324
  454.7 9.4 %reshape.1121 = f32[128,1,8192]{2,1,0:T(1,128)} reshape(f32[128,2,2,32,64]{4,3,2,1,0:T(8,128)} %bitcast.605) | data formatting | bytes 8388608
  464.1 7.5 %all-to-all-start.1 = ((f32[128,1,8192]{2,1,0:T(1,128)}), f32[128,1,8192]{2,1,0:T(1,128)}, u32[]{:S(2)}, u32[]{:S(2)}) async-start(f32[128,1,8192]{2,1,0:T(1,128)} %reshape.1121), calls=%async_computation.1 | async-start | bytes 8388608 | tf_op jit(solution)/shard_map/all_to_all | solution.py:403
  474.8 48.1 %all-to-all-done.1 = f32[128,1,8192]{2,1,0:T(1,128)} async-done(((f32[128,1,8192]{2,1,0:T(1,128)}), f32[128,1,8192]{2,1,0:T(1,128)}, u32[]{:S(2)}, u32[]{:S(2)}) %all-to-all-start.1) | async-done | bytes 4194336 | tf_op jit(solution)/shard_map/all_to_all | solution.py:403
  522.9 13.8 %reduce.23 = f32[128,8192]{1,0:T(8,128)} reduce(f32[128,1,8192]{2,1,0:T(1,128)} %all-to-all-done.1, f32[]{:T(128)} %broadcast.2637), dimensions={1}, to_apply=%all_to_all.7.reduce_sub_computation | reduce | bytes 8388612 | tf_op jit(solution)/shard_map/all_to_all | solution.py:403
  536.7 8.0 %reshape.1122 = f32[128,2,2,32,64]{4,3,2,1,0:T(8,128)} reshape(f32[128,8192]{1,0:T(8,128)} %reduce.23) | data formatting | bytes 8388608
  551.1 5.2 fusion.22
  556.3 5.2 fusion.51
  590.6 7.8 %reshape.1105 = f32[4,11,8,11,4,8]{5,4,3,2,1,0:T(4,128)} reshape(f32[4,11,8,11,32]{4,3,2,1,0:T(8,128)} %get-tuple-element.242) | data formatting | bytes 991232 | tf_op jit(solution)/shard_map/reshape | solution.py:240
  598.4 9.0 %copy.184 = f32[4,11,8,11,4,8]{5,3,1,2,0,4:T(8,128)} copy(f32[4,11,8,11,4,8]{5,4,3,2,1,0:T(4,128)} %reshape.1105) | data formatting | bytes 991232 | tf_op jit(solution)/shard_map/reshape | solution.py:240
  607.4 5.3 reshape.1106
  621.6 15.4 %multiply_reduce_fusion.30 = f32[4,4,8,16,11]{3,4,2,1,0:T(8,128)S(1)} fusion(f32[4,4,8,16,11]{3,4,2,1,0:T(8,128)S(1)} %copy-done.3, f32[4,11,8,11,4,3]{5,3,1,2,0,4:T(8,128)S(1)} %copy.260, f32[4,11,8,11,4,8]{5,3,1,2,0,4:T(8,128)} %copy.184, f32[4,4,8,16]{3,2,1,0:T(8,128)S(1)} %get-tuple-element.351, f32[4,4,8,16]{3,2,1,0:T(8,128)S(1)} %get-tuple-element.432, ...), kind=kOutput, calls=%fused_computation.119 | convolution fusion | flops 33601920 | bytes 927232 | tf_op jit(solution)/shard_map/befxyz,zbefa->befxya/dot_general | solution.py:267
  637.8 19.8 %multiply_reduce_fusion.31 = (f32[4,4,8,16,11]{3,4,2,1,0:T(8,128)}, f32[4,4,8,16,11]{3,4,2,1,0:T(8,128)}) fusion(f32[4,4,8,16,11]{3,4,2,1,0:T(8,128)} %get-tuple-element.340, f32[4,4,8,16,11]{3,4,2,1,0:T(8,128)S(1)} %copy-done.3, f32[4,4,8,16]{3,2,1,0:T(8,128)} %get-tuple-element.363, s32[4,4,8,16]{3,2,1,0:T(8,128)S(1)} %get-tuple-element.371, ...), kind=kOutput, calls=%fused_computation.120 | convolution fusion | flops 34075008 | bytes 1107456 | tf_op jit(solution)/shard_map/befxyz,zbefa->befxya/dot_general | solution.py:266
  (398 shorter events, 178.0 us)
Async XLA Ops:
  3.9 13.1 %collective-permute-start = (f32[7,4,1,8,16]{4,3,2,1,0:T(8,128)S(1)}, f32[7,4,1,8,16]{4,3,2,1,0:T(8,128)S(1)}, u32[]{:S(2)}, u32[]{:S(2)}) collective-permute-start(f32[7,4,1,8,16]{4,3,2,1,0:T(8,128)S(1)} %get-tuple-element.335), channel_id=1, source_target_pairs={{0,8},{8,16},{16,24},{24,32},{32,40},{40,48},{48,56},{56,64},{64,7... | collective-permute-start | bytes 43016 | tf_op jit(solution)/shard_map/ppermute | solution.py:28
  8.1 8.9 %collective-permute-start.1 = (f32[7,4,1,8,16]{4,3,2,1,0:T(8,128)S(1)}, f32[7,4,1,8,16]{4,3,2,1,0:T(8,128)S(1)}, u32[]{:S(2)}, u32[]{:S(2)}) collective-permute-start(f32[7,4,1,8,16]{4,3,2,1,0:T(8,128)S(1)} %get-tuple-element.336), channel_id=1, source_target_pairs={{8,0},{16,8},{24,16},{32,24},{40,32},{48,40},{56,48},{64,56},{72,6... | collective-permute-start | bytes 43016 | tf_op jit(solution)/shard_map/ppermute | solution.py:29
  17.2 5.7 collective-permute-start.2
  18.9 4.0 collective-permute-start.3
  38.3 3.8 copy-start.19
  38.3 3.8 copy-start.20
  38.3 3.8 copy-start.21
  83.3 2.6 copy-start.41
  83.3 3.6 copy-start.39
  83.3 4.7 copy-start.29
  83.3 4.7 copy-start.40
  85.8 2.5 copy-start.28
  85.8 2.5 copy-start.38
  85.8 2.9 copy-start.33
  85.9 2.9 copy-start.35
  85.9 2.9 copy-start.37
  85.9 3.1 copy-start.34
  85.9 3.1 copy-start.36
  88.0 7.7 %copy-start.8 = (f32[1,3,4,6,10,16]{5,4,3,2,1,0:T(8,128)S(1)}, f32[1,3,4,6,10,16]{5,4,3,2,1,0:T(8,128)}, u32[]{:S(2)}) copy-start(f32[1,3,4,6,10,16]{5,4,3,2,1,0:T(8,128)} %get-tuple-element.285) | copy-start | bytes 138244
  88.0 7.7 %copy-start.9 = (f32[1,3,4,6,10,16]{5,4,3,2,1,0:T(8,128)S(1)}, f32[1,3,4,6,10,16]{5,4,3,2,1,0:T(8,128)}, u32[]{:S(2)}) copy-start(f32[1,3,4,6,10,16]{5,4,3,2,1,0:T(8,128)} %get-tuple-element.286) | copy-start | bytes 138244
  90.5 7.4 %copy-start.12 = (f32[4,4,8,16]{3,2,1,0:T(8,128)}, f32[4,4,8,16]{3,2,1,0:T(8,128)S(1)}, u32[]{:S(2)}) copy-start(f32[4,4,8,16]{3,2,1,0:T(8,128)S(1)} %squeeze.53) | copy-start | bytes 24580
  90.5 7.3 %collective-permute-start.4 = (f32[4,1,8,16]{3,2,1,0:T(8,128)S(1)}, f32[4,1,8,16]{3,2,1,0:T(8,128)S(1)}, u32[]{:S(2)}, u32[]{:S(2)}) collective-permute-start(f32[4,1,8,16]{3,2,1,0:T(8,128)S(1)} %get-tuple-element.417), channel_id=1, source_target_pairs={{0,8},{8,16},{16,24},{24,32},{32,40},{40,48},{48,56},{56,64},{64,7... | collective-permute-start | bytes 6152 | tf_op jit(solution)/shard_map/ppermute | solution.py:28
  95.5 4.7 collective-permute-start.5
  100.2 5.1 collective-permute-start.6
  101.5 3.8 collective-permute-start.7
  184.2 63.5 %all-to-all-start = ((f32[128,1,8192]{2,1,0:T(1,128)}), f32[128,1,8192]{2,1,0:T(1,128)}, u32[]{:S(2)}, u32[]{:S(2)}) async-start(f32[128,1,8192]{2,1,0:T(1,128)} %reshape.1119), calls=%async_computation | async-start | bytes 8388608 | tf_op jit(solution)/shard_map/all_to_all | solution.py:379
  286.0 8.9 %copy-start.2 = (f32[1,2,16,32,8,64]{5,3,1,0,4,2:T(8,128)S(1)}, f32[1,2,16,32,8,64]{5,3,1,0,4,2:T(8,128)}, u32[]{:S(2)}) copy-start(f32[1,2,16,32,8,64]{5,3,1,0,4,2:T(8,128)} %get-tuple-element.241) | copy-start | bytes 6291460
  305.6 9.1 %copy-start.11 = (f32[2,512,512]{2,1,0:T(8,128)S(1)}, f32[2,512,512]{2,1,0:T(8,128)}, u32[]{:S(2)}) copy-start(f32[2,512,512]{2,1,0:T(8,128)} %squeeze.55) | copy-start | bytes 6291460
  305.6 9.1 %copy-start.42 = (f32[2,512,512]{2,1,0:T(8,128)S(1)}, f32[2,512,512]{2,1,0:T(8,128)}, u32[]{:S(2)}) copy-start(f32[2,512,512]{2,1,0:T(8,128)} %fusion.73) | copy-start | bytes 6291460
  428.6 5.0 copy-start.10
  446.9 3.4 copy-start.1
  464.1 7.5 %copy-start.23 = (f32[3,4,4,128]{3,2,1,0:T(4,128)S(1)}, f32[3,4,4,128]{3,2,1,0:T(4,128)}, u32[]{:S(2)}) copy-start(f32[3,4,4,128]{3,2,1,0:T(4,128)} %param.12) | copy-start | bytes 73732
  464.1 58.8 %all-to-all-start.1 = ((f32[128,1,8192]{2,1,0:T(1,128)}), f32[128,1,8192]{2,1,0:T(1,128)}, u32[]{:S(2)}, u32[]{:S(2)}) async-start(f32[128,1,8192]{2,1,0:T(1,128)} %reshape.1121), calls=%async_computation.1 | async-start | bytes 8388608 | tf_op jit(solution)/shard_map/all_to_all | solution.py:403
  561.5 5.9 collective-permute-start.8
  565.2 5.2 collective-permute-start.9
  567.4 3.0 copy-start.24
  572.3 10.9 %collective-permute-start.10 = (f32[36,2,35]{0,1,2:T(2,128)}, f32[36,2,35]{0,1,2:T(2,128)}, u32[]{:S(2)}, u32[]{:S(2)}) collective-permute-start(f32[36,2,35]{0,1,2:T(2,128)} %copy.175), channel_id=1, source_target_pairs={{0,1},{1,2},{2,3},{3,4},{4,5},{5,6},{6,7},{7,0},{8,9},{9,10},{10,1... | collective-permute-start | bytes 30248 | tf_op jit(solution)/shard_map/ppermute | solution.py:28
  573.3 11.1 %collective-permute-start.11 = (f32[36,2,35]{0,1,2:T(2,128)}, f32[36,2,35]{0,1,2:T(2,128)}, u32[]{:S(2)}, u32[]{:S(2)}) collective-permute-start(f32[36,2,35]{0,1,2:T(2,128)} %copy.176), channel_id=1, source_target_pairs={{1,0},{2,1},{3,2},{4,3},{5,4},{6,5},{7,6},{0,7},{9,8},{10,9},{11,1... | collective-permute-start | bytes 30248 | tf_op jit(solution)/shard_map/ppermute | solution.py:29
  578.8 3.7 copy-start.31
  578.8 3.7 copy-start.30
  580.7 4.9 copy-start.25
  580.7 4.9 copy-start.27
  612.7 8.9 %copy-start.3 = (f32[4,4,8,16,11]{3,4,2,1,0:T(8,128)S(1)}, f32[4,4,8,16,11]{3,4,2,1,0:T(8,128)}, u32[]{:S(2)}) copy-start(f32[4,4,8,16,11]{3,4,2,1,0:T(8,128)} %get-tuple-element.339) | copy-start | bytes 270340
  617.4 4.2 copy-start
  657.6 6.2 copy-start.4
  657.6 6.2 copy-start.5
  663.9 3.0 copy-start.13
  663.9 3.0 copy-start.22
  (9 other events, 13.1 us)
where the time goes:
time: 681 us; the launch traced here: 669 us
  matrix products  214 us (31%)
  local copies, waits for them, and re-layouts  201 us (30%)
  waiting for transfers between devices  105 us (15%)
  other arithmetic  101 us (15%)
  starting transfers between devices  44.4 us (7%)
    all_to_all x1, waiting for transfers between devices, shards(): lax.all_to_all(outgoing.reshape(count_x * count_y, 2, size_x, size_y, pla...  50.8 us
    unnamed x96, local copies, waits for them, and re-layouts  49.6 us
    all_to_all x1, waiting for transfers between devices, shards(): lax.all_to_all(filtered.reshape(count_x * count_y, 2, size_x, size_y, pla...  48.1 us
    dot_general x4, matrix products, rotate(): jnp.einsum(einsum_form, imag_part, sine_table, precision=highest)  35.1 us
    dot_general x4, matrix products, rotate(): jnp.einsum(einsum_form, real_part, sine_table, precision=highest)  34.7 us
    dot_general x4, matrix products, rotate(): jnp.einsum(einsum_form, imag_part, cosine, precision=highest)  33.9 us
    dot_general x4, matrix products, rotate(): jnp.einsum(einsum_form, real_part, cosine, precision=highest)  32.2 us
    reduce_sum x4, other arithmetic, pair_terms(): jnp.sum(masked[species_index] * chebyshev, axis=-1) / SLOTS  29.2 us
  transfers between devices with their start and end apart: 14, of which 5 were waited for; matrix products, arithmetic and copies ran while one was open for 4% of the time, Pallas kernels for 0%

commit v1 on v0

v1 whole, which is shorter than its diff:
```python
import functools

import jax
import jax.numpy as jnp
import ml_dtypes
import numpy as np
from jax import lax
from jax.experimental import pallas as pl
from jax.experimental.pallas import tpu as pltpu
from jax.sharding import PartitionSpec as P

NX = 512
NY = 512
NZ = 256
BLOCK = 8
SLOTS = 16
ZBLOCKS = 4
RADIAL = 16
SPECIES = 2
NEURONS = 15
ZROWS = 35
ZPAD = 40
PLANES = 128
EWALD_BETA = 1.0
LANES = 128
PATCH_ROWS = 18
WIRE_ROWS = PATCH_ROWS + 1
NT = (((1,), (1,)), ((), ()))
NN = (((1,), (0,)), ((), ()))
TN = (((0,), (0,)), ((), ()))
VMEM_BYTES = 40 * 1024 * 1024


def high_low(table):
    high = table.astype(ml_dtypes.bfloat16)
    low = (table - high.astype(np.float64)).astype(ml_dtypes.bfloat16)
    return high, low


def split(value):
    high = value.astype(jnp.bfloat16)
    low = (value - high.astype(jnp.float32)).astype(jnp.bfloat16)
    return high, low


def dot(left, right, dims=NN):
    return lax.dot_general(left, right, dims, preferred_element_type=jnp.float32)


def dot3(left, right, dims=NN):
    return (
        dot(left[0], right[0], dims) + dot(left[0], right[1], dims) + dot(left[1], right[0], dims)
    )


def cas(left, right, length):
    angle = 2.0 * np.pi / length * (np.outer(left, right) % length)
    return np.cos(angle) + np.sin(angle)


def wave_order(length):
    half = length // 2
    return np.concatenate([np.arange(half + 1), length - np.arange(1, half)])


def axis_factor(wave, length):
    signed = np.where(wave > length // 2, wave - length, wave) / length
    smooth = 2.0 / 3.0 + np.cos(2.0 * np.pi / length * wave) / 3.0
    return signed**2, np.exp(-((np.pi / EWALD_BETA) ** 2) * signed**2) / smooth**2


def spline_weight(distance):
    away = jnp.abs(distance)
    outer = jnp.maximum(2.0 - away, 0.0)
    inner = jnp.maximum(1.0 - away, 0.0)
    return (outer * outer * outer - 4.0 * (inner * inner * inner)) * (1.0 / 6.0)


def spline_both(distance):
    away = jnp.abs(distance)
    outer = jnp.maximum(2.0 - away, 0.0)
    inner = jnp.maximum(1.0 - away, 0.0)
    outer_sq = outer * outer
    inner_sq = inner * inner
    weight = (outer_sq * outer - 4.0 * (inner_sq * inner)) * (1.0 / 6.0)
    slope = 0.5 * outer_sq - 2.0 * inner_sq
    return weight, jnp.where(distance > 0.0, slope, -slope)


def iota(shape, dim):
    return lax.broadcasted_iota(jnp.int32, shape, dim)


def row_vector(rows):
    return jnp.concatenate(
        [rows[bz * 4 + bx : bz * 4 + bx + 1, :] for bx in range(4) for bz in range(4)], axis=1
    )


def z_distance(pos_z):
    shape = (ZPAD, pos_z.shape[1])
    layer = (iota(shape, 1) // LANES) % ZBLOCKS
    return (iota(shape, 0) - 8 * layer - 1).astype(jnp.float32) - 8.0 * pos_z


def y_distance(pos_y, shape, cell):
    block = (iota(shape, 1) % LANES) // SLOTS
    return (cell - 1 - 8 * block).astype(jnp.float32) - 8.0 * pos_y


def atoms_kernel(
    ext_ref,
    left_ref,
    right_ref,
    packed_ref,
    basis_ref,
    short_ref,
    charge_ref,
    wire_ref,
    near_ref,
    feature_ref,
    weight_ref,
    bias_ref,
):
    lane = iota((LANES, LANES), 1)
    own = ext_ref[...].reshape(LANES, LANES)
    left = left_ref[...].reshape(LANES, LANES)
    right = right_ref[...].reshape(LANES, LANES)
    shifted = [
        jnp.where(lane < SLOTS, pltpu.roll(left, SLOTS, 1), pltpu.roll(own, SLOTS, 1)),
        own,
        jnp.where(
            lane >= LANES - SLOTS,
            pltpu.roll(right, LANES - SLOTS, 1),
            pltpu.roll(own, LANES - SLOTS, 1),
        ),
    ]
    far = jnp.full((4, LANES), 100.0, jnp.float32)
    for dx in range(3):
        for dy in range(3):
            n = dx * 3 + dy
            for c in range(4):
                offset = float((dx - 1, dy - 1, 0, 0)[c])
                for bz in range(ZBLOCKS):
                    row = (c * ZBLOCKS + bz) * 8 + dx
                    near_ref[n, c, 4 + 4 * bz : 8 + 4 * bz, :] = shifted[dy][row : row + 4, :] + offset
                near_ref[n, c, 0:4, :] = far
                near_ref[n, c, 20:24, :] = far

    lane8 = iota((8, LANES), 1)
    for half in range(2):
        mine = [near_ref[4, c, 4 + 8 * half : 12 + 8 * half, :] for c in range(3)]

        def body(n, sums):
            sums = list(sums)
            keep = jnp.where(n == 4, 0.0, 1.0).astype(jnp.float32)
            for dz in range(3):
                near = [
                    near_ref[n, c, 4 * dz + 8 * half : 4 * dz + 8 * half + 8, :] for c in range(4)
                ]
                mine_z = mine[2] - float(dz - 1)
                for turn in range(SLOTS):
                    if turn == 0:
                        got = near
                    else:
                        index = (lane8 & (LANES - SLOTS)) | ((lane8 + turn) & (SLOTS - 1))
                        got = [jnp.take_along_axis(v, index, axis=1) for v in near]
                    gx = got[0] - mine[0]
                    gy = got[1] - mine[1]
                    gz = got[2] - mine_z
                    kind = got[3]
                    remain = jnp.maximum(1.0 - (gx * gx + gy * gy + gz * gz), 0.0)
                    if turn == 0 and dz == 1:
                        remain = remain * keep
                    twice = 2.0 - 4.0 * remain
                    previous = remain * remain
                    current = 0.5 * twice * previous
                    for k in range(RADIAL):
                        if k == 0:
                            term = previous
                        elif k == 1:
                            term = current
                        else:
                            term = twice * current - previous
                            previous, current = current, term
                        sums[k] = sums[k] + term
                        sums[RADIAL + k] = sums[RADIAL + k] + term * kind
            return tuple(sums)

        zero = jnp.zeros((8, LANES), jnp.float32)
        sums = lax.fori_loop(0, 9, body, (zero,) * (2 * RADIAL))
        for k in range(RADIAL):
            one = sums[RADIAL + k] * (1.0 / SLOTS)
            feature_ref[k, 8 * half : 8 * half + 8, :] = sums[k] * (1.0 / SLOTS) - one
            feature_ref[RADIAL + k, 8 * half : 8 * half + 8, :] = one

    features = jnp.concatenate(
        [feature_ref[:, bz * 4 + bx, :] for bx in range(4) for bz in range(4)], axis=1
    )
    weight_ref[...] = jnp.zeros(weight_ref.shape, jnp.float32)
    bias_ref[...] = jnp.zeros(bias_ref.shape, jnp.float32)
    for s in range(SPECIES):
        at = s * 16
        row = s * 72
        weight_ref[0, :, at : at + NEURONS] = packed_ref[row : row + 32, :NEURONS]
        weight_ref[1, at : at + NEURONS, at : at + NEURONS] = packed_ref[row + 32 : row + 47, :NEURONS]
        weight_ref[2, at : at + NEURONS, 2 * s : 2 * s + 2] = packed_ref[row + 48 : row + 63, :2]
        bias_ref[0:1, at : at + NEURONS] = packed_ref[row + 64 : row + 65, :NEURONS]
        bias_ref[1:2, at : at + NEURONS] = packed_ref[row + 65 : row + 66, :NEURONS]
        bias_ref[2:3, 2 * s : 2 * s + 2] = packed_ref[row + 66 : row + 67, :2]
    diagonal = iota((LANES, LANES), 0) == iota((LANES, LANES), 1)

    def layer(n, x, height):
        bias = jnp.sum(
            jnp.where(diagonal[:height], bias_ref[n : n + 1, :], 0.0), axis=1, keepdims=True
        )
        full = lax.dot_general(
            weight_ref[n, :, :height], x, TN, precision=lax.Precision.HIGHEST, preferred_element_type=jnp.float32
        )
        return full + bias

    rows = [near_ref[4, c, 4:20, :] for c in range(4)]
    pos_x, pos_y, pos_z, kinds = [row_vector(r) for r in rows]
    answers = layer(2, jnp.tanh(layer(1, jnp.tanh(layer(0, features, 32)), 32)), 8)
    answer = jnp.where(kinds == 0.0, answers[0:2, :], answers[2:4, :])
    charge = answer[1:2, :]
    for bx in range(4):
        for bz in range(4):
            at = (bx * 4 + bz) * LANES
            short_ref[bz, bx : bx + 1, :] = answer[0:1, at : at + LANES]
            charge_ref[bz, bx : bx + 1, :] = charge[:, at : at + LANES]

    along_z = split(spline_weight(z_distance(pos_z)))
    waves = dot3(split(basis_ref[...]), along_z) * charge
    waves_high, waves_low = split(waves)

    per = 4 * LANES
    carry = [None, None]
    tail = None
    for bx in range(4):
        cut = slice(bx * per, (bx + 1) * per)
        ux, uy = 8.0 * pos_x[:, cut], pos_y[:, cut]
        waves_cut = (waves_high[:, cut], waves_low[:, cut])
        weight_y = spline_weight(y_distance(uy, (64, per), iota((64, per), 0)))
        weight_x = spline_weight((iota((16, per), 0) - 1).astype(jnp.float32) - ux)
        for pair in range(6):
            product = jnp.concatenate(
                [weight_y * weight_x[2 * pair + h : 2 * pair + h + 1, :] for h in range(2)], axis=0
            )
            plane = dot3(waves_cut, split(product), NT)
            if pair < 2 and bx > 0:
                plane = plane + carry[pair]
            if pair >= 4 and bx < 3:
                carry[pair - 4] = plane
            else:
                wire_ref[pl.ds(4 * bx + pair, PLANES, stride=WIRE_ROWS), :] = plane
        place = iota((LANES, per), 0)
        tail_x = spline_weight((place // 3 - 1 - 8 * bx).astype(jnp.float32) - ux)
        tail_y = spline_weight(y_distance(uy, (LANES, per), 64 + place % 3))
        more = dot3(waves_cut, split(tail_x * tail_y), NT)
        tail = more if tail is None else tail + more
    wire_ref[pl.ds(PATCH_ROWS, PLANES, stride=WIRE_ROWS), :] = tail


def pack_weights(w_first, b_first, w_second, b_second, w_out, b_out):
    def wide(part, height):
        return jnp.pad(part, ((0, 0), (0, height - part.shape[1]), (0, LANES - part.shape[2])))

    biases = jnp.stack([b_first, b_second, jnp.pad(b_out, ((0, 0), (0, NEURONS - 2)))], axis=1)
    parts = [wide(w_first, 32), wide(w_second, 16), wide(w_out, 16), wide(biases, 8)]
    return jnp.concatenate(parts, axis=1).reshape(-1, LANES)


def atoms_call(ext, left, right, packed):
    wave = np.arange(PLANES)
    basis = np.zeros((PLANES, ZPAD))
    basis[:, :ZROWS] = cas(wave, np.arange(ZROWS), PLANES)
    f32 = jnp.float32
    return pl.pallas_call(
        atoms_kernel,
        out_shape=(
            jax.ShapeDtypeStruct((4, 4, LANES), f32),
            jax.ShapeDtypeStruct((4, 4, LANES), f32),
            jax.ShapeDtypeStruct((PLANES * WIRE_ROWS, LANES), f32),
        ),
        scratch_shapes=[
            pltpu.VMEM((9, 4, 24, LANES), f32),
            pltpu.VMEM((SPECIES * RADIAL, 16, LANES), f32),
            pltpu.VMEM((3, 32, LANES), f32),
            pltpu.VMEM((8, LANES), f32),
        ],
        compiler_params=pltpu.CompilerParams(vmem_limit_bytes=VMEM_BYTES),
        name="atoms",
    )(ext, left, right, packed, basis.astype(np.float32))


def filter_kernel(terms_ref, squares_ref, row_ref, column_ref, out_ref):
    half = NX // 2
    count = NZ // 4

    def series(square):
        total = None
        for t in range(1, count + 1, 4):
            near = [square + squares_ref[t + n] for n in range(4)]
            parts = [
                (
                    terms_ref[t + n] * near[n + 1] + terms_ref[t + n + 1] * near[n],
                    near[n] * near[n + 1],
                )
                for n in (0, 2)
            ]
            part = (parts[0][0] * parts[1][1] + parts[1][0] * parts[0][1]) / (
                parts[0][1] * parts[1][1]
            )
            total = part if total is None else total + part
        even = square + squares_ref[0]
        extra = terms_ref[0] / jnp.where(even > 0.0, even, 1.0)
        return total + jnp.where(even > 0.0, extra, 0.0)

    edge = series(row_ref[0:8, :] + 0.25) * row_ref[8:16, :] * column_ref[half : half + 8, 1:2]
    edge = edge[0:1, :]
    edge_low, edge_corner = edge[:, :half], edge[:, half : half + 1]
    first_lane = iota((16, half), 1) == 0

    def body(n, _):
        at = pl.multiple_of(n * 16, 16)
        column = column_ref[pl.ds(at, 16), :]
        value = series(row_ref[0:1, :half] + column[:, 0:1]) * row_ref[8:9, :half] * column[:, 1:2]
        row = at + iota((16, half), 0)
        mirror = jnp.sum(
            jnp.where(row == iota((16, half), 1), edge_low, 0.0), axis=1, keepdims=True
        )
        right = jnp.where(first_lane, mirror, value)
        out_ref[pl.ds(at, 16), :half] = value
        out_ref[pl.ds(at, 16), half:] = right
        out_ref[pl.ds(half + at, 16), :half] = jnp.where(row == 0, edge_low, value)
        corner = jnp.where(first_lane, edge_corner, edge_low)
        out_ref[pl.ds(half + at, 16), half:] = jnp.where(row == 0, corner, right)
        return 0

    lax.fori_loop(0, half // 16, body, 0)


def filter_tables():
    plane = np.arange(PLANES)[:, None]
    odd = np.arange(1, NZ // 2, 2)
    gaps = np.arange(-(PLANES // 2) + 1, PLANES // 2 + 1)
    window = np.cos(2.0 * np.pi / PLANES * plane * gaps) @ np.cos(
        2.0 * np.pi / NZ * gaps[:, None] * odd
    )
    even = 2 * np.minimum(plane, PLANES - plane)
    wave = np.concatenate([even, np.broadcast_to(odd, (PLANES, odd.size))], axis=1)
    square, factor = axis_factor(wave, NZ)
    count = np.concatenate([np.full((PLANES, 1), float(PLANES)), 2.0 * window], axis=1)
    terms = count * factor / (np.pi * NX * NY * NZ * PLANES)
    return terms.astype(np.float32), square.astype(np.float32)


def filter_call(plane):
    terms, squares = filter_tables()
    square, factor = axis_factor(wave_order(NX), NX)
    row = np.repeat(np.stack([square, factor]), 8, axis=0).astype(np.float32)
    column = np.stack([square, factor], axis=1).astype(np.float32)
    smem = pl.BlockSpec(memory_space=pltpu.SMEM)
    vmem = pl.BlockSpec(memory_space=pltpu.VMEM)
    return pl.pallas_call(
        filter_kernel,
        out_shape=jax.ShapeDtypeStruct((NX, NY), jnp.float32),
        in_specs=[smem, smem, vmem, vmem],
        compiler_params=pltpu.CompilerParams(vmem_limit_bytes=VMEM_BYTES),
        cost_estimate=pl.CostEstimate(flops=20_000_000, bytes_accessed=1 << 20, transcendentals=0),
        name="filter",
    )(
        lax.dynamic_index_in_dim(jnp.asarray(terms), plane, 0, keepdims=False),
        lax.dynamic_index_in_dim(jnp.asarray(squares), plane, 0, keepdims=False),
        row,
        column,
    )


def plane_kernel(
    count_x,
    count_y,
    wire_ref,
    filter_ref,
    square_ref,
    wide_ref,
    out_ref,
    grid_high,
    grid_low,
    result_ref,
):
    stride = count_y * WIRE_ROWS
    pairs = count_y // 2
    lane = iota((count_x, LANES), 1)
    low_half = lane < 64
    tails = [wire_ref[pl.ds(j * WIRE_ROWS + PATCH_ROWS, count_x, stride=stride), :] for j in range(count_y)]
    for m in range(pairs):
        before = tails[(2 * m - 1) % count_y]
        between = tails[2 * m]
        for r in range(PATCH_ROWS):
            one = wire_ref[pl.ds(2 * m * WIRE_ROWS + r, count_x, stride=stride), :]
            two = wire_ref[pl.ds((2 * m + 1) * WIRE_ROWS + r, count_x, stride=stride), :]
            for h in range(2):
                x = 2 * r + h
                if h == 0:
                    value = jnp.where(low_half, one, pltpu.roll(two, 64, 1))
                else:
                    value = jnp.where(low_half, pltpu.roll(one, 64, 1), two)
                first = pltpu.roll(before, (LANES - 3 * x) % LANES, 1) if x else before
                second = pltpu.roll(between, (LANES + 64 - 3 * x) % LANES, 1)
                value = value + jnp.where(lane < 3, first, 0.0)
                value = value + jnp.where((lane >= 64) & (lane < 67), second, 0.0)
                high, low = split(value)
                at = x * count_x
                grid_high[at : at + count_x, m * LANES : (m + 1) * LANES] = high
                grid_low[at : at + count_x, m * LANES : (m + 1) * LANES] = low

    rows = 2 * PATCH_ROWS * count_x

    def table(n, height):
        return square_ref[n : n + height, :], square_ref[n + height : n + 2 * height, :]

    step = split(dot3((grid_high[...], grid_low[...]), table(0, NY)))
    spectrum = dot3((wide_ref[:NX, :], wide_ref[NX:, :]), step) * filter_ref[...]
    mean = spectrum[0:1, 0:1]
    first = (iota((8, NY), 0) == 0) & (iota((8, NY), 1) == 0)
    spectrum = jnp.concatenate([jnp.where(first, 0.0, spectrum[:8]), spectrum[8:]], axis=0)
    step = split(dot3(table(4 * NY, rows), split(spectrum)))
    result_ref[...] = dot3(step, table(2 * NY, NY))

    for j in range(count_y):
        m = j // 2
        for r in range(PATCH_ROWS):
            even = result_ref[2 * r * count_x : (2 * r + 1) * count_x, m * LANES : (m + 1) * LANES]
            odd = result_ref[(2 * r + 1) * count_x : (2 * r + 2) * count_x, m * LANES : (m + 1) * LANES]
            if j % 2 == 0:
                value = jnp.where(low_half, even, pltpu.roll(odd, 64, 1))
            else:
                value = jnp.where(low_half, pltpu.roll(even, 64, 1), odd)
            out_ref[pl.ds(j * WIRE_ROWS + r, count_x, stride=stride), :] = value
        after = (j + 1) % count_y
        m = after // 2
        tail = jnp.where(lane == LANES - 1, mean, 0.0)
        for x in range(2 * PATCH_ROWS):
            value = result_ref[x * count_x : (x + 1) * count_x, m * LANES : (m + 1) * LANES]
            shift = (3 * x - 64 * (after % 2)) % LANES
            if shift:
                value = pltpu.roll(value, shift, 1)
            tail = jnp.where((lane >= 3 * x) & (lane < 3 * x + 3), value, tail)
        out_ref[pl.ds(j * WIRE_ROWS + PATCH_ROWS, count_x, stride=stride), :] = tail


def plane_call(wire, table, count_x, count_y):
    along_y = cas(np.arange(NY), wave_order(NY), NY)
    rows = 2 * PATCH_ROWS
    cell = (np.arange(rows)[:, None] + (NX // count_x) * np.arange(count_x)[None, :]).reshape(-1) % NX
    along_x = cas(cell, wave_order(NX), NX)
    square = np.concatenate([*high_low(along_y), *high_low(along_y.T), *high_low(along_x)], axis=0)
    wide = np.concatenate(high_low(along_x.T), axis=0)
    return pl.pallas_call(
        functools.partial(plane_kernel, count_x, count_y),
        out_shape=jax.ShapeDtypeStruct((PLANES * WIRE_ROWS, LANES), jnp.float32),
        scratch_shapes=[
            pltpu.VMEM((rows * count_x, NY), jnp.bfloat16),
            pltpu.VMEM((rows * count_x, NY), jnp.bfloat16),
            pltpu.VMEM((rows * count_x, NY), jnp.float32),
        ],
        compiler_params=pltpu.CompilerParams(vmem_limit_bytes=VMEM_BYTES),
        name="plane",
    )(wire, table, square, wide)


def force_kernel(
    wire_ref, place_ref, short_ref, charge_ref, basis_ref, energy_ref, force_ref, rows_ref
):
    for c in range(3):
        for bz in range(4):
            rows_ref[c, 4 * bz : 4 * bz + 4, :] = place_ref[c, bz, 1:5, :]
    pos_x, pos_y, pos_z = [row_vector(rows_ref[c]) for c in range(3)]
    planes = jnp.concatenate(
        [wire_ref[pl.ds(r, PLANES, stride=WIRE_ROWS), :] for r in range(WIRE_ROWS)], axis=1
    )
    basis = basis_ref[...]
    layers = dot3(split(basis), split(planes))
    mean = lax.dot_general(
        basis,
        planes[:, PATCH_ROWS * LANES :],
        NN,
        precision=lax.Precision.HIGHEST,
        preferred_element_type=jnp.float32,
    )[:, LANES - 1 :]
    high, low = split(layers)
    high, low = high.astype(jnp.float32), low.astype(jnp.float32)
    rest = jnp.zeros((LANES - 3 * ZPAD, layers.shape[1]), jnp.float32)
    columns = jnp.concatenate([high, high, low, rest], axis=0).T.astype(jnp.bfloat16)

    per = 4 * LANES
    for bx in range(4):
        cut = slice(bx * per, (bx + 1) * per)
        ux, uy = 8.0 * pos_x[:, cut], pos_y[:, cut]
        weight_z, slope_z = spline_both(z_distance(pos_z[:, cut]))
        z_both = jnp.concatenate([weight_z, slope_z], axis=1)
        z_high, z_low = split(z_both)
        z_high, z_low = z_high.astype(jnp.float32), z_low.astype(jnp.float32)
        z_rest = jnp.zeros((LANES - 3 * ZPAD, 2 * per), jnp.float32)
        z_table = jnp.concatenate([z_high, z_low, z_high, z_rest], axis=0).astype(jnp.bfloat16)
        weight_y, slope_y = spline_both(y_distance(uy, (64, per), iota((64, per), 0)))
        weight_x, slope_x = spline_both((iota((16, per), 0) - 1).astype(jnp.float32) - ux)
        def fold(value):
            out = value[0:8]
            for n in range(1, value.shape[0] // 8):
                out = out + value[8 * n : 8 * n + 8]
            return out

        zero = jnp.zeros((8, per), jnp.float32)
        total = [fold(weight_z * mean), zero, zero, fold(slope_z * mean)]
        for pair in range(6):
            r = 4 * bx + pair
            field = dot(columns[r * LANES : (r + 1) * LANES, :], z_table)
            for h in range(2):
                x = 2 * pair + h
                here = field[64 * h : 64 * h + 64, :per]
                slope = field[64 * h : 64 * h + 64, per:]
                plain = fold(here * weight_y)
                along_y = fold(here * slope_y)
                along_z = fold(slope * weight_y)
                wx, sx = weight_x[x : x + 1, :], slope_x[x : x + 1, :]
                total[0] = total[0] + plain * wx
                total[1] = total[1] + plain * sx
                total[2] = total[2] + along_y * wx
                total[3] = total[3] + along_z * wx
        field = dot(columns[PATCH_ROWS * LANES :, :], z_table)
        here, slope = field[:, :per], field[:, per:]
        place = iota((LANES, per), 0)
        tail_x, tail_sx = spline_both((place // 3 - 1 - 8 * bx).astype(jnp.float32) - ux)
        tail_y, tail_sy = spline_both(y_distance(uy, (LANES, per), 64 + place % 3))
        here_y = here * tail_y
        total[0] = total[0] + fold(here_y * tail_x)
        total[1] = total[1] + fold(here_y * tail_sx)
        total[2] = total[2] + fold(here * tail_sy * tail_x)
        total[3] = total[3] + fold(slope * tail_y * tail_x)
        sums = [jnp.sum(t, axis=0, keepdims=True) for t in total]
        for bz in range(4):
            at = slice(bz * LANES, (bz + 1) * LANES)
            charge = charge_ref[bz, bx : bx + 1, :]
            energy_ref[bz, bx : bx + 1, :] = short_ref[bz, bx : bx + 1, :] + 0.5 * charge * sums[0][:, at]
            for c in range(3):
                force_ref[c, bz, bx : bx + 1, :] = -charge * sums[1 + c][:, at]


def force_call(wire, place, short, charge):
    basis = np.zeros((ZPAD, PLANES))
    basis[:ZROWS] = cas(np.arange(ZROWS), np.arange(PLANES), PLANES)
    return pl.pallas_call(
        force_kernel,
        out_shape=(
            jax.ShapeDtypeStruct((4, 4, LANES), jnp.float32),
            jax.ShapeDtypeStruct((3, 4, 4, LANES), jnp.float32),
        ),
        scratch_shapes=[pltpu.VMEM((3, 16, LANES), jnp.float32)],
        compiler_params=pltpu.CompilerParams(vmem_limit_bytes=VMEM_BYTES),
        name="force",
    )(wire, place, short, charge, basis.astype(np.float32))


def ring(size):
    up = [(i, (i + 1) % size) for i in range(size)]
    return up, [(j, i) for i, j in up]


def exchange(wire):
    moved = lax.all_to_all(
        wire.reshape(PLANES, 1, WIRE_ROWS * LANES), ("gx", "gy"), split_axis=0, concat_axis=0, tiled=True
    )
    return moved.reshape(PLANES * WIRE_ROWS, LANES)


def shards(atom_cells, atom_frac, species, *weights):
    count_x, count_y = lax.axis_size("gx"), lax.axis_size("gy")
    assert count_x * count_y == PLANES and atom_cells.shape[1:] == (4, 4, LANES)
    place = ((atom_cells & (BLOCK - 1)).astype(jnp.float32) + atom_frac) * (1.0 / BLOCK)
    own = jnp.concatenate([place, species.astype(jnp.float32)[None]], axis=0)
    up, down = ring(count_x)
    before = lax.ppermute(own[:, :, 3:4, :], "gx", up)
    after = lax.ppermute(own[:, :, 0:1, :], "gx", down)
    ext = jnp.concatenate([before, own, after, after, after], axis=2)
    up, down = ring(count_y)
    left = lax.ppermute(ext, "gy", up)
    right = lax.ppermute(ext, "gy", down)
    table = filter_call(lax.axis_index(("gx", "gy")))
    packed = pack_weights(*weights)
    ext, left, right, packed, table = lax.optimization_barrier((ext, left, right, packed, table))
    short, charge, wire = atoms_call(ext, left, right, packed)
    wire = exchange(wire)
    wire = plane_call(wire, table, count_x, count_y)
    wire = exchange(wire)
    energy, force = force_call(wire, ext, short, charge)
    return energy, force, charge


def solution(mesh):
    atoms = P(None, "gx", "gy")
    vectors = P(None, None, "gx", "gy")
    return jax.shard_map(
        shards,
        mesh=mesh,
        in_specs=(vectors, vectors, atoms, P(), P(), P(), P(), P(), P()),
        out_specs=(atoms, vectors, atoms),
        check_vma=False,
    )
```

time: 681 us -> 110 us (0.16); the launches traced: 669 us -> 110 us
  matrix products: 214 us -> 0 us
  local copies, waits for them, and re-layouts: 201 us -> 4.87 us
  waiting for transfers between devices: 105 us -> 0.01 us
  other arithmetic: 101 us -> 3.04 us
  blocking collectives: 0 us -> 56.9 us
  starting transfers between devices: 44.4 us -> 8.9 us
  Pallas kernels: 0 us -> 35.1 us
    dot_general x29 -> x0, matrix products: 214 us -> none  [the longest x4 35.1 us: rotate(): jnp.einsum(einsum_form, imag_part, sine_table, precision=highest)]
    all_to_all x2 -> x0, waiting for transfers between devices: 98.9 us -> none  [the longest x1 50.8 us: shards(): lax.all_to_all(outgoing.reshape(count_x * count_y, 2, size_x, size_y, pla...]
    all_to_all x0 -> x2, blocking collectives: none -> 56.9 us  [exchange(): lax.all_to_all(wire.reshape(PLANES, 1, WIRE_ROWS * LANES), ('gx', 'gy'),...]
    unnamed x96 -> x17, local copies, waits for them, and re-layouts: 49.6 us -> 3.33 us
    slice x24 -> x0, local copies, waits for them, and re-layouts: 37.1 us -> none  [the longest x3 18.4 us: shards(): real_part, imag_part = transform(slab_data[0], slab_data[1], -1.0)]
    pallas_call x0 -> x4, Pallas kernels: none -> 35.1 us  [the longest x1 18.5 us: atoms_call(): pl.pallas_call(atoms_kernel, out_shape=(jax.ShapeDtypeStruct((4, 4, LANES...]
    reshape x12 -> x0, local copies, waits for them, and re-layouts: 35.1 us -> none  [the longest x4 17.7 us: cut_regions(): shifted_axes[..., first_index:first_index + BLOCK * block_count]]
    reduce_sum x4 -> x0, other arithmetic: 29.2 us -> none  [pair_terms(): jnp.sum(masked[species_index] * chebyshev, axis=-1) / SLOTS]
  transfers between devices with their start and end apart: 14 -> 4, of which waited for: 5 -> 0; matrix products, arithmetic and copies ran while one was open for 4% -> 4% of each run, Pallas kernels for 0% -> 5%
where the time goes in v1:
time: 110 us
  blocking collectives  56.9 us (52%)
  Pallas kernels  35.1 us (32%)
  starting transfers between devices  8.9 us (8%)
  local copies, waits for them, and re-layouts  4.87 us (4%)
  other arithmetic  3.04 us (3%)
    all_to_all x2, blocking collectives, exchange(): lax.all_to_all(wire.reshape(PLANES, 1, WIRE_ROWS * LANES), ('gx', 'gy'),...  56.9 us
    pallas_call x1, Pallas kernels, atoms_call(): pl.pallas_call(atoms_kernel, out_shape=(jax.ShapeDtypeStruct((4, 4, LANES...  18.5 us
    pallas_call x1, Pallas kernels, plane_call(): pl.pallas_call(functools.partial(plane_kernel, count_x, count_y), out_sha...  5.86 us
    pallas_call x1, Pallas kernels, force_call(): pl.pallas_call(force_kernel, out_shape=(jax.ShapeDtypeStruct((4, 4, LANES...  5.83 us
    pallas_call x1, Pallas kernels, filter_call(): pl.pallas_call(filter_kernel, out_shape=jax.ShapeDtypeStruct((NX, NY), jn...  5.01 us
    ppermute x1, starting transfers between devices, shards(): right = lax.ppermute(ext, 'gy', down)  4.62 us
    unnamed x17, local copies, waits for them, and re-layouts  3.33 us
    ppermute x1, starting transfers between devices, shards(): before = lax.ppermute(own[:, :, 3:4, :], 'gx', up)  2.79 us
  transfers between devices with their start and end apart: 4, of which 0 were waited for; matrix products, arithmetic and copies ran while one was open for 4% of the time, Pallas kernels for 5%

profile of v1, /device:TPU:1, one launch (start us, length us, event | category | flops | bytes accessed | tf_op | source)
XLA Modules:
  0.0 109.7 jit_solution(3912481457616528476)
XLA Ops:
  0.6 0.0 copy-start.3
  0.6 0.7 convert_bitcast_fusion
  1.4 0.8 add_multiply_fusion
  2.2 1.5 %collective-permute-start.1 = (f32[4,4,1,128]{3,2,1,0:T(1,128)S(1)}, f32[4,4,1,128]{3,2,1,0:T(1,128)S(1)}, u32[]{:S(2)}, u32[]{:S(2)}) collective-permute-start(f32[4,4,1,128]{3,2,1,0:T(1,128)S(1)} %get-tuple-element.23), channel_id=1, source_target_pairs={{8,0},{16,8},{24,16},{32,24},{40,32},{48,40},{56,48},{64,56},{72,6... | collective-permute-start | bytes 24584 | tf_op jit(solution)/shard_map/ppermute | solution.py:586
  3.7 2.8 %collective-permute-start = (f32[4,4,1,128]{3,2,1,0:T(1,128)S(1)}, f32[4,4,1,128]{3,2,1,0:T(1,128)S(1)}, u32[]{:S(2)}, u32[]{:S(2)}) collective-permute-start(f32[4,4,1,128]{3,2,1,0:T(1,128)S(1)} %get-tuple-element.24), channel_id=1, source_target_pairs={{0,8},{8,16},{16,24},{24,32},{32,40},{40,48},{48,56},{56,64},{64,7... | collective-permute-start | bytes 24584 | tf_op jit(solution)/shard_map/ppermute | solution.py:585
  6.5 0.7 pad_bitcast_fusion
  7.1 0.7 copy.31
  7.8 0.7 pad_maximum_fusion.1
  8.5 0.1 copy.32
  8.6 0.8 copy.30
  9.4 0.8 fusion.2
  10.3 0.0 copy-start.1
  10.3 0.1 copy.27
  10.4 0.0 collective-permute-done.1
  10.4 0.0 collective-permute-done
  10.4 0.1 concatenate.10.ext_ref.place_ref
  10.5 4.6 %collective-permute-start.3 = (f32[4,4,8,128]{3,2,1,0:T(8,128)S(1)}, f32[4,4,8,128]{3,2,1,0:T(8,128)S(1)}, u32[]{:S(2)}, u32[]{:S(2)}) collective-permute-start(f32[4,4,8,128]{3,2,1,0:T(8,128)S(1)} %concatenate.10.ext_ref.place_ref), channel_id=1, source_target_pairs={{1,0},{2,1},{3,2},{4,3},{5,4},{6,5},{7,6},{0,7},{9,8},{10,9},{11,1... | collective-permute-start | bytes 196616 | tf_op jit(solution)/shard_map/ppermute | solution.py:590
  15.1 0.0 collective-permute-start.2
  15.1 0.7 dynamic-slice_bitcast_fusion
  15.8 0.0 copy-start.2
  15.8 0.9 copy-done.2
  16.7 0.0 copy-start.4
  16.8 0.8 copy-done.4
  17.5 0.0 copy-start
  17.5 5.0 %filter.1.filter_ref = f32[512,512]{1,0:T(8,128)S(1)} custom-call(f32[65]{0:T(128)S(1)} %get-tuple-element.26.terms_ref, f32[65]{0:T(128)S(1)} %get-tuple-element.25.squares_ref, f32[16,512]{1,0:T(8,128)S(1)} %copy-done.4, f32[512,2]{1,0:T(8,128)S(1)} %copy-done.2), custom_call_target="tpu_custom_call" | custom-call | flops 20000000 | bytes 1048576 | tf_op jit(solution)/shard_map/filter/pallas_call | solution.py:366
  22.5 0.0 collective-permute-done.3.right_ref
  22.5 0.0 collective-permute-done.2.left_ref
  22.5 0.0 copy-done.3
  22.6 18.5 %atoms.1 = (f32[4,4,128]{2,1,0:T(4,128)S(1)}, f32[4,4,128]{2,1,0:T(4,128)}, f32[2432,128]{1,0:T(8,128)S(1)}) custom-call(f32[4,4,8,128]{3,2,1,0:T(8,128)S(1)} %concatenate.10.ext_ref.place_ref, f32[4,4,8,128]{3,2,1,0:T(8,128)S(1)} %collective-permute-done.2.left_ref, f32[4,4,8,128]{3,2,1,0:T(8,128)S(1)} %collective-permute-done.3.right_ref, ...), custom_call_target="tpu_custom_call" | custom-call | tf_op jit(solution)/shard_map/atoms/pallas_call | solution.py:279
  41.0 31.8 %all_to_all.10 = f32[128,1,2432]{2,1,0:T(1,128)S(1)} all-to-all(f32[128,1,2432]{2,1,0:T(1,128)S(1)} %bitcast.18), channel_id=1, replica_groups=mesh['gx'=16,'gy'=8] {'gx','gy'}, dimensions={0} | all-to-all | bytes 2490368 | tf_op jit(solution)/shard_map/all_to_all | solution.py:573
  72.9 0.0 copy-done.1
  72.9 0.0 copy-done
  72.9 5.9 %plane.1 = f32[2432,128]{1,0:T(8,128)S(1)} custom-call(f32[2432,128]{1,0:T(8,128)S(1)} %bitcast.15, f32[512,512]{1,0:T(8,128)S(1)} %filter.1.filter_ref, bf16[3200,512]{1,0:T(8,128)(2,1)S(1)} %copy-done, bf16[1024,576]{1,0:T(8,128)(2,1)S(1)} %copy-done.1), custom_call_target="tpu_custom_call" | custom-call | tf_op jit(solution)/shard_map/plane/pallas_call | solution.py:461
  78.7 0.0 copy-start.5
  78.7 0.0 copy-start.6
  78.8 25.1 %all_to_all.11 = f32[128,1,2432]{2,1,0:T(1,128)S(1)} all-to-all(f32[128,1,2432]{2,1,0:T(1,128)S(1)} %bitcast.16), channel_id=1, replica_groups=mesh['gx'=16,'gy'=8] {'gx','gy'}, dimensions={0} | all-to-all | bytes 2490368 | tf_op jit(solution)/shard_map/all_to_all | solution.py:573
  103.8 0.0 copy-done.5
  103.8 0.0 copy-done.6
  103.8 5.8 %force.1 = (f32[4,4,128]{2,1,0:T(4,128)}, f32[3,4,4,128]{3,2,1,0:T(4,128)}) custom-call(f32[2432,128]{1,0:T(8,128)S(1)} %bitcast.17, f32[4,4,8,128]{3,2,1,0:T(8,128)S(1)} %concatenate.10.ext_ref.place_ref, f32[4,4,128]{2,1,0:T(4,128)S(1)} %get-tuple-element.19.short_ref, f32[4,4,128]{2,1,0:T(4,128)S(1)} %copy-done.6, f32[40,128]{1,0:T(8,128)S(1)} %copy-done.5), custom_call_target="tpu_custom_call" | custom-call | tf_op jit(solution)/shard_map/force/pallas_call | solution.py:555
  (2 shorter events, 0.0 us)
Async XLA Ops:
  0.6 21.9 %copy-start.3 = (f32[128,40]{1,0:T(8,128)S(1)}, f32[128,40]{1,0:T(8,128)}, u32[]{:S(2)}) copy-start(f32[128,40]{1,0:T(8,128)} %constant.46.clone.basis_ref) | copy-start | bytes 61444
  2.2 8.2 %collective-permute-start.1 = (f32[4,4,1,128]{3,2,1,0:T(1,128)S(1)}, f32[4,4,1,128]{3,2,1,0:T(1,128)S(1)}, u32[]{:S(2)}, u32[]{:S(2)}) collective-permute-start(f32[4,4,1,128]{3,2,1,0:T(1,128)S(1)} %get-tuple-element.23), channel_id=1, source_target_pairs={{8,0},{16,8},{24,16},{32,24},{40,32},{48,40},{56,48},{64,56},{72,6... | collective-permute-start | bytes 24584 | tf_op jit(solution)/shard_map/ppermute | solution.py:586
  3.7 6.7 %collective-permute-start = (f32[4,4,1,128]{3,2,1,0:T(1,128)S(1)}, f32[4,4,1,128]{3,2,1,0:T(1,128)S(1)}, u32[]{:S(2)}, u32[]{:S(2)}) collective-permute-start(f32[4,4,1,128]{3,2,1,0:T(1,128)S(1)} %get-tuple-element.24), channel_id=1, source_target_pairs={{0,8},{8,16},{16,24},{24,32},{32,40},{40,48},{48,56},{56,64},{64,7... | collective-permute-start | bytes 24584 | tf_op jit(solution)/shard_map/ppermute | solution.py:585
  10.3 62.6 %copy-start.1 = (bf16[1024,576]{1,0:T(8,128)(2,1)S(1)}, bf16[1024,576]{1,0:T(8,128)(2,1)}, u32[]{:S(2)}) copy-start(bf16[1024,576]{1,0:T(8,128)(2,1)} %constant.48.clone.wide_ref) | copy-start | bytes 3538948
  10.5 12.1 %collective-permute-start.3 = (f32[4,4,8,128]{3,2,1,0:T(8,128)S(1)}, f32[4,4,8,128]{3,2,1,0:T(8,128)S(1)}, u32[]{:S(2)}, u32[]{:S(2)}) collective-permute-start(f32[4,4,8,128]{3,2,1,0:T(8,128)S(1)} %concatenate.10.ext_ref.place_ref), channel_id=1, source_target_pairs={{1,0},{2,1},{3,2},{4,3},{5,4},{6,5},{7,6},{0,7},{9,8},{10,9},{11,1... | collective-permute-start | bytes 196616 | tf_op jit(solution)/shard_map/ppermute | solution.py:590
  15.1 7.5 %collective-permute-start.2 = (f32[4,4,8,128]{3,2,1,0:T(8,128)S(1)}, f32[4,4,8,128]{3,2,1,0:T(8,128)S(1)}, u32[]{:S(2)}, u32[]{:S(2)}) collective-permute-start(f32[4,4,8,128]{3,2,1,0:T(8,128)S(1)} %concatenate.10.ext_ref.place_ref), channel_id=1, source_target_pairs={{0,1},{1,2},{2,3},{3,4},{4,5},{5,6},{6,7},{7,0},{8,9},{9,10},{10,1... | collective-permute-start | bytes 196616 | tf_op jit(solution)/shard_map/ppermute | solution.py:589
  15.8 0.9 copy-start.2
  16.7 0.8 copy-start.4
  17.5 55.4 %copy-start = (bf16[3200,512]{1,0:T(8,128)(2,1)S(1)}, bf16[3200,512]{1,0:T(8,128)(2,1)}, u32[]{:S(2)}) copy-start(bf16[3200,512]{1,0:T(8,128)(2,1)} %constant.47.clone.square_ref) | copy-start | bytes 9830404
  78.7 25.1 %copy-start.5 = (f32[40,128]{1,0:T(8,128)S(1)}, f32[40,128]{1,0:T(8,128)}, u32[]{:S(2)}) copy-start(f32[40,128]{1,0:T(8,128)} %constant.49.clone.basis_ref) | copy-start | bytes 61444
  78.7 25.1 %copy-start.6 = (f32[4,4,128]{2,1,0:T(4,128)S(1)}, f32[4,4,128]{2,1,0:T(4,128)}, u32[]{:S(2)}) copy-start(f32[4,4,128]{2,1,0:T(4,128)} %get-tuple-element.12.charge_ref) | copy-start | bytes 24580

commit v2 on v1

--- a/solution.py
+++ b/solution.py
@@ -28,7 +28,7 @@
 NT = (((1,), (1,)), ((), ()))
 NN = (((1,), (0,)), ((), ()))
 TN = (((0,), (0,)), ((), ()))
-VMEM_BYTES = 40 * 1024 * 1024
+VMEM_BYTES = 24 * 1024 * 1024
 
 
 def high_low(table):
@@ -87,6 +87,19 @@
     return weight, jnp.where(distance > 0.0, slope, -slope)
 
 
+def product_scale(k):
+    return float(np.prod([f for n, f in enumerate((-2.0, 8.0, 128.0, 32768.0)) if k >> n & 1]))
+
+
+def chebyshev_of_products(products):
+    out = list(products)
+    for top in (2, 4, 8):
+        for first in range(0, RADIAL, 2 * top):
+            for r in range(1, top):
+                out[first + top + r] = 2.0 * out[first + top + r] - out[first + top - r]
+    return out
+
+
 def iota(shape, dim):
     return lax.broadcasted_iota(jnp.int32, shape, dim)
 
@@ -95,6 +108,30 @@
     return jnp.concatenate(
         [rows[bz * 4 + bx : bz * 4 + bx + 1, :] for bx in range(4) for bz in range(4)], axis=1
     )
+
+
+def last_blocks(value):
+    rows = value.shape[0]
+    lane = iota((rows, LANES), 1)
+    out = []
+    for first in range(0, 16, 8):
+        block = jnp.zeros((rows, LANES), value.dtype)
+        for n in range(8):
+            piece = value[:, (first + n) * LANES : (first + n + 1) * LANES]
+            if n < 7:
+                piece = pltpu.roll(piece, SLOTS * (n + 1), 1)
+            block = jnp.where((lane >= SLOTS * n) & (lane < SLOTS * (n + 1)), piece, block)
+        out.append(block)
+    return jnp.concatenate(out, axis=1)
+
+
+def tail_distances(pos_x, pos_y):
+    shape = (LANES, pos_x.shape[1])
+    place = iota(shape, 0)
+    block = iota(shape, 1) // (ZBLOCKS * SLOTS)
+    along_x = (place // 3 - 1 - 8 * block).astype(jnp.float32) - 8.0 * pos_x
+    along_y = (64 - 1 - 8 * 7 + place % 3).astype(jnp.float32) - 8.0 * pos_y
+    return along_x, along_y
 
 
 def z_distance(pos_z):
@@ -108,16 +145,88 @@
     return (cell - 1 - 8 * block).astype(jnp.float32) - 8.0 * pos_y
 
 
+def place_blocks(near_ref, n, blocks, dx, dy):
+    far = jnp.full((4, LANES), 100.0, jnp.float32)
+    for c in range(4):
+        offset = float((dx - 1, dy - 1, 0, 0)[c])
+        for bz in range(ZBLOCKS):
+            row = (c * ZBLOCKS + bz) * 8 + dx
+            near_ref[n, c, 4 + 4 * bz : 8 + 4 * bz, :] = blocks[row : row + 4, :] + offset
+        near_ref[n, c, 0:4, :] = far
+        near_ref[n, c, 20:24, :] = far
+
+
+def pair_sums(near_ref, count, center, mine, half, sums):
+    lane8 = iota((8, LANES), 1)
+
+    def body(n, sums):
+        sums = list(sums)
+        for dz in range(3):
+            near = [near_ref[n, c, 4 * dz + 8 * half : 4 * dz + 8 * half + 8, :] for c in range(4)]
+            mine_z = mine[2] - float(dz - 1)
+            for turn in range(SLOTS):
+                if turn == 0:
+                    got = near
+                else:
+                    index = (lane8 & (LANES - SLOTS)) | ((lane8 + turn) & (SLOTS - 1))
+                    got = [jnp.take_along_axis(v, index, axis=1) for v in near]
+                gx = got[0] - mine[0]
+                gy = got[1] - mine[1]
+                gz = got[2] - mine_z
+                kind = got[3]
+                remain = jnp.maximum(1.0 - (gx * gx + gy * gy + gz * gz), 0.0)
+                if turn == 0 and dz == 1 and center is not None:
+                    remain = remain * jnp.where(n == center, 0.0, 1.0).astype(jnp.float32)
+                half_t = remain - 0.5
+                two = half_t * half_t - 1.0 / 8.0
+                four = two * two - 1.0 / 128.0
+                eight = four * four - 1.0 / 32768.0
+                terms = [remain * remain]
+                for factor in (half_t, two, four, eight):
+                    terms = terms + [term * factor for term in terms]
+                for k in range(RADIAL):
+                    sums[k] = sums[k] + terms[k]
+                    sums[RADIAL + k] = sums[RADIAL + k] + terms[k] * kind
+        return tuple(sums)
+
+    return lax.fori_loop(0, count, body, tuple(sums))
+
+
+def first_pairs_kernel(ext_ref, sums_ref, near_ref):
+    own = ext_ref[...].reshape(LANES, LANES)
+    for dx in range(3):
+        place_blocks(near_ref, dx, own, dx, 1)
+    zero = jnp.zeros((8, LANES), jnp.float32)
+    for half in range(2):
+        at = slice(8 * half, 8 * half + 8)
+        mine = [near_ref[1, c, 4 + 8 * half : 12 + 8 * half, :] for c in range(3)]
+        sums = pair_sums(near_ref, 3, 1, mine, half, (zero,) * (2 * RADIAL))
+        for k in range(2 * RADIAL):
+            sums_ref[k, at, :] = sums[k]
+
+
+def first_pairs_call(ext):
+    return pl.pallas_call(
+        first_pairs_kernel,
+        out_shape=jax.ShapeDtypeStruct((SPECIES * RADIAL, 16, LANES), jnp.float32),
+        scratch_shapes=[pltpu.VMEM((3, 4, 24, LANES), jnp.float32)],
+        compiler_params=pltpu.CompilerParams(vmem_limit_bytes=VMEM_BYTES),
+        cost_estimate=pl.CostEstimate(flops=24_000_000, bytes_accessed=1 << 19, transcendentals=0),
+        name="first_pairs",
+    )(ext)
+
+
 def atoms_kernel(
     ext_ref,
     left_ref,
     right_ref,
+    begun_ref,
     packed_ref,
-    basis_ref,
     short_ref,
     charge_ref,
     wire_ref,
     near_ref,
+    own_ref,
     feature_ref,
     weight_ref,
     bias_ref,
@@ -126,73 +235,31 @@
     own = ext_ref[...].reshape(LANES, LANES)
     left = left_ref[...].reshape(LANES, LANES)
     right = right_ref[...].reshape(LANES, LANES)
-    shifted = [
-        jnp.where(lane < SLOTS, pltpu.roll(left, SLOTS, 1), pltpu.roll(own, SLOTS, 1)),
-        own,
-        jnp.where(
-            lane >= LANES - SLOTS,
-            pltpu.roll(right, LANES - SLOTS, 1),
-            pltpu.roll(own, LANES - SLOTS, 1),
-        ),
-    ]
-    far = jnp.full((4, LANES), 100.0, jnp.float32)
+    before = jnp.where(lane < SLOTS, pltpu.roll(left, SLOTS, 1), pltpu.roll(own, SLOTS, 1))
+    after = jnp.where(
+        lane >= LANES - SLOTS,
+        pltpu.roll(right, LANES - SLOTS, 1),
+        pltpu.roll(own, LANES - SLOTS, 1),
+    )
     for dx in range(3):
-        for dy in range(3):
-            n = dx * 3 + dy
-            for c in range(4):
-                offset = float((dx - 1, dy - 1, 0, 0)[c])
-                for bz in range(ZBLOCKS):
-                    row = (c * ZBLOCKS + bz) * 8 + dx
-                    near_ref[n, c, 4 + 4 * bz : 8 + 4 * bz, :] = shifted[dy][row : row + 4, :] + offset
-                near_ref[n, c, 0:4, :] = far
-                near_ref[n, c, 20:24, :] = far
-
-    lane8 = iota((8, LANES), 1)
+        place_blocks(near_ref, 2 * dx, before, dx, 0)
+        place_blocks(near_ref, 2 * dx + 1, after, dx, 2)
+    for c in range(4):
+        for bz in range(ZBLOCKS):
+            row = (c * ZBLOCKS + bz) * 8 + 1
+            own_ref[c, 4 * bz : 4 * bz + 4, :] = own[row : row + 4, :]
+
     for half in range(2):
-        mine = [near_ref[4, c, 4 + 8 * half : 12 + 8 * half, :] for c in range(3)]
-
-        def body(n, sums):
-            sums = list(sums)
-            keep = jnp.where(n == 4, 0.0, 1.0).astype(jnp.float32)
-            for dz in range(3):
-                near = [
-                    near_ref[n, c, 4 * dz + 8 * half : 4 * dz + 8 * half + 8, :] for c in range(4)
-                ]
-                mine_z = mine[2] - float(dz - 1)
-                for turn in range(SLOTS):
-                    if turn == 0:
-                        got = near
-                    else:
-                        index = (lane8 & (LANES - SLOTS)) | ((lane8 + turn) & (SLOTS - 1))
-                        got = [jnp.take_along_axis(v, index, axis=1) for v in near]
-                    gx = got[0] - mine[0]
-                    gy = got[1] - mine[1]
-                    gz = got[2] - mine_z
-                    kind = got[3]
-                    remain = jnp.maximum(1.0 - (gx * gx + gy * gy + gz * gz), 0.0)
-                    if turn == 0 and dz == 1:
-                        remain = remain * keep
-                    twice = 2.0 - 4.0 * remain
-                    previous = remain * remain
-                    current = 0.5 * twice * previous
-                    for k in range(RADIAL):
-                        if k == 0:
-                            term = previous
-                        elif k == 1:
-                            term = current
-                        else:
-                            term = twice * current - previous
-                            previous, current = current, term
-                        sums[k] = sums[k] + term
-                        sums[RADIAL + k] = sums[RADIAL + k] + term * kind
-            return tuple(sums)
-
-        zero = jnp.zeros((8, LANES), jnp.float32)
-        sums = lax.fori_loop(0, 9, body, (zero,) * (2 * RADIAL))
+        at = slice(8 * half, 8 * half + 8)
+        mine = [own_ref[c, at, :] for c in range(3)]
+        begun = [begun_ref[k, at, :] for k in range(2 * RADIAL)]
+        sums = pair_sums(near_ref, 6, None, mine, half, begun)
+        scales = [product_scale(k) / SLOTS for k in range(RADIAL)]
+        both = chebyshev_of_products([sums[k] * scales[k] for k in range(RADIAL)])
+        ones = chebyshev_of_products([sums[RADIAL + k] * scales[k] for k in range(RADIAL)])
         for k in range(RADIAL):
-            one = sums[RADIAL + k] * (1.0 / SLOTS)
-            feature_ref[k, 8 * half : 8 * half + 8, :] = sums[k] * (1.0 / SLOTS) - one
-            feature_ref[RADIAL + k, 8 * half : 8 * half + 8, :] = one
+            feature_ref[k, 8 * half : 8 * half + 8, :] = both[k] - ones[k]
+            feature_ref[RADIAL + k, 8 * half : 8 * half + 8, :] = ones[k]
 
     features = jnp.concatenate(
         [feature_ref[:, bz * 4 + bx, :] for bx in range(4) for bz in range(4)], axis=1
@@ -201,13 +268,12 @@
     bias_ref[...] = jnp.zeros(bias_ref.shape, jnp.float32)
     for s in range(SPECIES):
         at = s * 16
-        row = s * 72
-        weight_ref[0, :, at : at + NEURONS] = packed_ref[row : row + 32, :NEURONS]
-        weight_ref[1, at : at + NEURONS, at : at + NEURONS] = packed_ref[row + 32 : row + 47, :NEURONS]
-        weight_ref[2, at : at + NEURONS, 2 * s : 2 * s + 2] = packed_ref[row + 48 : row + 63, :2]
-        bias_ref[0:1, at : at + NEURONS] = packed_ref[row + 64 : row + 65, :NEURONS]
-        bias_ref[1:2, at : at + NEURONS] = packed_ref[row + 65 : row + 66, :NEURONS]
-        bias_ref[2:3, 2 * s : 2 * s + 2] = packed_ref[row + 66 : row + 67, :2]
+        weight_ref[0, at : at + NEURONS, : SPECIES * RADIAL] = packed_ref[:15, s, : SPECIES * RADIAL]
+        weight_ref[1, at : at + NEURONS, at : at + NEURONS] = packed_ref[15:30, s, :NEURONS]
+        weight_ref[2, 2 * s : 2 * s + 2, at : at + NEURONS] = packed_ref[30 + s, :, :NEURONS]
+        bias_ref[0:1, at : at + NEURONS] = packed_ref[32, s : s + 1, :NEURONS]
+        bias_ref[1:2, at : at + NEURONS] = packed_ref[33, s : s + 1, :NEURONS]
+        bias_ref[2:3, 2 * s : 2 * s + 2] = packed_ref[34, s : s + 1, :2]
     diagonal = iota((LANES, LANES), 0) == iota((LANES, LANES), 1)
 
     def layer(n, x, height):
@@ -215,11 +281,11 @@
             jnp.where(diagonal[:height], bias_ref[n : n + 1, :], 0.0), axis=1, keepdims=True
         )
         full = lax.dot_general(
-            weight_ref[n, :, :height], x, TN, precision=lax.Precision.HIGHEST, preferred_element_type=jnp.float32
+            weight_ref[n, :height, :32], x, TN if n == 1 else NN, precision=lax.Precision.HIGHEST, preferred_element_type=jnp.float32
         )
         return full + bias
 
-    rows = [near_ref[4, c, 4:20, :] for c in range(4)]
+    rows = [own_ref[c] for c in range(4)]
     pos_x, pos_y, pos_z, kinds = [row_vector(r) for r in rows]
     answers = layer(2, jnp.tanh(layer(1, jnp.tanh(layer(0, features, 32)), 32)), 8)
     answer = jnp.where(kinds == 0.0, answers[0:2, :], answers[2:4, :])
@@ -231,50 +297,60 @@
             charge_ref[bz, bx : bx + 1, :] = charge[:, at : at + LANES]
 
     along_z = split(spline_weight(z_distance(pos_z)))
-    waves = dot3(split(basis_ref[...]), along_z) * charge
+    basis = jnp.concatenate([packed_ref[35:, n, :ZPAD] for n in range(2)], axis=0)
+    waves = dot3(split(basis), along_z) * charge
     waves_high, waves_low = split(waves)
 
     per = 4 * LANES
     carry = [None, None]
-    tail = None
     for bx in range(4):
         cut = slice(bx * per, (bx + 1) * per)
         ux, uy = 8.0 * pos_x[:, cut], pos_y[:, cut]
         waves_cut = (waves_high[:, cut], waves_low[:, cut])
         weight_y = spline_weight(y_distance(uy, (64, per), iota((64, per), 0)))
         weight_x = spline_weight((iota((16, per), 0) - 1).astype(jnp.float32) - ux)
-        for pair in range(6):
+        for group in range(3):
             product = jnp.concatenate(
-                [weight_y * weight_x[2 * pair + h : 2 * pair + h + 1, :] for h in range(2)], axis=0
+                [weight_y * weight_x[4 * group + h : 4 * group + h + 1, :] for h in range(4)], axis=0
             )
-            plane = dot3(waves_cut, split(product), NT)
-            if pair < 2 and bx > 0:
-                plane = plane + carry[pair]
-            if pair >= 4 and bx < 3:
-                carry[pair - 4] = plane
-            else:
-                wire_ref[pl.ds(4 * bx + pair, PLANES, stride=WIRE_ROWS), :] = plane
-        place = iota((LANES, per), 0)
-        tail_x = spline_weight((place // 3 - 1 - 8 * bx).astype(jnp.float32) - ux)
-        tail_y = spline_weight(y_distance(uy, (LANES, per), 64 + place % 3))
-        more = dot3(waves_cut, split(tail_x * tail_y), NT)
-        tail = more if tail is None else tail + more
+            both = dot3(waves_cut, split(product), NT)
+            for n in range(2):
+                pair = 2 * group + n
+                plane = both[:, n * LANES : (n + 1) * LANES]
+                if pair < 2 and bx > 0:
+                    plane = plane + carry[pair]
+                if pair >= 4 and bx < 3:
+                    carry[pair - 4] = plane
+                else:
+                    wire_ref[pl.ds(4 * bx + pair, PLANES, stride=WIRE_ROWS), :] = plane
+    tail_x, tail_y = tail_distances(last_blocks(pos_x), last_blocks(pos_y))
+    product = spline_weight(tail_x) * spline_weight(tail_y)
+    tail = dot3(split(last_blocks(waves)), split(product), NT)
     wire_ref[pl.ds(PATCH_ROWS, PLANES, stride=WIRE_ROWS), :] = tail
 
 
 def pack_weights(w_first, b_first, w_second, b_second, w_out, b_out):
-    def wide(part, height):
-        return jnp.pad(part, ((0, 0), (0, height - part.shape[1]), (0, LANES - part.shape[2])))
-
-    biases = jnp.stack([b_first, b_second, jnp.pad(b_out, ((0, 0), (0, NEURONS - 2)))], axis=1)
-    parts = [wide(w_first, 32), wide(w_second, 16), wide(w_out, 16), wide(biases, 8)]
-    return jnp.concatenate(parts, axis=1).reshape(-1, LANES)
-
-
-def atoms_call(ext, left, right, packed):
-    wave = np.arange(PLANES)
-    basis = np.zeros((PLANES, ZPAD))
-    basis[:, :ZROWS] = cas(wave, np.arange(ZROWS), PLANES)
+    parts = [
+        w_first.transpose(2, 0, 1),
+        w_second.transpose(1, 0, 2),
+        w_out.transpose(0, 2, 1),
+        b_first[None],
+        b_second[None],
+        b_out[None],
+    ]
+    basis = np.zeros((2, PLANES // 2, LANES), np.float32)
+    basis[:, :, :ZROWS] = cas(np.arange(PLANES), np.arange(ZROWS), PLANES).reshape(2, PLANES // 2, ZROWS)
+    parts.append(basis.transpose(1, 0, 2))
+    height = sum(part.shape[0] for part in parts)
+    total, first = 0.0, 0
+    for part in parts:
+        after = height - first - part.shape[0]
+        total = total + jnp.pad(part, ((first, after), (0, 0), (0, LANES - part.shape[2])))
+        first += part.shape[0]
+    return total
+
+
+def atoms_call(ext, left, right, begun, packed):
     f32 = jnp.float32
     return pl.pallas_call(
         atoms_kernel,
@@ -284,14 +360,15 @@
             jax.ShapeDtypeStruct((PLANES * WIRE_ROWS, LANES), f32),
         ),
         scratch_shapes=[
-            pltpu.VMEM((9, 4, 24, LANES), f32),
+            pltpu.VMEM((6, 4, 24, LANES), f32),
+            pltpu.VMEM((4, 16, LANES), f32),
             pltpu.VMEM((SPECIES * RADIAL, 16, LANES), f32),
             pltpu.VMEM((3, 32, LANES), f32),
             pltpu.VMEM((8, LANES), f32),
         ],
         compiler_params=pltpu.CompilerParams(vmem_limit_bytes=VMEM_BYTES),
         name="atoms",
-    )(ext, left, right, packed, basis.astype(np.float32))
+    )(ext, left, right, begun, packed)
 
 
 def filter_kernel(terms_ref, squares_ref, row_ref, column_ref, out_ref):
@@ -383,13 +460,50 @@
     count_y,
     wire_ref,
     filter_ref,
-    square_ref,
-    wide_ref,
+    table_ref,
     out_ref,
     grid_high,
     grid_low,
     result_ref,
+    y_high,
+    y_low,
+    yt_high,
+    yt_low,
+    x_high,
+    x_low,
+    xt_high,
+    xt_low,
 ):
+    width = x_high.shape[0]
+
+    def fill(high_ref, low_ref, first, value):
+        high_ref[first : first + 16, :], low_ref[first : first + 16, :] = split(value)
+
+    def part(name, lanes):
+        first, height = TABLE[name]
+        return table_ref[first : first + height, :lanes]
+
+    cosine, sine = part("y cos", NY), part("y sin", NY)
+    for a in range(32):
+        at = slice(a, a + 1)
+        fill(y_high, y_low, 16 * a, cosine[at] * part("y cas", NY) + sine[at] * part("y sac", NY))
+    cosine, sine = part("x cos", NX), part("x sin", NX)
+    plus, minus = part("x cas", NX), part("x sac", NX)
+    for x in range(2 * PATCH_ROWS):
+        at = slice(x, x + 1)
+        fill(x_high, x_low, 16 * x, cosine * plus[at] + sine * minus[at])
+    for name, lanes, high, low in (("yt", NY, yt_high, yt_low), ("xt", width, xt_high, xt_low)):
+        cosine, sine = part(name + " cos", lanes), part(name + " sin", lanes)
+        plus, minus = part(name + " cas", lanes), part(name + " sac", lanes)
+        middle = part(name + " mid", lanes)[0:1]
+        for a in range(16):
+            at = slice(a, a + 1)
+            fill(high, low, 16 * a, cosine[at] * plus + sine[at] * minus)
+            value = cosine[at] * minus - sine[at] * plus
+            if a == 0:
+                value = jnp.where(iota((16, lanes), 0) == 0, middle, value)
+            fill(high, low, 256 + 16 * a, value)
+
     stride = count_y * WIRE_ROWS
     pairs = count_y // 2
     lane = iota((count_x, LANES), 1)
@@ -416,18 +530,13 @@
                 grid_high[at : at + count_x, m * LANES : (m + 1) * LANES] = high
                 grid_low[at : at + count_x, m * LANES : (m + 1) * LANES] = low
 
-    rows = 2 * PATCH_ROWS * count_x
-
-    def table(n, height):
-        return square_ref[n : n + height, :], square_ref[n + height : n + 2 * height, :]
-
-    step = split(dot3((grid_high[...], grid_low[...]), table(0, NY)))
-    spectrum = dot3((wide_ref[:NX, :], wide_ref[NX:, :]), step) * filter_ref[...]
+    step = split(dot3((grid_high[...], grid_low[...]), (y_high[...], y_low[...])))
+    spectrum = dot3((xt_high[...], xt_low[...]), step) * filter_ref[...]
     mean = spectrum[0:1, 0:1]
-    first = (iota((8, NY), 0) == 0) & (iota((8, NY), 1) == 0)
+    first = (iota((8, NX), 0) == 0) & (iota((8, NX), 1) == 0)
     spectrum = jnp.concatenate([jnp.where(first, 0.0, spectrum[:8]), spectrum[8:]], axis=0)
-    step = split(dot3(table(4 * NY, rows), split(spectrum)))
-    result_ref[...] = dot3(step, table(2 * NY, NY))
+    step = split(dot3((x_high[...], x_low[...]), split(spectrum)))
+    result_ref[...] = dot3(step, (yt_high[...], yt_low[...]))
 
     for j in range(count_y):
         m = j // 2
@@ -451,13 +560,51 @@
         out_ref[pl.ds(j * WIRE_ROWS + PATCH_ROWS, count_x, stride=stride), :] = tail
 
 
-def plane_call(wire, table, count_x, count_y):
-    along_y = cas(np.arange(NY), wave_order(NY), NY)
+def table_layout():
+    heights = {"y cos": 32, "y sin": 32, "y cas": 16, "y sac": 16}
+    heights.update({"x cos": 16, "x sin": 16, "x cas": 40, "x sac": 40})
+    for name in ("yt", "xt"):
+        heights.update({name + " cos": 16, name + " sin": 16, name + " cas": 16, name + " sac": 16, name + " mid": 8})
+    layout, first = {}, 0
+    for name, height in heights.items():
+        layout[name] = (first, height)
+        first += height
+    return layout, first
+
+
+TABLE, TABLE_ROWS = table_layout()
+
+
+def plane_tables(count_x):
+    wave, cell = wave_order(NY), np.arange(NY)
+    place = (np.arange(2 * PATCH_ROWS)[:, None] + (NX // count_x) * np.arange(count_x)).reshape(-1)
+    out = np.zeros((TABLE_ROWS, 640), np.float32)
+
+    def put(name, rows, lanes):
+        angle = 2.0 * np.pi / NX * (np.outer(rows, lanes) % NX)
+        cosine, sine = np.cos(angle), np.sin(angle)
+        value = {"cos": cosine, "sin": sine, "cas": cosine + sine, "sac": cosine - sine, "mid": cosine}
+        first = TABLE[name][0]
+        out[first : first + len(rows), : len(lanes)] = value[name[-3:]]
+
+    sixteen = np.arange(16)
+    for kind in ("cos", "sin"):
+        put("y " + kind, 16 * np.arange(32), wave)
+        put("x " + kind, (NX // count_x) * np.arange(count_x), wave)
+        put("yt " + kind, 16 * sixteen, cell)
+        put("xt " + kind, 16 * sixteen, place)
+    for kind in ("cas", "sac"):
+        put("y " + kind, sixteen, wave)
+        put("x " + kind, np.arange(2 * PATCH_ROWS), wave)
+        put("yt " + kind, sixteen, cell)
+        put("xt " + kind, sixteen, place)
+    put("yt mid", np.array([NY // 2]), cell)
+    put("xt mid", np.array([NX // 2]), place)
+    return out
+
+
+def plane_call(wire, table, tables, count_x, count_y):
     rows = 2 * PATCH_ROWS
-    cell = (np.arange(rows)[:, None] + (NX // count_x) * np.arange(count_x)[None, :]).reshape(-1) % NX
-    along_x = cas(cell, wave_order(NX), NX)
-    square = np.concatenate([*high_low(along_y), *high_low(along_y.T), *high_low(along_x)], axis=0)
-    wide = np.concatenate(high_low(along_x.T), axis=0)
     return pl.pallas_call(
         functools.partial(plane_kernel, count_x, count_y),
         out_shape=jax.ShapeDtypeStruct((PLANES * WIRE_ROWS, LANES), jnp.float32),
@@ -465,10 +612,13 @@
             pltpu.VMEM((rows * count_x, NY), jnp.bfloat16),
             pltpu.VMEM((rows * count_x, NY), jnp.bfloat16),
             pltpu.VMEM((rows * count_x, NY), jnp.float32),
+            *[pltpu.VMEM((NY, NY), jnp.bfloat16)] * 4,
+            *[pltpu.VMEM((rows * count_x, NX), jnp.bfloat16)] * 2,
+            *[pltpu.VMEM((NX, rows * count_x), jnp.bfloat16)] * 2,
         ],
         compiler_params=pltpu.CompilerParams(vmem_limit_bytes=VMEM_BYTES),
         name="plane",
-    )(wire, table, square, wide)
+    )(wire, table, tables)
 
 
 def force_kernel(
@@ -495,29 +645,52 @@
     rest = jnp.zeros((LANES - 3 * ZPAD, layers.shape[1]), jnp.float32)
     columns = jnp.concatenate([high, high, low, rest], axis=0).T.astype(jnp.bfloat16)
 
+    def fold(value):
+        out = value[0:8]
+        for n in range(1, value.shape[0] // 8):
+            out = out + value[8 * n : 8 * n + 8]
+        return out
+
+    def z_table(weight, slope):
+        high, low = split(jnp.concatenate([weight, slope], axis=1))
+        high, low = high.astype(jnp.float32), low.astype(jnp.float32)
+        rest = jnp.zeros((LANES - 3 * ZPAD, high.shape[1]), jnp.float32)
+        return jnp.concatenate([high, low, high, rest], axis=0).astype(jnp.bfloat16)
+
+    last_x, last_y, last_z = [last_blocks(v) for v in (pos_x, pos_y, pos_z)]
+    size = last_x.shape[1]
+    layer = (iota((ZPAD, size), 1) // SLOTS) % ZBLOCKS
+    last_distance = (iota((ZPAD, size), 0) - 8 * layer - 1).astype(jnp.float32) - 8.0 * last_z
+    field = dot(columns[PATCH_ROWS * LANES :, :], z_table(*spline_both(last_distance)))
+    here, slope = field[:, :size], field[:, size:]
+    tail_x, tail_y = tail_distances(last_x, last_y)
+    (tail_x, tail_sx), (tail_y, tail_sy) = spline_both(tail_x), spline_both(tail_y)
+    here_y = here * tail_y
+    tails = [
+        jnp.sum(fold(v), axis=0, keepdims=True)
+        for v in (here_y * tail_x, here_y * tail_sx, here * tail_sy * tail_x, slope * tail_y * tail_x)
+    ]
+    last_lanes = iota((1, LANES), 1) >= LANES - SLOTS
+
+    def tail_of(n, bx, bz):
+        at = bx * ZBLOCKS + bz
+        half = tails[n][:, (at // 8) * LANES : (at // 8 + 1) * LANES]
+        shift = (LANES - SLOTS * (at % 8 + 1)) % LANES
+        return jnp.where(last_lanes, pltpu.roll(half, shift, 1) if shift else half, 0.0)
+
     per = 4 * LANES
     for bx in range(4):
         cut = slice(bx * per, (bx + 1) * per)
         ux, uy = 8.0 * pos_x[:, cut], pos_y[:, cut]
         weight_z, slope_z = spline_both(z_distance(pos_z[:, cut]))
-        z_both = jnp.concatenate([weight_z, slope_z], axis=1)
-        z_high, z_low = split(z_both)
-        z_high, z_low = z_high.astype(jnp.float32), z_low.astype(jnp.float32)
-        z_rest = jnp.zeros((LANES - 3 * ZPAD, 2 * per), jnp.float32)
-        z_table = jnp.concatenate([z_high, z_low, z_high, z_rest], axis=0).astype(jnp.bfloat16)
+        table = z_table(weight_z, slope_z)
         weight_y, slope_y = spline_both(y_distance(uy, (64, per), iota((64, per), 0)))
         weight_x, slope_x = spline_both((iota((16, per), 0) - 1).astype(jnp.float32) - ux)
-        def fold(value):
-            out = value[0:8]
-            for n in range(1, value.shape[0] // 8):
-                out = out + value[8 * n : 8 * n + 8]
-            return out
-
         zero = jnp.zeros((8, per), jnp.float32)
         total = [fold(weight_z * mean), zero, zero, fold(slope_z * mean)]
         for pair in range(6):
             r = 4 * bx + pair
-            field = dot(columns[r * LANES : (r + 1) * LANES, :], z_table)
+            field = dot(columns[r * LANES : (r + 1) * LANES, :], table)
             for h in range(2):
                 x = 2 * pair + h
                 here = field[64 * h : 64 * h + 64, :per]
@@ -530,23 +703,14 @@
                 total[1] = total[1] + plain * sx
                 total[2] = total[2] + along_y * wx
                 total[3] = total[3] + along_z * wx
-        field = dot(columns[PATCH_ROWS * LANES :, :], z_table)
-        here, slope = field[:, :per], field[:, per:]
-        place = iota((LANES, per), 0)
-        tail_x, tail_sx = spline_both((place // 3 - 1 - 8 * bx).astype(jnp.float32) - ux)
-        tail_y, tail_sy = spline_both(y_distance(uy, (LANES, per), 64 + place % 3))
-        here_y = here * tail_y
-        total[0] = total[0] + fold(here_y * tail_x)
-        total[1] = total[1] + fold(here_y * tail_sx)
-        total[2] = total[2] + fold(here * tail_sy * tail_x)
-        total[3] = total[3] + fold(slope * tail_y * tail_x)
         sums = [jnp.sum(t, axis=0, keepdims=True) for t in total]
         for bz in range(4):
             at = slice(bz * LANES, (bz + 1) * LANES)
             charge = charge_ref[bz, bx : bx + 1, :]
-            energy_ref[bz, bx : bx + 1, :] = short_ref[bz, bx : bx + 1, :] + 0.5 * charge * sums[0][:, at]
+            found = [sums[n][:, at] + tail_of(n, bx, bz) for n in range(4)]
+            energy_ref[bz, bx : bx + 1, :] = short_ref[bz, bx : bx + 1, :] + 0.5 * charge * found[0]
             for c in range(3):
-                force_ref[c, bz, bx : bx + 1, :] = -charge * sums[1 + c][:, at]
+                force_ref[c, bz, bx : bx + 1, :] = -charge * found[1 + c]
 
 
 def force_call(wire, place, short, charge):
@@ -580,7 +744,9 @@
     count_x, count_y = lax.axis_size("gx"), lax.axis_size("gy")
     assert count_x * count_y == PLANES and atom_cells.shape[1:] == (4, 4, LANES)
     place = ((atom_cells & (BLOCK - 1)).astype(jnp.float32) + atom_frac) * (1.0 / BLOCK)
-    own = jnp.concatenate([place, species.astype(jnp.float32)[None]], axis=0)
+    kinds = species.astype(jnp.float32)[None]
+    own = jnp.pad(place, ((0, 1), (0, 0), (0, 0), (0, 0)))
+    own = jnp.where(lax.broadcasted_iota(jnp.int32, own.shape, 0) == 3, kinds, own)
     up, down = ring(count_x)
     before = lax.ppermute(own[:, :, 3:4, :], "gx", up)
     after = lax.ppermute(own[:, :, 0:1, :], "gx", down)
@@ -588,12 +754,12 @@
     up, down = ring(count_y)
     left = lax.ppermute(ext, "gy", up)
     right = lax.ppermute(ext, "gy", down)
+    tables = plane_tables(count_x)
     table = filter_call(lax.axis_index(("gx", "gy")))
-    packed = pack_weights(*weights)
-    ext, left, right, packed, table = lax.optimization_barrier((ext, left, right, packed, table))
-    short, charge, wire = atoms_call(ext, left, right, packed)
+    begun = first_pairs_call(ext)
+    short, charge, wire = atoms_call(ext, left, right, begun, pack_weights(*weights))
     wire = exchange(wire)
-    wire = plane_call(wire, table, count_x, count_y)
+    wire = plane_call(wire, table, tables, count_x, count_y)
     wire = exchange(wire)
     energy, force = force_call(wire, ext, short, charge)
     return energy, force, charge

time: 110 us -> 101 us (0.918)
  blocking collectives: 56.9 us -> 25.1 us
  waiting for transfers between devices: 0.01 us -> 18.2 us
  starting transfers between devices: 8.9 us -> 19.4 us
  local copies, waits for them, and re-layouts: 4.87 us -> 1.51 us
  Pallas kernels: 35.1 us -> 33.4 us
    all_to_all x2 -> x1, blocking collectives: 56.9 us -> 25.1 us  [exchange(): lax.all_to_all(wire.reshape(PLANES, 1, WIRE_ROWS * LANES), ('gx', 'gy'),...]
    all_to_all x0 -> x1, waiting for transfers between devices: none -> 15.3 us  [exchange(): lax.all_to_all(wire.reshape(PLANES, 1, WIRE_ROWS * LANES), ('gx', 'gy'),...]
    all_to_all x0 -> x1, starting transfers between devices: none -> 11.2 us  [exchange(): lax.all_to_all(wire.reshape(PLANES, 1, WIRE_ROWS * LANES), ('gx', 'gy'),...]
    pallas_call x1, Pallas kernels: 18.5 us -> 13.7 us  [atoms_call(): pl.pallas_call(atoms_kernel, out_shape=(jax.ShapeDtypeStruct((4, 4, LANES...]
    pallas_call x0 -> x1, Pallas kernels: none -> 4.18 us  [first_pairs_call(): pl.pallas_call(first_pairs_kernel, out_shape=jax.ShapeDtypeStruct((SPECIE...]
    unnamed x17 -> x14, local copies, waits for them, and re-layouts: 3.33 us -> 0.63 us
    ppermute x1, waiting for transfers between devices: 0.01 us -> 1.61 us  [shards(): before = lax.ppermute(own[:, :, 3:4, :], 'gx', up)]
    pallas_call x1, Pallas kernels: 5.83 us -> 4.37 us  [force_call(): pl.pallas_call(force_kernel, out_shape=(jax.ShapeDtypeStruct((4, 4, LANES...]
  transfers between devices with their start and end apart: 4 -> 5, of which waited for: 0 -> 4; matrix products, arithmetic and copies ran while one was open for 4% -> 2% of each run, Pallas kernels for 5% -> 9%
where the time goes in v2:
time: 101 us
  Pallas kernels  33.4 us (33%)
  blocking collectives  25.1 us (25%)
  starting transfers between devices  19.4 us (19%)
  waiting for transfers between devices  18.2 us (18%)
  other arithmetic  2.49 us (2%)
  local copies, waits for them, and re-layouts  1.51 us (1%)
    all_to_all x1, blocking collectives, exchange(): lax.all_to_all(wire.reshape(PLANES, 1, WIRE_ROWS * LANES), ('gx', 'gy'),...  25.1 us
    all_to_all x1, waiting for transfers between devices, exchange(): lax.all_to_all(wire.reshape(PLANES, 1, WIRE_ROWS * LANES), ('gx', 'gy'),...  15.3 us
    pallas_call x1, Pallas kernels, atoms_call(): pl.pallas_call(atoms_kernel, out_shape=(jax.ShapeDtypeStruct((4, 4, LANES...  13.7 us
    all_to_all x1, starting transfers between devices, exchange(): lax.all_to_all(wire.reshape(PLANES, 1, WIRE_ROWS * LANES), ('gx', 'gy'),...  11.2 us
    pallas_call x1, Pallas kernels, plane_call(): pl.pallas_call(functools.partial(plane_kernel, count_x, count_y), out_sha...  6.1 us
    pallas_call x1, Pallas kernels, filter_call(): pl.pallas_call(filter_kernel, out_shape=jax.ShapeDtypeStruct((NX, NY), jn...  5.01 us
    pallas_call x1, Pallas kernels, force_call(): pl.pallas_call(force_kernel, out_shape=(jax.ShapeDtypeStruct((4, 4, LANES...  4.37 us
    pallas_call x1, Pallas kernels, first_pairs_call(): pl.pallas_call(first_pairs_kernel, out_shape=jax.ShapeDtypeStruct((SPECIE...  4.18 us
  transfers between devices with their start and end apart: 5, of which 4 were waited for; matrix products, arithmetic and copies ran while one was open for 2% of the time, Pallas kernels for 9%

profile of v2, /device:TPU:1, one launch (start us, length us, event | category | flops | bytes accessed | tf_op | source)
XLA Modules:
  0.0 100.8 jit_solution(10474339335206126568)
XLA Ops:
  0.6 0.7 convert_element_type.22
  1.3 0.8 add_multiply_fusion
  2.1 0.1 pad_select_fusion
  2.2 1.5 %collective-permute-start.1 = (f32[4,4,1,128]{3,2,1,0:T(1,128)S(1)}, f32[4,4,1,128]{3,2,1,0:T(1,128)S(1)}, u32[]{:S(2)}, u32[]{:S(2)}) collective-permute-start(f32[4,4,1,128]{3,2,1,0:T(1,128)S(1)} %get-tuple-element.13), channel_id=1, source_target_pairs={{8,0},{16,8},{24,16},{32,24},{40,32},{48,40},{56,48},{64,56},{72,6... | collective-permute-start | bytes 24584 | tf_op jit(solution)/shard_map/ppermute | solution.py:752
  3.7 2.8 %collective-permute-start = (f32[4,4,1,128]{3,2,1,0:T(1,128)S(1)}, f32[4,4,1,128]{3,2,1,0:T(1,128)S(1)}, u32[]{:S(2)}, u32[]{:S(2)}) collective-permute-start(f32[4,4,1,128]{3,2,1,0:T(1,128)S(1)} %get-tuple-element.14), channel_id=1, source_target_pairs={{0,8},{8,16},{16,24},{24,32},{32,40},{40,48},{48,56},{56,64},{64,7... | collective-permute-start | bytes 24584 | tf_op jit(solution)/shard_map/ppermute | solution.py:751
  6.5 1.3 %collective-permute-done.1 = f32[4,4,1,128]{3,2,1,0:T(1,128)S(1)} collective-permute-done((f32[4,4,1,128]{3,2,1,0:T(1,128)S(1)}, f32[4,4,1,128]{3,2,1,0:T(1,128)S(1)}, u32[]{:S(2)}, u32[]{:S(2)}) %collective-permute-start.1) | collective-permute-done | bytes 8224 | tf_op jit(solution)/shard_map/ppermute | solution.py:752
  7.7 1.6 %collective-permute-done = f32[4,4,1,128]{3,2,1,0:T(1,128)S(1)} collective-permute-done((f32[4,4,1,128]{3,2,1,0:T(1,128)S(1)}, f32[4,4,1,128]{3,2,1,0:T(1,128)S(1)}, u32[]{:S(2)}, u32[]{:S(2)}) %collective-permute-start) | collective-permute-done | bytes 8224 | tf_op jit(solution)/shard_map/ppermute | solution.py:751
  9.4 0.1 concatenate.3.ext_ref.place_ref
  9.4 3.9 %collective-permute-start.3 = (f32[4,4,8,128]{3,2,1,0:T(8,128)S(1)}, f32[4,4,8,128]{3,2,1,0:T(8,128)S(1)}, u32[]{:S(2)}, u32[]{:S(2)}) collective-permute-start(f32[4,4,8,128]{3,2,1,0:T(8,128)S(1)} %concatenate.3.ext_ref.place_ref), channel_id=1, source_target_pairs={{1,0},{2,1},{3,2},{4,3},{5,4},{6,5},{7,6},{0,7},{9,8},{10,9},{11,1... | collective-permute-start | bytes 196616 | tf_op jit(solution)/shard_map/ppermute | solution.py:756
  13.3 0.0 collective-permute-start.2
  13.3 0.9 add_add_fusion.packed_ref
  14.2 4.2 %first_pairs.1.begun_ref = f32[32,16,128]{2,1,0:T(8,128)S(1)} custom-call(f32[4,4,8,128]{3,2,1,0:T(8,128)S(1)} %concatenate.3.ext_ref.place_ref), custom_call_target="tpu_custom_call" | custom-call | flops 24000000 | bytes 524288 | tf_op jit(solution)/shard_map/first_pairs/pallas_call | solution.py:209
  18.4 0.0 collective-permute-done.3.right_ref
  18.4 0.1 collective-permute-done.2.left_ref
  18.5 13.7 %atoms.1 = (f32[4,4,128]{2,1,0:T(4,128)S(1)}, f32[4,4,128]{2,1,0:T(4,128)}, f32[2432,128]{1,0:T(8,128)}) custom-call(f32[4,4,8,128]{3,2,1,0:T(8,128)S(1)} %concatenate.3.ext_ref.place_ref, f32[4,4,8,128]{3,2,1,0:T(8,128)S(1)} %collective-permute-done.2.left_ref, f32[4,4,8,128]{3,2,1,0:T(8,128)S(1)} %collective-permute-done.3.right_ref, ...), custom_call_target="tpu_custom_call" | custom-call | tf_op jit(solution)/shard_map/atoms/pallas_call | solution.py:355
  32.3 0.0 copy-start.5
  32.3 0.6 copy-done.5
  32.9 0.0 copy-start.1
  32.9 0.0 copy-start.2
  32.9 11.2 %all-to-all-start = ((f32[128,1,2432]{2,1,0:T(1,128)}), f32[128,1,2432]{2,1,0:T(1,128)S(1)}, u32[]{:S(2)}, u32[]{:S(2)}) async-start(f32[128,1,2432]{2,1,0:T(1,128)} %bitcast.6), calls=%async_computation | async-start | bytes 2490368 | tf_op jit(solution)/shard_map/all_to_all | solution.py:737
  44.1 0.0 copy-start
  44.1 0.8 dynamic-slice_bitcast_fusion
  44.9 0.0 copy-done.1
  44.9 0.0 copy-done.2
  44.9 5.0 %filter.1.filter_ref = f32[512,512]{1,0:T(8,128)S(1)} custom-call(f32[65]{0:T(128)S(1)} %get-tuple-element.16.terms_ref, f32[65]{0:T(128)S(1)} %get-tuple-element.15.squares_ref, f32[16,512]{1,0:T(8,128)S(1)} %copy-done.2, f32[512,2]{1,0:T(8,128)S(1)} %copy-done.1), custom_call_target="tpu_custom_call" | custom-call | flops 20000000 | bytes 1048576 | tf_op jit(solution)/shard_map/filter/pallas_call | solution.py:443
  49.9 15.3 %all-to-all-done = f32[128,1,2432]{2,1,0:T(1,128)S(1)} async-done(((f32[128,1,2432]{2,1,0:T(1,128)}), f32[128,1,2432]{2,1,0:T(1,128)S(1)}, u32[]{:S(2)}, u32[]{:S(2)}) %all-to-all-start) | async-done | bytes 1245216 | tf_op jit(solution)/shard_map/all_to_all | solution.py:737
  65.2 0.0 copy-done
  65.2 6.1 %plane.1 = f32[2432,128]{1,0:T(8,128)S(1)} custom-call(f32[2432,128]{1,0:T(8,128)S(1)} %bitcast.14, f32[512,512]{1,0:T(8,128)S(1)} %filter.1.filter_ref, f32[352,640]{1,0:T(8,128)S(1)} %copy-done), custom_call_target="tpu_custom_call" | custom-call | tf_op jit(solution)/shard_map/plane/pallas_call | solution.py:608
  71.3 0.0 copy-start.3
  71.3 0.0 copy-start.4
  71.3 0.0 copy-start.6
  71.4 25.1 %all_to_all.10 = f32[128,1,2432]{2,1,0:T(1,128)S(1)} all-to-all(f32[128,1,2432]{2,1,0:T(1,128)S(1)} %bitcast.15), channel_id=1, replica_groups=mesh['gx'=16,'gy'=8] {'gx','gy'}, dimensions={0} | all-to-all | bytes 2490368 | tf_op jit(solution)/shard_map/all_to_all | solution.py:737
  96.4 0.0 copy-done.3
  96.4 0.0 copy-done.4
  96.4 0.0 copy-done.6
  96.4 4.4 %force.1 = (f32[4,4,128]{2,1,0:T(4,128)}, f32[3,4,4,128]{3,2,1,0:T(4,128)}) custom-call(f32[2432,128]{1,0:T(8,128)S(1)} %bitcast.16, f32[4,4,8,128]{3,2,1,0:T(8,128)S(1)} %concatenate.3.ext_ref.place_ref, f32[4,4,128]{2,1,0:T(4,128)S(1)} %copy-done.6, f32[4,4,128]{2,1,0:T(4,128)S(1)} %copy-done.4, f32[40,128]{1,0:T(8,128)S(1)} %copy-done.3), custom_call_target="tpu_custom_call" | custom-call | tf_op jit(solution)/shard_map/force/pallas_call | solution.py:719
  (2 shorter events, 0.0 us)
Async XLA Ops:
  2.2 5.5 %collective-permute-start.1 = (f32[4,4,1,128]{3,2,1,0:T(1,128)S(1)}, f32[4,4,1,128]{3,2,1,0:T(1,128)S(1)}, u32[]{:S(2)}, u32[]{:S(2)}) collective-permute-start(f32[4,4,1,128]{3,2,1,0:T(1,128)S(1)} %get-tuple-element.13), channel_id=1, source_target_pairs={{8,0},{16,8},{24,16},{32,24},{40,32},{48,40},{56,48},{64,56},{72,6... | collective-permute-start | bytes 24584 | tf_op jit(solution)/shard_map/ppermute | solution.py:752
  3.7 5.7 %collective-permute-start = (f32[4,4,1,128]{3,2,1,0:T(1,128)S(1)}, f32[4,4,1,128]{3,2,1,0:T(1,128)S(1)}, u32[]{:S(2)}, u32[]{:S(2)}) collective-permute-start(f32[4,4,1,128]{3,2,1,0:T(1,128)S(1)} %get-tuple-element.14), channel_id=1, source_target_pairs={{0,8},{8,16},{16,24},{24,32},{32,40},{40,48},{48,56},{56,64},{64,7... | collective-permute-start | bytes 24584 | tf_op jit(solution)/shard_map/ppermute | solution.py:751
  9.4 9.0 %collective-permute-start.3 = (f32[4,4,8,128]{3,2,1,0:T(8,128)S(1)}, f32[4,4,8,128]{3,2,1,0:T(8,128)S(1)}, u32[]{:S(2)}, u32[]{:S(2)}) collective-permute-start(f32[4,4,8,128]{3,2,1,0:T(8,128)S(1)} %concatenate.3.ext_ref.place_ref), channel_id=1, source_target_pairs={{1,0},{2,1},{3,2},{4,3},{5,4},{6,5},{7,6},{0,7},{9,8},{10,9},{11,1... | collective-permute-start | bytes 196616 | tf_op jit(solution)/shard_map/ppermute | solution.py:756
  13.3 5.2 %collective-permute-start.2 = (f32[4,4,8,128]{3,2,1,0:T(8,128)S(1)}, f32[4,4,8,128]{3,2,1,0:T(8,128)S(1)}, u32[]{:S(2)}, u32[]{:S(2)}) collective-permute-start(f32[4,4,8,128]{3,2,1,0:T(8,128)S(1)} %concatenate.3.ext_ref.place_ref), channel_id=1, source_target_pairs={{0,1},{1,2},{2,3},{3,4},{4,5},{5,6},{6,7},{7,0},{8,9},{9,10},{10,1... | collective-permute-start | bytes 196616 | tf_op jit(solution)/shard_map/ppermute | solution.py:755
  32.3 0.6 copy-start.5
  32.9 12.1 %copy-start.1 = (f32[512,2]{1,0:T(8,128)S(1)}, f32[512,2]{1,0:T(8,128)}, u32[]{:S(2)}) copy-start(f32[512,2]{1,0:T(8,128)} %constant.45.clone.column_ref) | copy-start | bytes 12292
  32.9 12.1 %copy-start.2 = (f32[16,512]{1,0:T(8,128)S(1)}, f32[16,512]{1,0:T(8,128)}, u32[]{:S(2)}) copy-start(f32[16,512]{1,0:T(8,128)} %constant.44.clone.row_ref) | copy-start | bytes 98308
  32.9 32.4 %all-to-all-start = ((f32[128,1,2432]{2,1,0:T(1,128)}), f32[128,1,2432]{2,1,0:T(1,128)S(1)}, u32[]{:S(2)}, u32[]{:S(2)}) async-start(f32[128,1,2432]{2,1,0:T(1,128)} %bitcast.6), calls=%async_computation | async-start | bytes 2490368 | tf_op jit(solution)/shard_map/all_to_all | solution.py:737
  44.1 21.1 %copy-start = (f32[352,640]{1,0:T(8,128)S(1)}, f32[352,640]{1,0:T(8,128)}, u32[]{:S(2)}) copy-start(f32[352,640]{1,0:T(8,128)} %constant.47.clone.table_ref) | copy-start | bytes 2703364
  71.3 25.1 %copy-start.3 = (f32[40,128]{1,0:T(8,128)S(1)}, f32[40,128]{1,0:T(8,128)}, u32[]{:S(2)}) copy-start(f32[40,128]{1,0:T(8,128)} %constant.48.clone.basis_ref) | copy-start | bytes 61444
  71.3 25.1 %copy-start.4 = (f32[4,4,128]{2,1,0:T(4,128)S(1)}, f32[4,4,128]{2,1,0:T(4,128)}, u32[]{:S(2)}) copy-start(f32[4,4,128]{2,1,0:T(4,128)} %get-tuple-element.7.charge_ref) | copy-start | bytes 24580
  71.3 25.1 %copy-start.6 = (f32[4,4,128]{2,1,0:T(4,128)S(1)}, f32[4,4,128]{2,1,0:T(4,128)}, u32[]{:S(2)}) copy-start(f32[4,4,128]{2,1,0:T(4,128)} %copy-done.5) | copy-start | bytes 24580

commit v3 on v2

--- a/solution.py
+++ b/solution.py
@@ -371,7 +371,7 @@
     )(ext, left, right, begun, packed)
 
 
-def filter_kernel(terms_ref, squares_ref, row_ref, column_ref, out_ref):
+def filter_kernel(terms_ref, squares_ref, row_ref, out_ref):
     half = NX // 2
     count = NZ // 4
 
@@ -394,25 +394,25 @@
         extra = terms_ref[0] / jnp.where(even > 0.0, even, 1.0)
         return total + jnp.where(even > 0.0, extra, 0.0)
 
-    edge = series(row_ref[0:8, :] + 0.25) * row_ref[8:16, :] * column_ref[half : half + 8, 1:2]
-    edge = edge[0:1, :]
-    edge_low, edge_corner = edge[:, :half], edge[:, half : half + 1]
+    square_row, factor_row = row_ref[0:1, :], row_ref[8:9, :]
+    middle = row_ref[8:9, half : half + 1]
+    edge = series(row_ref[0:8, :] + 0.25) * factor_row * middle
+    out_ref[half:, :half] = edge[:, :half]
+    first = iota((8, half), 1) == 0
+    out_ref[half:, half:] = jnp.where(first, edge[:, half : half + 1], edge[:, :half])
     first_lane = iota((16, half), 1) == 0
+    edge = edge[0:1, :half]
 
     def body(n, _):
         at = pl.multiple_of(n * 16, 16)
-        column = column_ref[pl.ds(at, 16), :]
-        value = series(row_ref[0:1, :half] + column[:, 0:1]) * row_ref[8:9, :half] * column[:, 1:2]
-        row = at + iota((16, half), 0)
-        mirror = jnp.sum(
-            jnp.where(row == iota((16, half), 1), edge_low, 0.0), axis=1, keepdims=True
-        )
-        right = jnp.where(first_lane, mirror, value)
+        here = at + iota((16, half), 0) == iota((16, half), 1)
+
+        def column(row):
+            return jnp.sum(jnp.where(here, row[:, :half], 0.0), axis=1, keepdims=True)
+
+        value = series(square_row[:, :half] + column(square_row)) * factor_row[:, :half] * column(factor_row)
         out_ref[pl.ds(at, 16), :half] = value
-        out_ref[pl.ds(at, 16), half:] = right
-        out_ref[pl.ds(half + at, 16), :half] = jnp.where(row == 0, edge_low, value)
-        corner = jnp.where(first_lane, edge_corner, edge_low)
-        out_ref[pl.ds(half + at, 16), half:] = jnp.where(row == 0, corner, right)
+        out_ref[pl.ds(at, 16), half:] = jnp.where(first_lane, column(edge), value)
         return 0
 
     lax.fori_loop(0, half // 16, body, 0)
@@ -437,13 +437,12 @@
     terms, squares = filter_tables()
     square, factor = axis_factor(wave_order(NX), NX)
     row = np.repeat(np.stack([square, factor]), 8, axis=0).astype(np.float32)
-    column = np.stack([square, factor], axis=1).astype(np.float32)
     smem = pl.BlockSpec(memory_space=pltpu.SMEM)
     vmem = pl.BlockSpec(memory_space=pltpu.VMEM)
     return pl.pallas_call(
         filter_kernel,
-        out_shape=jax.ShapeDtypeStruct((NX, NY), jnp.float32),
-        in_specs=[smem, smem, vmem, vmem],
+        out_shape=jax.ShapeDtypeStruct((NX // 2 + 8, NY), jnp.float32),
+        in_specs=[smem, smem, vmem],
         compiler_params=pltpu.CompilerParams(vmem_limit_bytes=VMEM_BYTES),
         cost_estimate=pl.CostEstimate(flops=20_000_000, bytes_accessed=1 << 20, transcendentals=0),
         name="filter",
@@ -451,7 +450,6 @@
         lax.dynamic_index_in_dim(jnp.asarray(terms), plane, 0, keepdims=False),
         lax.dynamic_index_in_dim(jnp.asarray(squares), plane, 0, keepdims=False),
         row,
-        column,
     )
 
 
@@ -489,7 +487,7 @@
         fill(y_high, y_low, 16 * a, cosine[at] * part("y cas", NY) + sine[at] * part("y sac", NY))
     cosine, sine = part("x cos", NX), part("x sin", NX)
     plus, minus = part("x cas", NX), part("x sac", NX)
-    for x in range(2 * PATCH_ROWS):
+    for x in range(width // 16):
         at = slice(x, x + 1)
         fill(x_high, x_low, 16 * x, cosine * plus[at] + sine * minus[at])
     for name, lanes, high, low in (("yt", NY, yt_high, yt_low), ("xt", width, xt_high, xt_low)):
@@ -509,40 +507,54 @@
     lane = iota((count_x, LANES), 1)
     low_half = lane < 64
     tails = [wire_ref[pl.ds(j * WIRE_ROWS + PATCH_ROWS, count_x, stride=stride), :] for j in range(count_y)]
+    own_rows = PATCH_ROWS - 2
     for m in range(pairs):
         before = tails[(2 * m - 1) % count_y]
         between = tails[2 * m]
-        for r in range(PATCH_ROWS):
+
+        def unpacked(x):
+            r, h = x // 2, x % 2
             one = wire_ref[pl.ds(2 * m * WIRE_ROWS + r, count_x, stride=stride), :]
             two = wire_ref[pl.ds((2 * m + 1) * WIRE_ROWS + r, count_x, stride=stride), :]
-            for h in range(2):
-                x = 2 * r + h
-                if h == 0:
-                    value = jnp.where(low_half, one, pltpu.roll(two, 64, 1))
-                else:
-                    value = jnp.where(low_half, pltpu.roll(one, 64, 1), two)
-                first = pltpu.roll(before, (LANES - 3 * x) % LANES, 1) if x else before
-                second = pltpu.roll(between, (LANES + 64 - 3 * x) % LANES, 1)
-                value = value + jnp.where(lane < 3, first, 0.0)
-                value = value + jnp.where((lane >= 64) & (lane < 67), second, 0.0)
-                high, low = split(value)
-                at = x * count_x
-                grid_high[at : at + count_x, m * LANES : (m + 1) * LANES] = high
-                grid_low[at : at + count_x, m * LANES : (m + 1) * LANES] = low
+            if h == 0:
+                value = jnp.where(low_half, one, pltpu.roll(two, 64, 1))
+            else:
+                value = jnp.where(low_half, pltpu.roll(one, 64, 1), two)
+            first = pltpu.roll(before, (LANES - 3 * x) % LANES, 1) if x else before
+            second = pltpu.roll(between, (LANES + 64 - 3 * x) % LANES, 1)
+            value = value + jnp.where(lane < 3, first, 0.0)
+            return value + jnp.where((lane >= 64) & (lane < 67), second, 0.0)
+
+        for x in range(2 * own_rows):
+            value = unpacked(x)
+            if x < 3:
+                value = value + pltpu.roll(unpacked(x + 2 * own_rows), 1, 0)
+            high, low = split(value)
+            at = x * count_x
+            grid_high[at : at + count_x, m * LANES : (m + 1) * LANES] = high
+            grid_low[at : at + count_x, m * LANES : (m + 1) * LANES] = low
 
     step = split(dot3((grid_high[...], grid_low[...]), (y_high[...], y_low[...])))
-    spectrum = dot3((xt_high[...], xt_low[...]), step) * filter_ref[...]
+    spectrum = dot3((xt_high[...], xt_low[...]), step)
+    half = NX // 2
+    upper = filter_ref[:half, :]
+    lower = jnp.where(iota((half, NY), 0) == 0, filter_ref[half : half + 1, :], upper)
+    spectrum = jnp.concatenate([spectrum[:half] * upper, spectrum[half:] * lower], axis=0)
     mean = spectrum[0:1, 0:1]
     first = (iota((8, NX), 0) == 0) & (iota((8, NX), 1) == 0)
     spectrum = jnp.concatenate([jnp.where(first, 0.0, spectrum[:8]), spectrum[8:]], axis=0)
     step = split(dot3((x_high[...], x_low[...]), split(spectrum)))
     result_ref[...] = dot3(step, (yt_high[...], yt_low[...]))
 
+    def result_row(x, m):
+        here = x % (2 * own_rows)
+        value = result_ref[here * count_x : (here + 1) * count_x, m * LANES : (m + 1) * LANES]
+        return pltpu.roll(value, count_x - 1, 0) if x >= 2 * own_rows else value
+
     for j in range(count_y):
         m = j // 2
         for r in range(PATCH_ROWS):
-            even = result_ref[2 * r * count_x : (2 * r + 1) * count_x, m * LANES : (m + 1) * LANES]
-            odd = result_ref[(2 * r + 1) * count_x : (2 * r + 2) * count_x, m * LANES : (m + 1) * LANES]
+            even, odd = result_row(2 * r, m), result_row(2 * r + 1, m)
             if j % 2 == 0:
                 value = jnp.where(low_half, even, pltpu.roll(odd, 64, 1))
             else:
@@ -552,7 +564,7 @@
         m = after // 2
         tail = jnp.where(lane == LANES - 1, mean, 0.0)
         for x in range(2 * PATCH_ROWS):
-            value = result_ref[x * count_x : (x + 1) * count_x, m * LANES : (m + 1) * LANES]
+            value = result_row(x, m)
             shift = (3 * x - 64 * (after % 2)) % LANES
             if shift:
                 value = pltpu.roll(value, shift, 1)
@@ -562,7 +574,7 @@
 
 def table_layout():
     heights = {"y cos": 32, "y sin": 32, "y cas": 16, "y sac": 16}
-    heights.update({"x cos": 16, "x sin": 16, "x cas": 40, "x sac": 40})
+    heights.update({"x cos": 16, "x sin": 16, "x cas": 32, "x sac": 32})
     for name in ("yt", "xt"):
         heights.update({name + " cos": 16, name + " sin": 16, name + " cas": 16, name + " sac": 16, name + " mid": 8})
     layout, first = {}, 0
@@ -577,8 +589,9 @@
 
 def plane_tables(count_x):
     wave, cell = wave_order(NY), np.arange(NY)
-    place = (np.arange(2 * PATCH_ROWS)[:, None] + (NX // count_x) * np.arange(count_x)).reshape(-1)
-    out = np.zeros((TABLE_ROWS, 640), np.float32)
+    own = np.arange(NX // count_x)
+    place = (own[:, None] + (NX // count_x) * np.arange(count_x)).reshape(-1)
+    out = np.zeros((TABLE_ROWS, NX), np.float32)
 
     def put(name, rows, lanes):
         angle = 2.0 * np.pi / NX * (np.outer(rows, lanes) % NX)
@@ -595,7 +608,7 @@
         put("xt " + kind, 16 * sixteen, place)
     for kind in ("cas", "sac"):
         put("y " + kind, sixteen, wave)
-        put("x " + kind, np.arange(2 * PATCH_ROWS), wave)
+        put("x " + kind, own, wave)
         put("yt " + kind, sixteen, cell)
         put("xt " + kind, sixteen, place)
     put("yt mid", np.array([NY // 2]), cell)
@@ -604,17 +617,16 @@
 
 
 def plane_call(wire, table, tables, count_x, count_y):
-    rows = 2 * PATCH_ROWS
     return pl.pallas_call(
         functools.partial(plane_kernel, count_x, count_y),
         out_shape=jax.ShapeDtypeStruct((PLANES * WIRE_ROWS, LANES), jnp.float32),
         scratch_shapes=[
-            pltpu.VMEM((rows * count_x, NY), jnp.bfloat16),
-            pltpu.VMEM((rows * count_x, NY), jnp.bfloat16),
-            pltpu.VMEM((rows * count_x, NY), jnp.float32),
+            pltpu.VMEM((NX, NY), jnp.bfloat16),
+            pltpu.VMEM((NX, NY), jnp.bfloat16),
+            pltpu.VMEM((NX, NY), jnp.float32),
             *[pltpu.VMEM((NY, NY), jnp.bfloat16)] * 4,
-            *[pltpu.VMEM((rows * count_x, NX), jnp.bfloat16)] * 2,
-            *[pltpu.VMEM((NX, rows * count_x), jnp.bfloat16)] * 2,
+            *[pltpu.VMEM((NX, NX), jnp.bfloat16)] * 2,
+            *[pltpu.VMEM((NX, NX), jnp.bfloat16)] * 2,
         ],
         compiler_params=pltpu.CompilerParams(vmem_limit_bytes=VMEM_BYTES),
         name="plane",
@@ -743,13 +755,16 @@
 def shards(atom_cells, atom_frac, species, *weights):
     count_x, count_y = lax.axis_size("gx"), lax.axis_size("gy")
     assert count_x * count_y == PLANES and atom_cells.shape[1:] == (4, 4, LANES)
-    place = ((atom_cells & (BLOCK - 1)).astype(jnp.float32) + atom_frac) * (1.0 / BLOCK)
-    kinds = species.astype(jnp.float32)[None]
-    own = jnp.pad(place, ((0, 1), (0, 0), (0, 0), (0, 0)))
-    own = jnp.where(lax.broadcasted_iota(jnp.int32, own.shape, 0) == 3, kinds, own)
+    shape = (4,) + species.shape
+    is_kind = lax.broadcasted_iota(jnp.int32, shape, 0) == 3
+    last = ((0, 1), (0, 0), (0, 0), (0, 0))
+    whole = jnp.where(is_kind, jnp.broadcast_to(species, shape), jnp.pad(atom_cells & (BLOCK - 1), last))
+    own = (whole.astype(jnp.float32) + jnp.pad(atom_frac, last)) * jnp.where(is_kind, 1.0, 1.0 / BLOCK)
+    packed = pack_weights(*weights)
     up, down = ring(count_x)
     before = lax.ppermute(own[:, :, 3:4, :], "gx", up)
     after = lax.ppermute(own[:, :, 0:1, :], "gx", down)
+    before, after, packed = lax.optimization_barrier((before, after, packed))
     ext = jnp.concatenate([before, own, after, after, after], axis=2)
     up, down = ring(count_y)
     left = lax.ppermute(ext, "gy", up)
@@ -757,7 +772,7 @@
     tables = plane_tables(count_x)
     table = filter_call(lax.axis_index(("gx", "gy")))
     begun = first_pairs_call(ext)
-    short, charge, wire = atoms_call(ext, left, right, begun, pack_weights(*weights))
+    short, charge, wire = atoms_call(ext, left, right, begun, packed)
     wire = exchange(wire)
     wire = plane_call(wire, table, tables, count_x, count_y)
     wire = exchange(wire)

time: 101 us -> 96.9 us (0.959)
  starting transfers between devices: 19.4 us -> 15.6 us
    all_to_all x1, starting transfers between devices: 11.2 us -> 7.44 us  [exchange(): lax.all_to_all(wire.reshape(PLANES, 1, WIRE_ROWS * LANES), ('gx', 'gy'),...]
    ppermute x1, waiting for transfers between devices: 1.25 us -> 3.62 us  [shards(): after = lax.ppermute(own[:, :, 0:1, :], 'gx', down)]
    ppermute x1, starting transfers between devices: 0.01 us -> 1.7 us  [shards(): left = lax.ppermute(ext, 'gy', up)]
    ppermute x1, starting transfers between devices: 3.85 us -> 2.23 us  [shards(): right = lax.ppermute(ext, 'gy', down)]
    ppermute x1, waiting for transfers between devices: 1.61 us -> 0.01 us  [shards(): before = lax.ppermute(own[:, :, 3:4, :], 'gx', up)]
    ppermute x1, starting transfers between devices: 1.49 us -> 0.01 us  [shards(): after = lax.ppermute(own[:, :, 0:1, :], 'gx', down)]
    ppermute x1, starting transfers between devices: 2.79 us -> 4.2 us  [shards(): before = lax.ppermute(own[:, :, 3:4, :], 'gx', up)]
  transfers between devices with their start and end apart: 5 -> 5, of which waited for: 4 -> 2; matrix products, arithmetic and copies ran while one was open for 2% -> 2% of each run, Pallas kernels for 9% -> 9%
where the time goes in v3:
time: 96.9 us; the launch traced here: 96.5 us
  Pallas kernels  32.6 us (34%)
  blocking collectives  25.1 us (26%)
  waiting for transfers between devices  19.1 us (20%)
  starting transfers between devices  15.6 us (16%)
  other arithmetic  2.51 us (3%)
    all_to_all x1, blocking collectives, exchange(): lax.all_to_all(wire.reshape(PLANES, 1, WIRE_ROWS * LANES), ('gx', 'gy'),...  25.1 us
    all_to_all x1, waiting for transfers between devices, exchange(): lax.all_to_all(wire.reshape(PLANES, 1, WIRE_ROWS * LANES), ('gx', 'gy'),...  15.5 us
    pallas_call x1, Pallas kernels, atoms_call(): pl.pallas_call(atoms_kernel, out_shape=(jax.ShapeDtypeStruct((4, 4, LANES...  13.7 us
    all_to_all x1, starting transfers between devices, exchange(): lax.all_to_all(wire.reshape(PLANES, 1, WIRE_ROWS * LANES), ('gx', 'gy'),...  7.44 us
    pallas_call x1, Pallas kernels, plane_call(): pl.pallas_call(functools.partial(plane_kernel, count_x, count_y), out_sha...  5.43 us
    pallas_call x1, Pallas kernels, filter_call(): pl.pallas_call(filter_kernel, out_shape=jax.ShapeDtypeStruct((NX // 2 + 8...  4.9 us
    pallas_call x1, Pallas kernels, force_call(): pl.pallas_call(force_kernel, out_shape=(jax.ShapeDtypeStruct((4, 4, LANES...  4.37 us
    ppermute x1, starting transfers between devices, shards(): before = lax.ppermute(own[:, :, 3:4, :], 'gx', up)  4.2 us
  transfers between devices with their start and end apart: 5, of which 2 were waited for; matrix products, arithmetic and copies ran while one was open for 2% of the time, Pallas kernels for 9%

profile of v3, /device:TPU:1, one launch (start us, length us, event | category | flops | bytes accessed | tf_op | source)
XLA Modules:
  0.0 96.5 jit_solution(15641410654501661915)
XLA Ops:
  0.7 0.7 broadcast_and_fusion
  1.4 0.8 add_multiply_fusion
  2.2 4.2 %collective-permute-start = (f32[4,4,1,128]{3,2,1,0:T(1,128)S(1)}, f32[4,4,1,128]{3,2,1,0:T(1,128)S(1)}, u32[]{:S(2)}, u32[]{:S(2)}) collective-permute-start(f32[4,4,1,128]{3,2,1,0:T(1,128)S(1)} %get-tuple-element.20), channel_id=1, source_target_pairs={{0,8},{8,16},{16,24},{24,32},{32,40},{40,48},{48,56},{56,64},{64,7... | collective-permute-start | bytes 24584 | tf_op jit(solution)/shard_map/ppermute | solution.py:765
  6.4 0.0 collective-permute-start.1
  6.5 0.9 add_add_fusion.packed_ref
  7.4 0.0 collective-permute-done
  7.4 3.6 %collective-permute-done.1 = f32[4,4,1,128]{3,2,1,0:T(1,128)S(1)} collective-permute-done((f32[4,4,1,128]{3,2,1,0:T(1,128)S(1)}, f32[4,4,1,128]{3,2,1,0:T(1,128)S(1)}, u32[]{:S(2)}, u32[]{:S(2)}) %collective-permute-start.1) | collective-permute-done | bytes 8224 | tf_op jit(solution)/shard_map/ppermute | solution.py:766
  11.0 0.1 concatenate.3.ext_ref.place_ref
  11.1 1.7 %collective-permute-start.2 = (f32[4,4,8,128]{3,2,1,0:T(8,128)S(1)}, f32[4,4,8,128]{3,2,1,0:T(8,128)S(1)}, u32[]{:S(2)}, u32[]{:S(2)}) collective-permute-start(f32[4,4,8,128]{3,2,1,0:T(8,128)S(1)} %concatenate.3.ext_ref.place_ref), channel_id=1, source_target_pairs={{0,1},{1,2},{2,3},{3,4},{4,5},{5,6},{6,7},{7,0},{8,9},{9,10},{10,1... | collective-permute-start | bytes 196616 | tf_op jit(solution)/shard_map/ppermute | solution.py:770
  12.8 2.2 %collective-permute-start.3 = (f32[4,4,8,128]{3,2,1,0:T(8,128)S(1)}, f32[4,4,8,128]{3,2,1,0:T(8,128)S(1)}, u32[]{:S(2)}, u32[]{:S(2)}) collective-permute-start(f32[4,4,8,128]{3,2,1,0:T(8,128)S(1)} %concatenate.3.ext_ref.place_ref), channel_id=1, source_target_pairs={{1,0},{2,1},{3,2},{4,3},{5,4},{6,5},{7,6},{0,7},{9,8},{10,9},{11,1... | collective-permute-start | bytes 196616 | tf_op jit(solution)/shard_map/ppermute | solution.py:771
  15.0 4.2 %first_pairs.1.begun_ref = f32[32,16,128]{2,1,0:T(8,128)S(1)} custom-call(f32[4,4,8,128]{3,2,1,0:T(8,128)S(1)} %concatenate.3.ext_ref.place_ref), custom_call_target="tpu_custom_call" | custom-call | flops 24000000 | bytes 524288 | tf_op jit(solution)/shard_map/first_pairs/pallas_call | solution.py:209
  19.2 0.0 collective-permute-done.2.left_ref
  19.2 0.0 collective-permute-done.3.right_ref
  19.2 13.7 %atoms.1 = (f32[4,4,128]{2,1,0:T(4,128)S(1)}, f32[4,4,128]{2,1,0:T(4,128)}, f32[2432,128]{1,0:T(8,128)}) custom-call(f32[4,4,8,128]{3,2,1,0:T(8,128)S(1)} %concatenate.3.ext_ref.place_ref, f32[4,4,8,128]{3,2,1,0:T(8,128)S(1)} %collective-permute-done.2.left_ref, f32[4,4,8,128]{3,2,1,0:T(8,128)S(1)} %collective-permute-done.3.right_ref, ...), custom_call_target="tpu_custom_call" | custom-call | tf_op jit(solution)/shard_map/atoms/pallas_call | solution.py:355
  33.0 0.0 copy-start.1
  33.0 0.0 copy-start
  33.0 7.4 %all-to-all-start = ((f32[128,1,2432]{2,1,0:T(1,128)}), f32[128,1,2432]{2,1,0:T(1,128)S(1)}, u32[]{:S(2)}, u32[]{:S(2)}) async-start(f32[128,1,2432]{2,1,0:T(1,128)} %bitcast.6), calls=%async_computation | async-start | bytes 2490368 | tf_op jit(solution)/shard_map/all_to_all | solution.py:749
  40.4 0.7 dynamic-slice_bitcast_fusion
  41.2 0.0 copy-done.1
  41.2 4.9 %filter.1.filter_ref = f32[264,512]{1,0:T(8,128)S(1)} custom-call(f32[65]{0:T(128)S(1)} %get-tuple-element.22.terms_ref, f32[65]{0:T(128)S(1)} %get-tuple-element.21.squares_ref, f32[16,512]{1,0:T(8,128)S(1)} %copy-done.1), custom_call_target="tpu_custom_call" | custom-call | flops 20000000 | bytes 1048576 | tf_op jit(solution)/shard_map/filter/pallas_call | solution.py:442
  46.1 15.5 %all-to-all-done = f32[128,1,2432]{2,1,0:T(1,128)S(1)} async-done(((f32[128,1,2432]{2,1,0:T(1,128)}), f32[128,1,2432]{2,1,0:T(1,128)S(1)}, u32[]{:S(2)}, u32[]{:S(2)}) %all-to-all-start) | async-done | bytes 1245216 | tf_op jit(solution)/shard_map/all_to_all | solution.py:749
  61.5 0.0 copy-done
  61.5 5.4 %plane.1 = f32[2432,128]{1,0:T(8,128)S(1)} custom-call(f32[2432,128]{1,0:T(8,128)S(1)} %bitcast.14, f32[264,512]{1,0:T(8,128)S(1)} %filter.1.filter_ref, f32[336,512]{1,0:T(8,128)S(1)} %copy-done), custom_call_target="tpu_custom_call" | custom-call | tf_op jit(solution)/shard_map/plane/pallas_call | solution.py:620
  67.0 0.0 copy-start.2
  67.0 0.0 copy-start.3
  67.0 25.1 %all_to_all.10 = f32[128,1,2432]{2,1,0:T(1,128)S(1)} all-to-all(f32[128,1,2432]{2,1,0:T(1,128)S(1)} %bitcast.15), channel_id=1, replica_groups=mesh['gx'=16,'gy'=8] {'gx','gy'}, dimensions={0} | all-to-all | bytes 2490368 | tf_op jit(solution)/shard_map/all_to_all | solution.py:749
  92.1 0.0 copy-done.2
  92.1 0.0 copy-done.3
  92.1 4.4 %force.1 = (f32[4,4,128]{2,1,0:T(4,128)}, f32[3,4,4,128]{3,2,1,0:T(4,128)}) custom-call(f32[2432,128]{1,0:T(8,128)S(1)} %bitcast.16, f32[4,4,8,128]{3,2,1,0:T(8,128)S(1)} %concatenate.3.ext_ref.place_ref, f32[4,4,128]{2,1,0:T(4,128)S(1)} %get-tuple-element.15.short_ref, f32[4,4,128]{2,1,0:T(4,128)S(1)} %copy-done.3, f32[40,128]{1,0:T(8,128)S(1)} %copy-done.2), custom_call_target="tpu_custom_call" | custom-call | tf_op jit(solution)/shard_map/force/pallas_call | solution.py:731
  (3 shorter events, 0.0 us)
Async XLA Ops:
  2.2 5.2 %collective-permute-start = (f32[4,4,1,128]{3,2,1,0:T(1,128)S(1)}, f32[4,4,1,128]{3,2,1,0:T(1,128)S(1)}, u32[]{:S(2)}, u32[]{:S(2)}) collective-permute-start(f32[4,4,1,128]{3,2,1,0:T(1,128)S(1)} %get-tuple-element.20), channel_id=1, source_target_pairs={{0,8},{8,16},{16,24},{24,32},{32,40},{40,48},{48,56},{56,64},{64,7... | collective-permute-start | bytes 24584 | tf_op jit(solution)/shard_map/ppermute | solution.py:765
  6.4 4.6 %collective-permute-start.1 = (f32[4,4,1,128]{3,2,1,0:T(1,128)S(1)}, f32[4,4,1,128]{3,2,1,0:T(1,128)S(1)}, u32[]{:S(2)}, u32[]{:S(2)}) collective-permute-start(f32[4,4,1,128]{3,2,1,0:T(1,128)S(1)} %get-tuple-element.19), channel_id=1, source_target_pairs={{8,0},{16,8},{24,16},{32,24},{40,32},{48,40},{56,48},{64,56},{72,6... | collective-permute-start | bytes 24584 | tf_op jit(solution)/shard_map/ppermute | solution.py:766
  11.1 8.1 %collective-permute-start.2 = (f32[4,4,8,128]{3,2,1,0:T(8,128)S(1)}, f32[4,4,8,128]{3,2,1,0:T(8,128)S(1)}, u32[]{:S(2)}, u32[]{:S(2)}) collective-permute-start(f32[4,4,8,128]{3,2,1,0:T(8,128)S(1)} %concatenate.3.ext_ref.place_ref), channel_id=1, source_target_pairs={{0,1},{1,2},{2,3},{3,4},{4,5},{5,6},{6,7},{7,0},{8,9},{9,10},{10,1... | collective-permute-start | bytes 196616 | tf_op jit(solution)/shard_map/ppermute | solution.py:770
  12.8 6.4 %collective-permute-start.3 = (f32[4,4,8,128]{3,2,1,0:T(8,128)S(1)}, f32[4,4,8,128]{3,2,1,0:T(8,128)S(1)}, u32[]{:S(2)}, u32[]{:S(2)}) collective-permute-start(f32[4,4,8,128]{3,2,1,0:T(8,128)S(1)} %concatenate.3.ext_ref.place_ref), channel_id=1, source_target_pairs={{1,0},{2,1},{3,2},{4,3},{5,4},{6,5},{7,6},{0,7},{9,8},{10,9},{11,1... | collective-permute-start | bytes 196616 | tf_op jit(solution)/shard_map/ppermute | solution.py:771
  33.0 8.2 %copy-start.1 = (f32[16,512]{1,0:T(8,128)S(1)}, f32[16,512]{1,0:T(8,128)}, u32[]{:S(2)}) copy-start(f32[16,512]{1,0:T(8,128)} %constant.45.clone.row_ref) | copy-start | bytes 98308
  33.0 28.6 %copy-start = (f32[336,512]{1,0:T(8,128)S(1)}, f32[336,512]{1,0:T(8,128)}, u32[]{:S(2)}) copy-start(f32[336,512]{1,0:T(8,128)} %constant.46.clone.table_ref) | copy-start | bytes 2064388
  33.0 28.6 %all-to-all-start = ((f32[128,1,2432]{2,1,0:T(1,128)}), f32[128,1,2432]{2,1,0:T(1,128)S(1)}, u32[]{:S(2)}, u32[]{:S(2)}) async-start(f32[128,1,2432]{2,1,0:T(1,128)} %bitcast.6), calls=%async_computation | async-start | bytes 2490368 | tf_op jit(solution)/shard_map/all_to_all | solution.py:749
  67.0 25.1 %copy-start.2 = (f32[40,128]{1,0:T(8,128)S(1)}, f32[40,128]{1,0:T(8,128)}, u32[]{:S(2)}) copy-start(f32[40,128]{1,0:T(8,128)} %constant.47.clone.basis_ref) | copy-start | bytes 61444
  67.0 25.1 %copy-start.3 = (f32[4,4,128]{2,1,0:T(4,128)S(1)}, f32[4,4,128]{2,1,0:T(4,128)}, u32[]{:S(2)}) copy-start(f32[4,4,128]{2,1,0:T(4,128)} %get-tuple-element.10.charge_ref) | copy-start | bytes 24580

commit v4 on v3

--- a/solution.py
+++ b/solution.py
@@ -145,25 +145,52 @@
     return (cell - 1 - 8 * block).astype(jnp.float32) - 8.0 * pos_y
 
 
+def place_rows(near_ref, n, c, bz, value):
+    near_ref[n, c, 4 * bz : 4 * bz + 4, :] = value
+    if bz == 0:
+        near_ref[n, c, 16:20, :] = value
+    if bz == ZBLOCKS - 1:
+        near_ref[n, c, 20:24, :] = value
+
+
 def place_blocks(near_ref, n, blocks, dx, dy):
-    far = jnp.full((4, LANES), 100.0, jnp.float32)
     for c in range(4):
         offset = float((dx - 1, dy - 1, 0, 0)[c])
         for bz in range(ZBLOCKS):
             row = (c * ZBLOCKS + bz) * 8 + dx
-            near_ref[n, c, 4 + 4 * bz : 8 + 4 * bz, :] = blocks[row : row + 4, :] + offset
-        near_ref[n, c, 0:4, :] = far
-        near_ref[n, c, 20:24, :] = far
-
-
-def pair_sums(near_ref, count, center, mine, half, sums):
+            place_rows(near_ref, n, c, bz, blocks[row : row + 4, :] + offset)
+
+
+def own_rows(own_ref, blocks):
+    for c in range(4):
+        for bz in range(ZBLOCKS):
+            row = (c * ZBLOCKS + bz) * 8 + 1
+            own_ref[c, 4 * bz : 4 * bz + 4, :] = blocks[row : row + 4, :]
+
+
+def pair_sums(near_ref, count, center, own_rows_of, begun_ref, out_ref):
+    zero = jnp.zeros((8, LANES), jnp.float32)
+    for first, steps in ((0, ((0, 0), (4, 1))), (8, ((8, 0), (4, -1))), (4, ((16, None),))):
+        at = slice(first, first + 8)
+        mine = [own_rows_of(c, at) for c in range(3)]
+        if begun_ref is None or first == 4:
+            sums = (zero,) * (2 * RADIAL)
+        else:
+            sums = tuple(begun_ref[k, at, :] for k in range(2 * RADIAL))
+        sums = pair_loop(near_ref, count, center, mine, steps, sums)
+        for k in range(2 * RADIAL):
+            out_ref[k, at, :] = out_ref[k, at, :] + sums[k] if first == 4 else sums[k]
+
+
+def pair_loop(near_ref, count, center, mine, steps, sums):
     lane8 = iota((8, LANES), 1)
+    mixed = jnp.where(iota((8, LANES), 0) < 4, -1.0, 1.0)
 
     def body(n, sums):
         sums = list(sums)
-        for dz in range(3):
-            near = [near_ref[n, c, 4 * dz + 8 * half : 4 * dz + 8 * half + 8, :] for c in range(4)]
-            mine_z = mine[2] - float(dz - 1)
+        for row, dz in steps:
+            near = [near_ref[n, c, row : row + 8, :] for c in range(4)]
+            mine_z = mine[2] - (mixed if dz is None else float(dz))
             for turn in range(SLOTS):
                 if turn == 0:
                     got = near
@@ -175,7 +202,7 @@
                 gz = got[2] - mine_z
                 kind = got[3]
                 remain = jnp.maximum(1.0 - (gx * gx + gy * gy + gz * gz), 0.0)
-                if turn == 0 and dz == 1 and center is not None:
+                if turn == 0 and dz == 0 and center is not None:
                     remain = remain * jnp.where(n == center, 0.0, 1.0).astype(jnp.float32)
                 half_t = remain - 0.5
                 two = half_t * half_t - 1.0 / 8.0
@@ -192,28 +219,44 @@
     return lax.fori_loop(0, count, body, tuple(sums))
 
 
-def first_pairs_kernel(ext_ref, sums_ref, near_ref):
-    own = ext_ref[...].reshape(LANES, LANES)
-    for dx in range(3):
-        place_blocks(near_ref, dx, own, dx, 1)
-    zero = jnp.zeros((8, LANES), jnp.float32)
-    for half in range(2):
-        at = slice(8 * half, 8 * half + 8)
-        mine = [near_ref[1, c, 4 + 8 * half : 12 + 8 * half, :] for c in range(3)]
-        sums = pair_sums(near_ref, 3, 1, mine, half, (zero,) * (2 * RADIAL))
-        for k in range(2 * RADIAL):
-            sums_ref[k, at, :] = sums[k]
-
-
-def first_pairs_call(ext):
+def column_pairs_kernel(own_ref, sums_ref, near_ref):
+    for c in range(4):
+        for bz in range(ZBLOCKS):
+            place_rows(near_ref, 0, c, bz, own_ref[c, bz])
+    pair_sums(near_ref, 1, 0, lambda c, at: near_ref[0, c, at, :], None, sums_ref)
+
+
+def column_pairs_call(own):
+    return pl.pallas_call(
+        column_pairs_kernel,
+        out_shape=jax.ShapeDtypeStruct((SPECIES * RADIAL, 16, LANES), jnp.float32),
+        scratch_shapes=[pltpu.VMEM((1, 4, 24, LANES), jnp.float32)],
+        compiler_params=pltpu.CompilerParams(vmem_limit_bytes=VMEM_BYTES),
+        cost_estimate=pl.CostEstimate(flops=8_000_000, bytes_accessed=1 << 18, transcendentals=0),
+        name="column_pairs",
+    )(own)
+
+
+def first_pairs_kernel(ext_ref, begun_ref, sums_ref, near_ref, own_ref):
+    blocks = ext_ref[...].reshape(LANES, LANES)
+    place_blocks(near_ref, 0, blocks, 0, 1)
+    place_blocks(near_ref, 1, blocks, 2, 1)
+    own_rows(own_ref, blocks)
+    pair_sums(near_ref, 2, None, lambda c, at: own_ref[c, at, :], begun_ref, sums_ref)
+
+
+def first_pairs_call(ext, begun):
     return pl.pallas_call(
         first_pairs_kernel,
         out_shape=jax.ShapeDtypeStruct((SPECIES * RADIAL, 16, LANES), jnp.float32),
-        scratch_shapes=[pltpu.VMEM((3, 4, 24, LANES), jnp.float32)],
+        scratch_shapes=[
+            pltpu.VMEM((2, 4, 24, LANES), jnp.float32),
+            pltpu.VMEM((4, 16, LANES), jnp.float32),
+        ],
         compiler_params=pltpu.CompilerParams(vmem_limit_bytes=VMEM_BYTES),
-        cost_estimate=pl.CostEstimate(flops=24_000_000, bytes_accessed=1 << 19, transcendentals=0),
+        cost_estimate=pl.CostEstimate(flops=16_000_000, bytes_accessed=1 << 19, transcendentals=0),
         name="first_pairs",
-    )(ext)
+    )(ext, begun)
 
 
 def atoms_kernel(
@@ -244,16 +287,11 @@
     for dx in range(3):
         place_blocks(near_ref, 2 * dx, before, dx, 0)
         place_blocks(near_ref, 2 * dx + 1, after, dx, 2)
-    for c in range(4):
-        for bz in range(ZBLOCKS):
-            row = (c * ZBLOCKS + bz) * 8 + 1
-            own_ref[c, 4 * bz : 4 * bz + 4, :] = own[row : row + 4, :]
-
+    own_rows(own_ref, own)
+
+    pair_sums(near_ref, 6, None, lambda c, at: own_ref[c, at, :], begun_ref, feature_ref)
     for half in range(2):
-        at = slice(8 * half, 8 * half + 8)
-        mine = [own_ref[c, at, :] for c in range(3)]
-        begun = [begun_ref[k, at, :] for k in range(2 * RADIAL)]
-        sums = pair_sums(near_ref, 6, None, mine, half, begun)
+        sums = [feature_ref[k, 8 * half : 8 * half + 8, :] for k in range(2 * RADIAL)]
         scales = [product_scale(k) / SLOTS for k in range(RADIAL)]
         both = chebyshev_of_products([sums[k] * scales[k] for k in range(RADIAL)])
         ones = chebyshev_of_products([sums[RADIAL + k] * scales[k] for k in range(RADIAL)])
@@ -764,14 +802,15 @@
     up, down = ring(count_x)
     before = lax.ppermute(own[:, :, 3:4, :], "gx", up)
     after = lax.ppermute(own[:, :, 0:1, :], "gx", down)
-    before, after, packed = lax.optimization_barrier((before, after, packed))
+    begun = column_pairs_call(own)
+    before, after, packed, begun = lax.optimization_barrier((before, after, packed, begun))
     ext = jnp.concatenate([before, own, after, after, after], axis=2)
     up, down = ring(count_y)
     left = lax.ppermute(ext, "gy", up)
     right = lax.ppermute(ext, "gy", down)
     tables = plane_tables(count_x)
     table = filter_call(lax.axis_index(("gx", "gy")))
-    begun = first_pairs_call(ext)
+    begun = first_pairs_call(ext, begun)
     short, charge, wire = atoms_call(ext, left, right, begun, packed)
     wire = exchange(wire)
     wire = plane_call(wire, table, tables, count_x, count_y)

time: 96.9 us -> 95.3 us (0.983)
  Pallas kernels: 32.6 us -> 30.6 us
  starting transfers between devices: 15.6 us -> 17 us
  waiting for transfers between devices: 19.1 us -> 18.1 us
    pallas_call x1, Pallas kernels: 4.18 us -> 2.4 us  [first_pairs_call(): pl.pallas_call(first_pairs_kernel, out_shape=jax.ShapeDtypeStruct((SPECIE...]
    all_to_all x1, starting transfers between devices: 7.44 us -> 8.86 us  [exchange(): lax.all_to_all(wire.reshape(PLANES, 1, WIRE_ROWS * LANES), ('gx', 'gy'),...]
    pallas_call x1, Pallas kernels: 13.7 us -> 12.5 us  [atoms_call(): pl.pallas_call(atoms_kernel, out_shape=(jax.ShapeDtypeStruct((4, 4, LANES...]
    ppermute x1, waiting for transfers between devices: 3.62 us -> 2.57 us  [shards(): after = lax.ppermute(own[:, :, 0:1, :], 'gx', down)]
    pallas_call x0 -> x1, Pallas kernels: none -> 1.04 us  [column_pairs_call(): pl.pallas_call(column_pairs_kernel, out_shape=jax.ShapeDtypeStruct((SPECI...]
where the time goes in v4:
time: 95.3 us; the launch traced here: 94.8 us
  Pallas kernels  30.6 us (32%)
  blocking collectives  25.1 us (26%)
  waiting for transfers between devices  18.1 us (19%)
  starting transfers between devices  17 us (18%)
  other arithmetic  2.51 us (3%)
    all_to_all x1, blocking collectives, exchange(): lax.all_to_all(wire.reshape(PLANES, 1, WIRE_ROWS * LANES), ('gx', 'gy'),...  25.1 us
    all_to_all x1, waiting for transfers between devices, exchange(): lax.all_to_all(wire.reshape(PLANES, 1, WIRE_ROWS * LANES), ('gx', 'gy'),...  15.5 us
    pallas_call x1, Pallas kernels, atoms_call(): pl.pallas_call(atoms_kernel, out_shape=(jax.ShapeDtypeStruct((4, 4, LANES...  12.5 us
    all_to_all x1, starting transfers between devices, exchange(): lax.all_to_all(wire.reshape(PLANES, 1, WIRE_ROWS * LANES), ('gx', 'gy'),...  8.86 us
    pallas_call x1, Pallas kernels, plane_call(): pl.pallas_call(functools.partial(plane_kernel, count_x, count_y), out_sha...  5.43 us
    pallas_call x1, Pallas kernels, filter_call(): pl.pallas_call(filter_kernel, out_shape=jax.ShapeDtypeStruct((NX // 2 + 8...  4.9 us
    pallas_call x1, Pallas kernels, force_call(): pl.pallas_call(force_kernel, out_shape=(jax.ShapeDtypeStruct((4, 4, LANES...  4.37 us
    ppermute x1, starting transfers between devices, shards(): before = lax.ppermute(own[:, :, 3:4, :], 'gx', up)  4.2 us
  transfers between devices with their start and end apart: 5, of which 2 were waited for; matrix products, arithmetic and copies ran while one was open for 2% of the time, Pallas kernels for 9%

profile of v4, /device:TPU:1, one launch (start us, length us, event | category | flops | bytes accessed | tf_op | source)
XLA Modules:
  0.0 94.8 jit_solution(11858387210722048484)
XLA Ops:
  0.7 0.7 broadcast_and_fusion
  1.4 0.8 add_multiply_fusion.own_ref
  2.2 4.2 %collective-permute-start = (f32[4,4,1,128]{3,2,1,0:T(1,128)S(1)}, f32[4,4,1,128]{3,2,1,0:T(1,128)S(1)}, u32[]{:S(2)}, u32[]{:S(2)}) collective-permute-start(f32[4,4,1,128]{3,2,1,0:T(1,128)S(1)} %get-tuple-element.22), channel_id=1, source_target_pairs={{0,8},{8,16},{16,24},{24,32},{32,40},{40,48},{48,56},{56,64},{64,7... | collective-permute-start | bytes 24584 | tf_op jit(solution)/shard_map/ppermute | solution.py:803
  6.4 0.0 collective-permute-start.1
  6.5 0.9 add_add_fusion.packed_ref
  7.4 1.0 %column_pairs.1.begun_ref = f32[32,16,128]{2,1,0:T(8,128)S(1)} custom-call(f32[4,4,4,128]{3,2,1,0:T(4,128)S(1)} %add_multiply_fusion.own_ref), custom_call_target="tpu_custom_call" | custom-call | flops 8000000 | bytes 262144 | tf_op jit(solution)/shard_map/column_pairs/pallas_call | solution.py:230
  8.4 0.0 collective-permute-done
  8.5 2.6 %collective-permute-done.1 = f32[4,4,1,128]{3,2,1,0:T(1,128)S(1)} collective-permute-done((f32[4,4,1,128]{3,2,1,0:T(1,128)S(1)}, f32[4,4,1,128]{3,2,1,0:T(1,128)S(1)}, u32[]{:S(2)}, u32[]{:S(2)}) %collective-permute-start.1) | collective-permute-done | bytes 8224 | tf_op jit(solution)/shard_map/ppermute | solution.py:804
  11.0 0.1 concatenate.3.ext_ref.place_ref
  11.1 1.7 %collective-permute-start.2 = (f32[4,4,8,128]{3,2,1,0:T(8,128)S(1)}, f32[4,4,8,128]{3,2,1,0:T(8,128)S(1)}, u32[]{:S(2)}, u32[]{:S(2)}) collective-permute-start(f32[4,4,8,128]{3,2,1,0:T(8,128)S(1)} %concatenate.3.ext_ref.place_ref), channel_id=1, source_target_pairs={{0,1},{1,2},{2,3},{3,4},{4,5},{5,6},{6,7},{7,0},{8,9},{9,10},{10,1... | collective-permute-start | bytes 196616 | tf_op jit(solution)/shard_map/ppermute | solution.py:809
  12.8 2.2 %collective-permute-start.3 = (f32[4,4,8,128]{3,2,1,0:T(8,128)S(1)}, f32[4,4,8,128]{3,2,1,0:T(8,128)S(1)}, u32[]{:S(2)}, u32[]{:S(2)}) collective-permute-start(f32[4,4,8,128]{3,2,1,0:T(8,128)S(1)} %concatenate.3.ext_ref.place_ref), channel_id=1, source_target_pairs={{1,0},{2,1},{3,2},{4,3},{5,4},{6,5},{7,6},{0,7},{9,8},{10,9},{11,1... | collective-permute-start | bytes 196616 | tf_op jit(solution)/shard_map/ppermute | solution.py:810
  15.0 2.4 %first_pairs.1.begun_ref = f32[32,16,128]{2,1,0:T(8,128)S(1)} custom-call(f32[4,4,8,128]{3,2,1,0:T(8,128)S(1)} %concatenate.3.ext_ref.place_ref, f32[32,16,128]{2,1,0:T(8,128)S(1)} %column_pairs.1.begun_ref), custom_call_target="tpu_custom_call" | custom-call | flops 16000000 | bytes 524288 | tf_op jit(solution)/shard_map/first_pairs/pallas_call | solution.py:249
  17.4 0.0 collective-permute-done.2.left_ref
  17.4 0.0 collective-permute-done.3.right_ref
  17.5 12.5 %atoms.1 = (f32[4,4,128]{2,1,0:T(4,128)S(1)}, f32[4,4,128]{2,1,0:T(4,128)}, f32[2432,128]{1,0:T(8,128)}) custom-call(f32[4,4,8,128]{3,2,1,0:T(8,128)S(1)} %concatenate.3.ext_ref.place_ref, f32[4,4,8,128]{3,2,1,0:T(8,128)S(1)} %collective-permute-done.2.left_ref, f32[4,4,8,128]{3,2,1,0:T(8,128)S(1)} %collective-permute-done.3.right_ref, ...), custom_call_target="tpu_custom_call" | custom-call | tf_op jit(solution)/shard_map/atoms/pallas_call | solution.py:393
  29.9 0.0 copy-start.1
  29.9 0.0 copy-start
  29.9 8.9 %all-to-all-start = ((f32[128,1,2432]{2,1,0:T(1,128)}), f32[128,1,2432]{2,1,0:T(1,128)S(1)}, u32[]{:S(2)}, u32[]{:S(2)}) async-start(f32[128,1,2432]{2,1,0:T(1,128)} %bitcast.6), calls=%async_computation | async-start | bytes 2490368 | tf_op jit(solution)/shard_map/all_to_all | solution.py:787
  38.8 0.7 dynamic-slice_bitcast_fusion
  39.5 0.0 copy-done.1
  39.5 4.9 %filter.1.filter_ref = f32[264,512]{1,0:T(8,128)S(1)} custom-call(f32[65]{0:T(128)S(1)} %get-tuple-element.24.terms_ref, f32[65]{0:T(128)S(1)} %get-tuple-element.23.squares_ref, f32[16,512]{1,0:T(8,128)S(1)} %copy-done.1), custom_call_target="tpu_custom_call" | custom-call | flops 20000000 | bytes 1048576 | tf_op jit(solution)/shard_map/filter/pallas_call | solution.py:480
  44.5 15.5 %all-to-all-done = f32[128,1,2432]{2,1,0:T(1,128)S(1)} async-done(((f32[128,1,2432]{2,1,0:T(1,128)}), f32[128,1,2432]{2,1,0:T(1,128)S(1)}, u32[]{:S(2)}, u32[]{:S(2)}) %all-to-all-start) | async-done | bytes 1245216 | tf_op jit(solution)/shard_map/all_to_all | solution.py:787
  59.9 0.0 copy-done
  59.9 5.4 %plane.1 = f32[2432,128]{1,0:T(8,128)S(1)} custom-call(f32[2432,128]{1,0:T(8,128)S(1)} %bitcast.14, f32[264,512]{1,0:T(8,128)S(1)} %filter.1.filter_ref, f32[336,512]{1,0:T(8,128)S(1)} %copy-done), custom_call_target="tpu_custom_call" | custom-call | tf_op jit(solution)/shard_map/plane/pallas_call | solution.py:658
  65.4 0.0 copy-start.2
  65.4 0.0 copy-start.3
  65.4 25.1 %all_to_all.10 = f32[128,1,2432]{2,1,0:T(1,128)S(1)} all-to-all(f32[128,1,2432]{2,1,0:T(1,128)S(1)} %bitcast.15), channel_id=1, replica_groups=mesh['gx'=16,'gy'=8] {'gx','gy'}, dimensions={0} | all-to-all | bytes 2490368 | tf_op jit(solution)/shard_map/all_to_all | solution.py:787
  90.5 0.0 copy-done.2
  90.5 0.0 copy-done.3
  90.5 4.4 %force.1 = (f32[4,4,128]{2,1,0:T(4,128)}, f32[3,4,4,128]{3,2,1,0:T(4,128)}) custom-call(f32[2432,128]{1,0:T(8,128)S(1)} %bitcast.16, f32[4,4,8,128]{3,2,1,0:T(8,128)S(1)} %concatenate.3.ext_ref.place_ref, f32[4,4,128]{2,1,0:T(4,128)S(1)} %get-tuple-element.17.short_ref, f32[4,4,128]{2,1,0:T(4,128)S(1)} %copy-done.3, f32[40,128]{1,0:T(8,128)S(1)} %copy-done.2), custom_call_target="tpu_custom_call" | custom-call | tf_op jit(solution)/shard_map/force/pallas_call | solution.py:769
  (3 shorter events, 0.0 us)
Async XLA Ops:
  2.2 6.2 %collective-permute-start = (f32[4,4,1,128]{3,2,1,0:T(1,128)S(1)}, f32[4,4,1,128]{3,2,1,0:T(1,128)S(1)}, u32[]{:S(2)}, u32[]{:S(2)}) collective-permute-start(f32[4,4,1,128]{3,2,1,0:T(1,128)S(1)} %get-tuple-element.22), channel_id=1, source_target_pairs={{0,8},{8,16},{16,24},{24,32},{32,40},{40,48},{48,56},{56,64},{64,7... | collective-permute-start | bytes 24584 | tf_op jit(solution)/shard_map/ppermute | solution.py:803
  6.4 4.6 %collective-permute-start.1 = (f32[4,4,1,128]{3,2,1,0:T(1,128)S(1)}, f32[4,4,1,128]{3,2,1,0:T(1,128)S(1)}, u32[]{:S(2)}, u32[]{:S(2)}) collective-permute-start(f32[4,4,1,128]{3,2,1,0:T(1,128)S(1)} %get-tuple-element.21), channel_id=1, source_target_pairs={{8,0},{16,8},{24,16},{32,24},{40,32},{48,40},{56,48},{64,56},{72,6... | collective-permute-start | bytes 24584 | tf_op jit(solution)/shard_map/ppermute | solution.py:804
  11.1 6.3 %collective-permute-start.2 = (f32[4,4,8,128]{3,2,1,0:T(8,128)S(1)}, f32[4,4,8,128]{3,2,1,0:T(8,128)S(1)}, u32[]{:S(2)}, u32[]{:S(2)}) collective-permute-start(f32[4,4,8,128]{3,2,1,0:T(8,128)S(1)} %concatenate.3.ext_ref.place_ref), channel_id=1, source_target_pairs={{0,1},{1,2},{2,3},{3,4},{4,5},{5,6},{6,7},{7,0},{8,9},{9,10},{10,1... | collective-permute-start | bytes 196616 | tf_op jit(solution)/shard_map/ppermute | solution.py:809
  12.8 4.6 %collective-permute-start.3 = (f32[4,4,8,128]{3,2,1,0:T(8,128)S(1)}, f32[4,4,8,128]{3,2,1,0:T(8,128)S(1)}, u32[]{:S(2)}, u32[]{:S(2)}) collective-permute-start(f32[4,4,8,128]{3,2,1,0:T(8,128)S(1)} %concatenate.3.ext_ref.place_ref), channel_id=1, source_target_pairs={{1,0},{2,1},{3,2},{4,3},{5,4},{6,5},{7,6},{0,7},{9,8},{10,9},{11,1... | collective-permute-start | bytes 196616 | tf_op jit(solution)/shard_map/ppermute | solution.py:810
  29.9 9.6 %copy-start.1 = (f32[16,512]{1,0:T(8,128)S(1)}, f32[16,512]{1,0:T(8,128)}, u32[]{:S(2)}) copy-start(f32[16,512]{1,0:T(8,128)} %constant.45.clone.row_ref) | copy-start | bytes 98308
  29.9 30.0 %copy-start = (f32[336,512]{1,0:T(8,128)S(1)}, f32[336,512]{1,0:T(8,128)}, u32[]{:S(2)}) copy-start(f32[336,512]{1,0:T(8,128)} %constant.46.clone.table_ref) | copy-start | bytes 2064388
  29.9 30.0 %all-to-all-start = ((f32[128,1,2432]{2,1,0:T(1,128)}), f32[128,1,2432]{2,1,0:T(1,128)S(1)}, u32[]{:S(2)}, u32[]{:S(2)}) async-start(f32[128,1,2432]{2,1,0:T(1,128)} %bitcast.6), calls=%async_computation | async-start | bytes 2490368 | tf_op jit(solution)/shard_map/all_to_all | solution.py:787
  65.4 25.1 %copy-start.2 = (f32[40,128]{1,0:T(8,128)S(1)}, f32[40,128]{1,0:T(8,128)}, u32[]{:S(2)}) copy-start(f32[40,128]{1,0:T(8,128)} %constant.47.clone.basis_ref) | copy-start | bytes 61444
  65.4 25.1 %copy-start.3 = (f32[4,4,128]{2,1,0:T(4,128)S(1)}, f32[4,4,128]{2,1,0:T(4,128)}, u32[]{:S(2)}) copy-start(f32[4,4,128]{2,1,0:T(4,128)} %get-tuple-element.11.charge_ref) | copy-start | bytes 24580

commit v5 on v4

--- a/solution.py
+++ b/solution.py
@@ -216,7 +216,8 @@
                     sums[RADIAL + k] = sums[RADIAL + k] + terms[k] * kind
         return tuple(sums)
 
-    return lax.fori_loop(0, count, body, tuple(sums))
+    unroll = 2 if len(steps) == 1 and count % 2 == 0 else 1
+    return lax.fori_loop(0, count, body, tuple(sums), unroll=unroll)
 
 
 def column_pairs_kernel(own_ref, sums_ref, near_ref):

time: 95.3 us -> 95.1 us (level)
  no operation moved by 1% of the time
where the time goes in v5:
time: 95.1 us; the launch traced here: 94.7 us
  Pallas kernels  30.4 us (32%)
  blocking collectives  25.1 us (26%)
  waiting for transfers between devices  18.1 us (19%)
  starting transfers between devices  17.1 us (18%)
  other arithmetic  2.51 us (3%)
    all_to_all x1, blocking collectives, exchange(): lax.all_to_all(wire.reshape(PLANES, 1, WIRE_ROWS * LANES), ('gx', 'gy'),...  25.1 us
    all_to_all x1, waiting for transfers between devices, exchange(): lax.all_to_all(wire.reshape(PLANES, 1, WIRE_ROWS * LANES), ('gx', 'gy'),...  15.5 us
    pallas_call x1, Pallas kernels, atoms_call(): pl.pallas_call(atoms_kernel, out_shape=(jax.ShapeDtypeStruct((4, 4, LANES...  12.4 us
    all_to_all x1, starting transfers between devices, exchange(): lax.all_to_all(wire.reshape(PLANES, 1, WIRE_ROWS * LANES), ('gx', 'gy'),...  8.95 us
    pallas_call x1, Pallas kernels, plane_call(): pl.pallas_call(functools.partial(plane_kernel, count_x, count_y), out_sha...  5.44 us
    pallas_call x1, Pallas kernels, filter_call(): pl.pallas_call(filter_kernel, out_shape=jax.ShapeDtypeStruct((NX // 2 + 8...  4.9 us
    pallas_call x1, Pallas kernels, force_call(): pl.pallas_call(force_kernel, out_shape=(jax.ShapeDtypeStruct((4, 4, LANES...  4.37 us
    ppermute x1, starting transfers between devices, shards(): before = lax.ppermute(own[:, :, 3:4, :], 'gx', up)  4.2 us
  transfers between devices with their start and end apart: 5, of which 2 were waited for; matrix products, arithmetic and copies ran while one was open for 2% of the time, Pallas kernels for 9%

profile of v5, /device:TPU:1, one launch (start us, length us, event | category | flops | bytes accessed | tf_op | source)
XLA Modules:
  0.0 94.7 jit_solution(8294926489455324923)
XLA Ops:
  0.7 0.7 broadcast_and_fusion
  1.4 0.8 add_multiply_fusion.own_ref
  2.2 4.2 %collective-permute-start = (f32[4,4,1,128]{3,2,1,0:T(1,128)S(1)}, f32[4,4,1,128]{3,2,1,0:T(1,128)S(1)}, u32[]{:S(2)}, u32[]{:S(2)}) collective-permute-start(f32[4,4,1,128]{3,2,1,0:T(1,128)S(1)} %get-tuple-element.22), channel_id=1, source_target_pairs={{0,8},{8,16},{16,24},{24,32},{32,40},{40,48},{48,56},{56,64},{64,7... | collective-permute-start | bytes 24584 | tf_op jit(solution)/shard_map/ppermute | solution.py:804
  6.4 0.0 collective-permute-start.1
  6.5 0.9 add_add_fusion.packed_ref
  7.4 1.0 %column_pairs.1.begun_ref = f32[32,16,128]{2,1,0:T(8,128)S(1)} custom-call(f32[4,4,4,128]{3,2,1,0:T(4,128)S(1)} %add_multiply_fusion.own_ref), custom_call_target="tpu_custom_call" | custom-call | flops 8000000 | bytes 262144 | tf_op jit(solution)/shard_map/column_pairs/pallas_call | solution.py:231
  8.4 0.0 collective-permute-done
  8.5 2.6 %collective-permute-done.1 = f32[4,4,1,128]{3,2,1,0:T(1,128)S(1)} collective-permute-done((f32[4,4,1,128]{3,2,1,0:T(1,128)S(1)}, f32[4,4,1,128]{3,2,1,0:T(1,128)S(1)}, u32[]{:S(2)}, u32[]{:S(2)}) %collective-permute-start.1) | collective-permute-done | bytes 8224 | tf_op jit(solution)/shard_map/ppermute | solution.py:805
  11.0 0.1 concatenate.3.ext_ref.place_ref
  11.1 1.7 %collective-permute-start.2 = (f32[4,4,8,128]{3,2,1,0:T(8,128)S(1)}, f32[4,4,8,128]{3,2,1,0:T(8,128)S(1)}, u32[]{:S(2)}, u32[]{:S(2)}) collective-permute-start(f32[4,4,8,128]{3,2,1,0:T(8,128)S(1)} %concatenate.3.ext_ref.place_ref), channel_id=1, source_target_pairs={{0,1},{1,2},{2,3},{3,4},{4,5},{5,6},{6,7},{7,0},{8,9},{9,10},{10,1... | collective-permute-start | bytes 196616 | tf_op jit(solution)/shard_map/ppermute | solution.py:810
  12.8 2.2 %collective-permute-start.3 = (f32[4,4,8,128]{3,2,1,0:T(8,128)S(1)}, f32[4,4,8,128]{3,2,1,0:T(8,128)S(1)}, u32[]{:S(2)}, u32[]{:S(2)}) collective-permute-start(f32[4,4,8,128]{3,2,1,0:T(8,128)S(1)} %concatenate.3.ext_ref.place_ref), channel_id=1, source_target_pairs={{1,0},{2,1},{3,2},{4,3},{5,4},{6,5},{7,6},{0,7},{9,8},{10,9},{11,1... | collective-permute-start | bytes 196616 | tf_op jit(solution)/shard_map/ppermute | solution.py:811
  15.0 2.3 %first_pairs.1.begun_ref = f32[32,16,128]{2,1,0:T(8,128)S(1)} custom-call(f32[4,4,8,128]{3,2,1,0:T(8,128)S(1)} %concatenate.3.ext_ref.place_ref, f32[32,16,128]{2,1,0:T(8,128)S(1)} %column_pairs.1.begun_ref), custom_call_target="tpu_custom_call" | custom-call | flops 16000000 | bytes 524288 | tf_op jit(solution)/shard_map/first_pairs/pallas_call | solution.py:250
  17.4 0.0 collective-permute-done.2.left_ref
  17.4 0.0 collective-permute-done.3.right_ref
  17.4 12.4 %atoms.1 = (f32[4,4,128]{2,1,0:T(4,128)S(1)}, f32[4,4,128]{2,1,0:T(4,128)}, f32[2432,128]{1,0:T(8,128)}) custom-call(f32[4,4,8,128]{3,2,1,0:T(8,128)S(1)} %concatenate.3.ext_ref.place_ref, f32[4,4,8,128]{3,2,1,0:T(8,128)S(1)} %collective-permute-done.2.left_ref, f32[4,4,8,128]{3,2,1,0:T(8,128)S(1)} %collective-permute-done.3.right_ref, ...), custom_call_target="tpu_custom_call" | custom-call | tf_op jit(solution)/shard_map/atoms/pallas_call | solution.py:394
  29.7 0.0 copy-start.1
  29.7 0.0 copy-start
  29.7 8.9 %all-to-all-start = ((f32[128,1,2432]{2,1,0:T(1,128)}), f32[128,1,2432]{2,1,0:T(1,128)S(1)}, u32[]{:S(2)}, u32[]{:S(2)}) async-start(f32[128,1,2432]{2,1,0:T(1,128)} %bitcast.6), calls=%async_computation | async-start | bytes 2490368 | tf_op jit(solution)/shard_map/all_to_all | solution.py:788
  38.7 0.7 dynamic-slice_bitcast_fusion
  39.4 0.0 copy-done.1
  39.4 4.9 %filter.1.filter_ref = f32[264,512]{1,0:T(8,128)S(1)} custom-call(f32[65]{0:T(128)S(1)} %get-tuple-element.24.terms_ref, f32[65]{0:T(128)S(1)} %get-tuple-element.23.squares_ref, f32[16,512]{1,0:T(8,128)S(1)} %copy-done.1), custom_call_target="tpu_custom_call" | custom-call | flops 20000000 | bytes 1048576 | tf_op jit(solution)/shard_map/filter/pallas_call | solution.py:481
  44.3 15.5 %all-to-all-done = f32[128,1,2432]{2,1,0:T(1,128)S(1)} async-done(((f32[128,1,2432]{2,1,0:T(1,128)}), f32[128,1,2432]{2,1,0:T(1,128)S(1)}, u32[]{:S(2)}, u32[]{:S(2)}) %all-to-all-start) | async-done | bytes 1245216 | tf_op jit(solution)/shard_map/all_to_all | solution.py:788
  59.8 0.0 copy-done
  59.8 5.4 %plane.1 = f32[2432,128]{1,0:T(8,128)S(1)} custom-call(f32[2432,128]{1,0:T(8,128)S(1)} %bitcast.14, f32[264,512]{1,0:T(8,128)S(1)} %filter.1.filter_ref, f32[336,512]{1,0:T(8,128)S(1)} %copy-done), custom_call_target="tpu_custom_call" | custom-call | tf_op jit(solution)/shard_map/plane/pallas_call | solution.py:659
  65.2 0.0 copy-start.2
  65.3 0.0 copy-start.3
  65.3 25.1 %all_to_all.10 = f32[128,1,2432]{2,1,0:T(1,128)S(1)} all-to-all(f32[128,1,2432]{2,1,0:T(1,128)S(1)} %bitcast.15), channel_id=1, replica_groups=mesh['gx'=16,'gy'=8] {'gx','gy'}, dimensions={0} | all-to-all | bytes 2490368 | tf_op jit(solution)/shard_map/all_to_all | solution.py:788
  90.3 0.0 copy-done.2
  90.3 0.0 copy-done.3
  90.3 4.4 %force.1 = (f32[4,4,128]{2,1,0:T(4,128)}, f32[3,4,4,128]{3,2,1,0:T(4,128)}) custom-call(f32[2432,128]{1,0:T(8,128)S(1)} %bitcast.16, f32[4,4,8,128]{3,2,1,0:T(8,128)S(1)} %concatenate.3.ext_ref.place_ref, f32[4,4,128]{2,1,0:T(4,128)S(1)} %get-tuple-element.17.short_ref, f32[4,4,128]{2,1,0:T(4,128)S(1)} %copy-done.3, f32[40,128]{1,0:T(8,128)S(1)} %copy-done.2), custom_call_target="tpu_custom_call" | custom-call | tf_op jit(solution)/shard_map/force/pallas_call | solution.py:770
  (3 shorter events, 0.0 us)
Async XLA Ops:
  2.2 6.2 %collective-permute-start = (f32[4,4,1,128]{3,2,1,0:T(1,128)S(1)}, f32[4,4,1,128]{3,2,1,0:T(1,128)S(1)}, u32[]{:S(2)}, u32[]{:S(2)}) collective-permute-start(f32[4,4,1,128]{3,2,1,0:T(1,128)S(1)} %get-tuple-element.22), channel_id=1, source_target_pairs={{0,8},{8,16},{16,24},{24,32},{32,40},{40,48},{48,56},{56,64},{64,7... | collective-permute-start | bytes 24584 | tf_op jit(solution)/shard_map/ppermute | solution.py:804
  6.4 4.6 %collective-permute-start.1 = (f32[4,4,1,128]{3,2,1,0:T(1,128)S(1)}, f32[4,4,1,128]{3,2,1,0:T(1,128)S(1)}, u32[]{:S(2)}, u32[]{:S(2)}) collective-permute-start(f32[4,4,1,128]{3,2,1,0:T(1,128)S(1)} %get-tuple-element.21), channel_id=1, source_target_pairs={{8,0},{16,8},{24,16},{32,24},{40,32},{48,40},{56,48},{64,56},{72,6... | collective-permute-start | bytes 24584 | tf_op jit(solution)/shard_map/ppermute | solution.py:805
  11.1 6.3 %collective-permute-start.2 = (f32[4,4,8,128]{3,2,1,0:T(8,128)S(1)}, f32[4,4,8,128]{3,2,1,0:T(8,128)S(1)}, u32[]{:S(2)}, u32[]{:S(2)}) collective-permute-start(f32[4,4,8,128]{3,2,1,0:T(8,128)S(1)} %concatenate.3.ext_ref.place_ref), channel_id=1, source_target_pairs={{0,1},{1,2},{2,3},{3,4},{4,5},{5,6},{6,7},{7,0},{8,9},{9,10},{10,1... | collective-permute-start | bytes 196616 | tf_op jit(solution)/shard_map/ppermute | solution.py:810
  12.8 4.6 %collective-permute-start.3 = (f32[4,4,8,128]{3,2,1,0:T(8,128)S(1)}, f32[4,4,8,128]{3,2,1,0:T(8,128)S(1)}, u32[]{:S(2)}, u32[]{:S(2)}) collective-permute-start(f32[4,4,8,128]{3,2,1,0:T(8,128)S(1)} %concatenate.3.ext_ref.place_ref), channel_id=1, source_target_pairs={{1,0},{2,1},{3,2},{4,3},{5,4},{6,5},{7,6},{0,7},{9,8},{10,9},{11,1... | collective-permute-start | bytes 196616 | tf_op jit(solution)/shard_map/ppermute | solution.py:811
  29.7 9.7 %copy-start.1 = (f32[16,512]{1,0:T(8,128)S(1)}, f32[16,512]{1,0:T(8,128)}, u32[]{:S(2)}) copy-start(f32[16,512]{1,0:T(8,128)} %constant.45.clone.row_ref) | copy-start | bytes 98308
  29.7 30.1 %copy-start = (f32[336,512]{1,0:T(8,128)S(1)}, f32[336,512]{1,0:T(8,128)}, u32[]{:S(2)}) copy-start(f32[336,512]{1,0:T(8,128)} %constant.46.clone.table_ref) | copy-start | bytes 2064388
  29.7 30.1 %all-to-all-start = ((f32[128,1,2432]{2,1,0:T(1,128)}), f32[128,1,2432]{2,1,0:T(1,128)S(1)}, u32[]{:S(2)}, u32[]{:S(2)}) async-start(f32[128,1,2432]{2,1,0:T(1,128)} %bitcast.6), calls=%async_computation | async-start | bytes 2490368 | tf_op jit(solution)/shard_map/all_to_all | solution.py:788
  65.2 25.1 %copy-start.2 = (f32[40,128]{1,0:T(8,128)S(1)}, f32[40,128]{1,0:T(8,128)}, u32[]{:S(2)}) copy-start(f32[40,128]{1,0:T(8,128)} %constant.47.clone.basis_ref) | copy-start | bytes 61444
  65.3 25.1 %copy-start.3 = (f32[4,4,128]{2,1,0:T(4,128)S(1)}, f32[4,4,128]{2,1,0:T(4,128)}, u32[]{:S(2)}) copy-start(f32[4,4,128]{2,1,0:T(4,128)} %get-tuple-element.11.charge_ref) | copy-start | bytes 24580
